TPU v7x, 32 devices: a whole 2x2x4 slice. The times are simulated.
32 devices in a mesh: dp: 4 (over x, core), space: 8 (over z, y).
Axes of the slice: x: 2, y: 2, z: 4, core: 2. Of those that a mesh axis runs over, the one named last changes fastest.
Arguments:
- layer_input: bfloat16 [4, 64, 16, 1024], P('dp', None, 'space'), may hold values from -6 to 6
- hidden_pre: bfloat16 [4, 128, 16, 1024], P('dp', None, 'space'), may hold values from -6 to 6
- output_pre: bfloat16 [4, 256, 8, 256], P('dp', None, 'space'), may hold values from -6 to 6
- output_grad: bfloat16 [4, 256, 8, 256], P('dp', None, 'space'), may hold values from -48 to 48
- weight_a: bfloat16 [27, 64, 128], replicated, may hold values from -0.15625 to 0.15625
- weight_b: bfloat16 [27, 128, 256], replicated, may hold values from -0.109375 to 0.109375
Outputs:
- input_grad: bfloat16 [4, 64, 16, 1024], P('dp', None, 'space')
- weight_grad_a: float32 [27, 64, 128], replicated
- weight_grad_b: float32 [27, 128, 256], replicated
All inputs are finite; a program needn't handle non-finite values.
Results may differ from a plain program's by a relative error of at most 0.013.
Values may be sent and summed in bfloat16 or wider, within the bound.
No kernel may reach another device: no remote copies, remote signals or barrier semaphores. Data moves between devices by JAX's collectives and lax.ppermute only.
A program may use at most 64 MiB of HBM per device.

v0:
```python
import math

import jax
import jax.numpy as jnp
from jax import lax
from jax.experimental import pallas as pl
from jax.experimental.pallas import tpu as pltpu
from jax.sharding import PartitionSpec as P

negative_slope = 0.3
f32 = jnp.float32
bf16 = jnp.bfloat16
vmem = pl.BlockSpec(memory_space=pltpu.VMEM)
transposed = (((1,), (1,)), ((), ()))


def shifted(cells, rows, columns, side):
    size = side * side
    offset = rows * side + columns
    if offset:
        cells = pltpu.roll(cells, (-offset) % size, 1)
    place = lax.broadcasted_iota(jnp.int32, cells.shape, 1)
    if rows:
        y = place // side + rows
        cells = jnp.where((y >= 0) & (y < side), cells, 0.0)
    if columns:
        x = place % side + columns
        cells = jnp.where((x >= 0) & (x < side), cells, 0.0)
    return cells


def gathered(parts, side):
    total = None
    for c in range(3):
        line = parts(1, c) + shifted(parts(0, c), 1, 0, side) + shifted(parts(2, c), -1, 0, side)
        line = shifted(line, 0, 1 - c, side)
        total = line if total is None else total + line
    return total


def pool_matrix(side):
    half = side // 2
    fine = lax.broadcasted_iota(jnp.int32, (side * side, half * half), 0)
    coarse = lax.broadcasted_iota(jnp.int32, (side * side, half * half), 1)
    parent = (fine // (2 * side)) * half + (fine % side) // 2
    return jnp.where(parent == coarse, 0.125, 0.0).astype(bf16)


def sides(even_pairs, odd_pairs):
    here = lax.axis_index("space")
    even = here % 2 == 0
    nothing = jnp.zeros(even_pairs.shape, bf16)
    before = jnp.where(here == 0, nothing, jnp.where(even, odd_pairs, even_pairs))
    after = jnp.where(here == lax.axis_size("space") - 1, nothing, jnp.where(even, even_pairs, odd_pairs))
    return before, after


def for_sides(before, after):
    even = lax.axis_index("space") % 2 == 0
    return jnp.where(even, after, before), jnp.where(even, before, after)


def call(kernel, out_shape, scratch, flops, *args, out_specs=None):
    result = pl.pallas_call(
        kernel,
        out_shape=out_shape,
        in_specs=[vmem] * len(args),
        out_specs=out_specs or jax.tree.map(lambda _: vmem, out_shape),
        scratch_shapes=scratch,
        compiler_params=pltpu.CompilerParams(vmem_limit_bytes=48 * 1024 * 1024),
        cost_estimate=pl.CostEstimate(flops=flops >> 12, bytes_accessed=1 << 10, transcendentals=0),
    )(*args)
    return list(result) if isinstance(out_shape, list) else result


def pool_kernel(side, hidden, pooled, matrix):
    width = hidden.shape[1]
    pool = pool_matrix(side)
    matrix[...] = pool
    total = None
    for plane in range(2):
        cells = hidden[plane].astype(f32)
        stacked = jnp.concatenate([jnp.maximum(cells, 0.0), jnp.minimum(cells, 0.0)], 0).astype(bf16)
        part = jnp.dot(stacked, pool, preferred_element_type=f32)
        total = part if total is None else total + part
    pooled[...] = (total[:width] + negative_slope * total[width:]).astype(bf16)


def pack_kernel(plan, pooled, grad, even_pairs, odd_pairs, *refs):
    me = lax.axis_index("dp")
    messages, (before, after) = refs[:-2], refs[-2:]
    before[...], after[...] = sides(even_pairs[...], odd_pairs[...])
    for distance, message in enumerate(messages):
        row = message.shape[0] - 3 * plan.share
        if row:
            message[:row] = pooled[...]
        start = pl.multiple_of((me ^ distance) * plan.share, plan.share)
        for a, plane in enumerate((after, grad, before)):
            message[row + a * plan.share : row + (a + 1) * plan.share] = plane[pl.ds(start, plan.share)]


def share_kernel(plan, *refs):
    pooled, channels, (out, moved, totals) = refs[: plan.samples], refs[plan.samples : -3], refs[-3:]
    size = pooled[0].shape[1]
    half = math.isqrt(size)
    width, share = plan.width, plan.share
    for k, message in enumerate(pooled):
        cells = message[:width]
        cells = cells.astype(f32)
        for tap in range(9):
            moved[tap * width : (tap + 1) * width, k * size : (k + 1) * size] = shifted(
                cells, tap // 3 - 1, tap % 3 - 1, half
            ).astype(bf16)
    right = jnp.concatenate([message[message.shape[0] - 3 * share :] for message in channels], 1)
    result = lax.dot_general(moved[...], right, transposed, preferred_element_type=f32)
    for a in range(3):
        pieces = [
            result[k * plan.tall : (k + 1) * plan.tall, a * share : (a + 1) * share] for k in range(plan.pieces)
        ]
        totals[a * plan.tall : (a + 1) * plan.tall] = jnp.concatenate(pieces, 1)
    spare = totals.shape[0] - 3 * plan.tall
    if spare:
        totals[3 * plan.tall :] = jnp.zeros((spare, 128), f32)
    for slab in range(plan.slabs):
        out[slab] = totals[slab * plan.rows_b : (slab + 1) * plan.rows_b]


def blocks_kernel(plan, totals, *refs):
    mine, got, *blocks, first = refs
    first[...] = mine[...] + got[...].astype(f32)
    me = lax.axis_index("space")
    for distance, block in enumerate(blocks):
        for k in range(2):
            slab = me ^ distance ^ (k * plan.far)
            row = pl.multiple_of(slab * plan.rows_a, plan.rows_a)
            parts = [totals[slab], first[pl.ds(row, plan.rows_a)]]
            spare = plan.block - plan.rows_b - plan.rows_a
            if spare:
                parts.append(jnp.zeros((spare, 128), f32))
            block[k] = jnp.concatenate(parts, 0).astype(bf16)


def near_kernel(*refs):
    total = refs[0][...].astype(f32)
    for part in refs[1:-1]:
        total += part[...].astype(f32)
    refs[-1][...] = total.astype(bf16)


def far_kernel(plan, here, there, pair, low):
    for k in range(2):
        pair[k] = (here[k].astype(f32) + there[1 - k].astype(f32)).astype(bf16)
        low[k] = pair[k, : plan.low]


def flat_kernel(*refs):
    row = 0
    for part in refs[:-1]:
        for k in range(part.shape[0]):
            refs[-1][row : row + part.shape[1]] = part[k]
            row += part.shape[1]


def high_kernel(plan, pair, hop, high):
    for k in range(2):
        high[k], high[2 + k] = pair[k, plan.low :], hop[k, plan.low :]


def stack_kernel(*refs):
    count = refs[0].shape[0]
    for k, part in enumerate(refs[:-1]):
        refs[-1][count * k : count * (k + 1)] = part[...]


def last_kernel(plan, scale_a, scale_b, *refs):
    got, (out_a, out_b, shares, rows_a, rows, sems) = refs[:-6], refs[-6:]
    me, here = lax.axis_index("dp"), lax.axis_index("space")
    far, groups = plan.far, plan.samples // 2
    each = len(got) // groups
    for group in range(groups):
        flat, lows_hop, *highs = got[group * each : (group + 1) * each]
        for hop in range(2):
            sample = me ^ group ^ (hop * groups)
            for k in range(plan.slabs):
                slab = here ^ (k // 2) ^ (k % 2 * far)
                if k < 2:
                    row = (2 * hop + k) * plan.block
                    shares[sample, slab] = flat[row : row + plan.block]
                else:
                    row = 4 * plan.block + (k - 2) * plan.low
                    shares[sample, slab, : plan.low] = lows_hop[k - 2] if hop else flat[row : row + plan.low]
                    shares[sample, slab, plan.low :] = highs[k // 2 - 1][2 * hop + k % 2]
    for sample in range(plan.samples):
        for slab in range(plan.slabs):
            row = (sample * plan.slabs + slab) * plan.rows_a
            height = min(plan.rows_a, out_a.shape[0] - row)
            if height > 0:
                base = plan.rows_b // 16 * 16
                block = shares[sample, slab, base:].astype(f32)[plan.rows_b - base :]
                rows_a[row : row + height] = block[:height] * scale_a
    copy_a = pltpu.make_async_copy(rows_a, out_a, sems.at[3])
    copy_a.start()
    copies = []
    for slab in range(plan.slabs):
        blocks = [shares[sample, slab].astype(f32) for sample in range(plan.samples)]
        for k in range(plan.pieces):
            lanes = slice(k * plan.share, (k + 1) * plan.share)
            wide = jnp.concatenate([block[: plan.rows_b, lanes] for block in blocks], 1) * scale_b
            start, stop = slab * plan.rows_b, min((slab + 1) * plan.rows_b, 3 * plan.tall)
            while start < stop:
                a = start // plan.tall
                end = min(stop, (a + 1) * plan.tall)
                row = (a * (plan.pieces - 1) + k) * plan.tall + start
                rows[row : row + end - start] = wide[start - slab * plan.rows_b : end - slab * plan.rows_b]
                start = end
        height = plan.pieces * plan.tall
        while len(copies) < 3 and (slab + 1) * plan.rows_b >= (len(copies) + 1) * plan.tall:
            place = pl.ds(len(copies) * height, height)
            copies.append(pltpu.make_async_copy(rows.at[place], out_b.at[place], sems.at[len(copies)]))
            copies[-1].start()
    for copy in (copy_a, *copies):
        copy.wait()


class Plan:
    def __init__(self, samples, slabs, chan, width, width_b):
        self.samples, self.slabs, self.width = samples, slabs, width
        self.share = width_b // samples
        self.pieces = 128 // self.share
        self.tall = 9 * width // self.pieces
        self.rows_b = -(-3 * self.tall // (8 * slabs)) * 8
        self.rows_a = -(-27 * chan // (8 * samples * slabs)) * 8
        self.block = -(-(self.rows_b + self.rows_a) // 16) * 16
        self.low = -(-self.block * 4 // 112) * 16
        self.far = slabs // 2


def hidden_kernel(side, weight, grad, before, after, hidden, matrix, grad_hidden, products):
    half = side // 2
    width = hidden.shape[1]
    block = 9 * width
    taps = jnp.concatenate([weight[a * block : (a + 1) * block] for a in range(3)], 1)
    planes = jnp.concatenate([after[...], grad[...], before[...]], 0)
    products[...] = jnp.dot(taps, planes, preferred_element_type=f32)

    def part(b, c):
        tap = 3 * b + c
        return products[tap * width : (tap + 1) * width]

    back = gathered(part, half)
    high = back.astype(bf16)
    low = (back - high.astype(f32)).astype(bf16)
    pool = matrix[...]
    spread = lax.dot_general(high, pool, transposed, preferred_element_type=f32)
    spread += lax.dot_general(low, pool, transposed, preferred_element_type=f32)
    for plane in range(2):
        slope = jnp.where(hidden[plane].astype(f32) > 0, 1.0, negative_slope)
        grad_hidden[plane * width : (plane + 1) * width] = (spread * slope).astype(bf16)


def taps_kernel(side, source, moved):
    chan = source.shape[1]
    for plane in range(2):
        cells = source[plane].astype(f32)
        for tap in range(9):
            moved[plane, tap * chan : (tap + 1) * chan] = shifted(
                cells, tap // 3 - 1, tap % 3 - 1, side
            ).astype(bf16)


def sums_a_kernel(side, plan, grad_hidden, inner, even_pairs, odd_pairs, *refs):
    half = plan.samples // 2
    keep, send, (moved, sums) = refs[:half], refs[half:-2], refs[-2:]
    width = plan.width
    chan = even_pairs.shape[0]
    before, after = sides(even_pairs[...], odd_pairs[...])
    for index, plane in enumerate((before, after)):
        cells = plane.astype(f32)
        for tap in range(9):
            moved[index, tap * chan : (tap + 1) * chan] = shifted(
                cells, tap // 3 - 1, tap % 3 - 1, side
            ).astype(bf16)
    both = grad_hidden[...]
    outer0 = lax.dot_general(moved[0], both[:width], transposed, preferred_element_type=f32)
    inner0 = lax.dot_general(inner[0], both, transposed, preferred_element_type=f32)
    inner1 = lax.dot_general(inner[1], both, transposed, preferred_element_type=f32)
    outer1 = lax.dot_general(moved[1], both[width:], transposed, preferred_element_type=f32)
    tall = 9 * chan
    sums[:tall] = outer0 + inner0[:, width:]
    sums[tall : 2 * tall] = inner0[:, :width] + inner1[:, width:]
    sums[2 * tall : 3 * tall] = inner1[:, :width] + outer1
    sums[3 * tall :] = jnp.zeros((sums.shape[0] - 3 * tall, width), f32)
    me = lax.axis_index("dp")
    rows = keep[0].shape[0]
    for k in range(plan.samples):
        part = sums[pl.ds(pl.multiple_of((me ^ k) * rows, rows), rows)]
        if k % 2:
            send[k // 2][...] = part.astype(bf16)
        else:
            keep[k // 2][...] = part


def halve_kernel(*refs):
    count = len(refs) // 3
    mine, got, out = refs[:count], refs[count : 2 * count], refs[2 * count :]
    for k in range(count):
        total = mine[k][...] + got[k][...].astype(f32)
        out[k // 2 + k % 2 * (count // 2)][...] = total.astype(out[k // 2 + k % 2 * (count // 2)].dtype)


def tap_parts(products):
    chan = products.shape[0] // 9

    def part(b, c):
        tap = 3 * b + c
        return products[tap * chan : (tap + 1) * chan]

    return part


def edges_kernel(side, weight, grad_hidden, even_pairs, odd_pairs, products):
    width = weight.shape[1]
    tall = weight.shape[0] // 3
    both = grad_hidden[...]
    products[...] = jnp.dot(weight[:tall], both[:width], preferred_element_type=f32)
    to_before = gathered(tap_parts(products), side).astype(bf16)
    products[...] = jnp.dot(weight[2 * tall :], both[width:], preferred_element_type=f32)
    to_after = gathered(tap_parts(products), side).astype(bf16)
    even_pairs[...], odd_pairs[...] = for_sides(to_before, to_after)


def own_kernel(side, weight, grad_hidden, own, products):
    tall = weight.shape[0] // 3
    both = grad_hidden[...]
    for plane in range(2):
        mixed = jnp.concatenate(
            [weight[(plane + 1) * tall : (plane + 2) * tall], weight[plane * tall : (plane + 1) * tall]], 1
        )
        products[...] = jnp.dot(mixed, both, preferred_element_type=f32)
        own[plane] = gathered(tap_parts(products), side)


def swapped(part, axis, distance):
    return lax.ppermute(part, axis, [(i, i ^ distance) for i in range(lax.axis_size(axis))])


def per_device(layer_input, hidden_pre, output_pre, output_grad, weight_a, weight_b):
    side = math.isqrt(layer_input.shape[3])
    half = side // 2
    size, small = side * side, half * half
    depth_a = layer_input.shape[2]
    samples, slabs = lax.axis_size("dp"), lax.axis_size("space")
    even = [(i, i ^ 1) for i in range(slabs)]
    odd = [(i, ((i + 1 ^ 1) - 1) % slabs) for i in range(slabs)]
    odd_inside = [(i, k) if abs(i - k) == 1 else (i, i) for i, k in odd]
    shape = jax.ShapeDtypeStruct
    outer = output_pre[0, :, 0].astype(f32)
    grad = (output_grad[0, :, 0].astype(f32) * jnp.where(outer > 0, 1.0, negative_slope)).astype(bf16)
    grad, layer_input, hidden_pre = lax.optimization_barrier((grad, layer_input, hidden_pre))
    grad_sides = [lax.ppermute(grad, "space", pairs) for pairs in (even, odd)]
    source = layer_input[0].transpose(1, 0, 2)
    hidden = hidden_pre[0].transpose(1, 0, 2)
    chan = source.shape[1]
    width_a = hidden.shape[1]
    width_b = grad.shape[0]
    plan = Plan(samples, slabs, chan, width_a, width_b)
    pooled, matrix = call(
        lambda *refs: pool_kernel(side, *refs),
        [shape((width_a, small), bf16), shape((size, small), bf16)],
        [],
        1 << 28,
        hidden,
    )
    source, pooled = lax.optimization_barrier((source, pooled))
    edge_planes, source = lax.optimization_barrier((for_sides(source[0], source[1]), source))
    source_sides = [lax.ppermute(part, "space", pairs) for part, pairs in zip(edge_planes, (even, odd))]
    inner = call(
        lambda *refs: taps_kernel(side, *refs), shape((2, 9 * chan, size), bf16), [], 1 << 20, source
    )
    grad_sides, inner = lax.optimization_barrier((grad_sides, inner))
    channels = 3 * plan.share
    heights = [channels + (plan.width if k == 1 or k % 2 == 0 else 0) for k in range(samples)]
    packed = call(
        lambda *refs: pack_kernel(plan, *refs),
        [shape((height, small), bf16) for height in heights] + [shape(grad.shape, bf16)] * 2,
        [],
        1 << 20,
        pooled,
        grad,
        *grad_sides,
    )
    packed, (before, after) = packed[:-2], packed[-2:]
    crossed = [swapped(packed[k], "dp", k // 2 * 2) for k in range(2, samples)]
    core_b = swapped(packed[1], "dp", 1)
    grad_hidden = call(
        lambda *refs: hidden_kernel(side, *refs),
        shape((2 * width_a, size), bf16),
        [pltpu.VMEM((9 * width_a, small), f32)],
        1 << 30,
        weight_b.reshape(27 * width_a, width_b),
        grad,
        before,
        after,
        hidden,
        matrix,
    )
    halves = call(
        lambda *refs: sums_a_kernel(side, plan, *refs),
        [shape((plan.rows_a * slabs, width_a), kind) for kind in (f32, bf16) for _ in range(samples // 2)],
        [
            pltpu.VMEM((2, 9 * chan, size), bf16),
            pltpu.VMEM((plan.rows_a * samples * slabs, width_a), f32),
        ],
        1 << 30,
        grad_hidden,
        inner,
        *source_sides,
    )
    keep, send = halves[: samples // 2], halves[samples // 2 :]
    edges = call(
        lambda *refs: edges_kernel(side, *refs),
        [shape((chan, size), bf16)] * 2,
        [pltpu.VMEM((9 * chan, size), f32)],
        1 << 28,
        weight_a.reshape(27 * chan, width_a),
        grad_hidden,
    )
    got_a, edges = lax.optimization_barrier(([swapped(part, "dp", 1) for part in send], edges))
    for stride in [1 << k for k in range(1, samples.bit_length() - 1)]:
        count = len(keep) // 2
        halves = call(
            halve_kernel,
            [shape(keep[0].shape, kind) for kind in (f32, bf16) for _ in range(count)],
            [],
            1 << 20,
            *keep,
            *got_a,
        )
        keep, send = halves[:count], halves[count:]
        got_a = [swapped(part, "dp", stride) for part in send]
    crossed, keep = lax.optimization_barrier((crossed, keep))
    pooled_parts, channel_parts = [packed[0], core_b], [packed[0], core_b]
    for first, second in zip(crossed[::2], crossed[1::2]):
        pooled_parts += [first, swapped(first[: plan.width], "dp", 1)]
        channel_parts += [first, swapped(second, "dp", 1)]
    totals = call(
        lambda *refs: share_kernel(plan, *refs),
        shape((slabs, plan.rows_b, 128), f32),
        [
            pltpu.VMEM((9 * width_a, samples * small), bf16),
            pltpu.VMEM((slabs * plan.rows_b, 128), f32),
        ],
        1 << 30,
        *pooled_parts,
        *channel_parts,
    )
    from_odd = lax.ppermute(edges[1], "space", odd_inside)
    far = plan.far
    blocks = call(
        lambda *refs: blocks_kernel(plan, *refs),
        [shape((2, plan.block, 128), bf16)] * far,
        [pltpu.VMEM((plan.rows_a * slabs, 128), f32)],
        1 << 20,
        totals,
        keep[0],
        got_a[0],
    )
    parts = blocks[:1] + [swapped(blocks[k], "space", k) for k in range(1, far)]
    own = call(
        lambda *refs: own_kernel(side, *refs),
        shape((2, chan, size), f32),
        [pltpu.VMEM((9 * chan, size), f32)],
        1 << 28,
        weight_a.reshape(27 * chan, width_a),
        grad_hidden,
    )
    parts, from_odd, own = lax.optimization_barrier((parts, from_odd, own))
    both = call(near_kernel, shape((2, plan.block, 128), bf16), [], 1 << 20, *parts)
    there = swapped(both, "space", far)
    both, even_edge = lax.optimization_barrier((both, edges[0]))
    from_even = lax.ppermute(even_edge, "space", even)
    there, from_even = lax.optimization_barrier((there, from_even))
    input_grad = own + jnp.stack(sides(from_even, from_odd)).astype(f32)
    input_grad = input_grad.astype(bf16).transpose(1, 0, 2)[None]
    pair, low = call(
        lambda *refs: far_kernel(plan, *refs),
        [shape((2, rows, 128), bf16) for rows in (plan.block, plan.low)],
        [],
        1 << 20,
        both,
        there,
    )
    strides = [samples >> k for k in range(1, samples.bit_length())]

    def stacked(parts):
        rows = sum(part.shape[0] for part in parts)
        return call(stack_kernel, shape((rows, *parts[0].shape[1:]), bf16), [], 1 << 20, *parts)

    hop = swapped(pair, "dp", strides[0])
    near = [swapped(low, "space", k) for k in range(1, far)]
    pair, hop, near = lax.optimization_barrier((pair, hop, near))
    lows = stacked(near)
    rows = 4 * plan.block + (slabs - 2) * plan.low
    flat = call(flat_kernel, shape((rows, 128), bf16), [], 1 << 20, pair, hop, *near)
    first = [swapped(flat, "dp", stride) for stride in strides[1:]]
    high = call(
        lambda *refs: high_kernel(plan, *refs),
        shape((4, plan.block - plan.low, 128), bf16),
        [],
        1 << 20,
        pair,
        hop,
    )
    lows_hop = swapped(lows, "dp", strides[0])
    highs = [swapped(high, "space", k) for k in range(1, far)]
    lows_hop, highs, first, input_grad = lax.optimization_barrier((lows_hop, highs, first, input_grad))
    known = {0: [flat, lows_hop, *highs]}
    for stride, part in zip(strides[1:], first):
        for k in list(known):
            done = [] if k else [part]
            known[k ^ stride] = done + [swapped(part, "dp", stride) for part in known[k][len(done) :]]
    shares = [known[k] for k in sorted(known)]
    planes_a = depth_a * slabs
    total_a, total_b = call(
        lambda *refs: last_kernel(
            plan,
            1.0 / math.sqrt(samples * planes_a * size),
            1.0 / math.sqrt(samples * (planes_a // 2) * small),
            *refs,
        ),
        [shape((27 * chan, width_a), f32), shape((27 * width_a, width_b), f32)],
        [
            pltpu.VMEM((samples, slabs, plan.block, 128), bf16),
            pltpu.VMEM((27 * chan, width_a), f32),
            pltpu.VMEM((27 * width_a, width_b), f32),
            pltpu.SemaphoreType.DMA((4,)),
        ],
        1 << 20,
        *[part for parts in shares for part in parts],
        out_specs=[pl.BlockSpec(memory_space=pl.ANY)] * 2,
    )
    return (input_grad, total_a.reshape(weight_a.shape), total_b.reshape(weight_b.shape))


def solution(mesh):
    in_specs = (
        P("dp", None, "space", None),
        P("dp", None, "space", None),
        P("dp", None, "space", None),
        P("dp", None, "space", None),
        P(),
        P(),
    )
    out_specs = (P("dp", None, "space", None), P(), P())
    return jax.shard_map(
        per_device, mesh=mesh, in_specs=in_specs, out_specs=out_specs, check_vma=False
    )
```

profile of v0, /device:TPU:0, one launch (start us, length us, event | category | flops | bytes accessed | tf_op | source)
XLA Modules:
  0.0 73.5 jit_solution(10558456777998748127)
XLA Ops:
  0.6 1.0 %fusion.1.refs_1_ = bf16[256,256]{1,0:T(8,128)(2,1)S(1)} fusion(bf16[1,256,1,256]{3,1,2,0:T(8,128)(2,1)} %param.8, bf16[1,256,1,256]{3,1,2,0:T(8,128)(2,1)} %param.9), kind=kLoop, calls=%fused_computation.6 | loop fusion | flops 393216 | bytes 393216 | tf_op jit(solution)/shard_map/mul | solution.py:358
  1.7 6.1 %collective-permute-start.1 = (bf16[256,256]{1,0:T(8,128)(2,1)S(1)}, bf16[256,256]{1,0:T(8,128)(2,1)S(1)}, u32[]{:S(2)}, u32[]{:S(2)}) collective-permute-start(bf16[256,256]{1,0:T(8,128)(2,1)S(1)} %fusion.1.refs_1_), channel_id=1, source_target_pairs={{0,7},{1,2},{2,1},{3,4},{4,3},{5,6},{6,5},{7,0},{8,15},{9,10},{10,... | collective-permute-start | bytes 393224 | tf_op jit(solution)/shard_map/ppermute | solution.py:360
  7.7 1.0 %copy.15 = bf16[1,64,2,1024]{3,1,2,0:T(8,128)(2,1)S(1)} copy(bf16[1,64,2,1024]{3,2,1,0:T(2,128)(2,1)} %param.6) | data formatting | bytes 524288 | tf_op jit(solution)/shard_map/optimization_barrier | solution.py:359
  8.7 1.3 %copy.14 = bf16[1,128,2,1024]{3,1,2,0:T(8,128)(2,1)S(1)} copy(bf16[1,128,2,1024]{3,2,1,0:T(2,128)(2,1)} %param.7) | data formatting | bytes 1048576 | tf_op jit(solution)/shard_map/optimization_barrier | solution.py:359
  10.0 0.5 shard_map.85
  10.6 2.1 %collective-permute-start.5 = (bf16[64,1024]{1,0:T(8,128)(2,1)S(1)}, bf16[64,1024]{1,0:T(8,128)(2,1)S(1)}, u32[]{:S(2)}, u32[]{:S(2)}) collective-permute-start(bf16[64,1024]{1,0:T(8,128)(2,1)S(1)} %get-tuple-element.83), channel_id=1, source_target_pairs={{0,1},{1,0},{2,3},{3,2},{4,5},{5,4},{6,7},{7,6},{8,9},{9,8},{10,11... | collective-permute-start | bytes 393224 | tf_op jit(solution)/shard_map/ppermute | solution.py:376
  12.8 0.7 shard_map.86.refs_1_
  13.5 0.7 collective-permute-done.refs_2_
  14.2 1.6 %collective-permute-start.3 = (bf16[320,256]{1,0:T(8,128)(2,1)S(1)}, bf16[320,256]{1,0:T(8,128)(2,1)S(1)}, u32[]{:S(2)}, u32[]{:S(2)}) collective-permute-start(bf16[320,256]{1,0:T(8,128)(2,1)S(1)} %get-tuple-element.77), channel_id=1, source_target_pairs={{0,16},{8,24},{16,0},{24,8},{1,17},{9,25},{17,1},{25,9},{2,18},{10... | collective-permute-start | bytes 491528 | tf_op jit(solution)/shard_map/ppermute | solution.py:344
  15.8 1.6 %shard_map.88.refs_0_.refs_1_ = bf16[256,1024]{1,0:T(8,128)(2,1)S(1)} custom-call(bf16[3456,256]{1,0:T(8,128)(2,1)S(1)} %bitcast.32, bf16[256,256]{1,0:T(8,128)(2,1)S(1)} %fusion.1.refs_1_, bf16[256,256]{1,0:T(8,128)(2,1)S(1)} %get-tuple-element.79.refs_2_, bf16[256,256]{1,0:T(8,128)(2,1)S(1)} %get-tuple-element.80.refs_3_, ...), custom_call_target="tpu_custom_call" | custom-call | flops 262144 | bytes 1024 | tf_op jit(solution)/shard_map/pallas_call | solution.py:64
  17.4 0.3 collective-permute-done.5.refs_2_
  17.7 2.7 %collective-permute-done.6.refs_3_ = bf16[64,1024]{1,0:T(8,128)(2,1)S(1)} collective-permute-done((bf16[64,1024]{1,0:T(8,128)(2,1)S(1)}, bf16[64,1024]{1,0:T(8,128)(2,1)S(1)}, u32[]{:S(2)}, u32[]{:S(2)}) %collective-permute-start.6) | collective-permute-done | bytes 131104 | tf_op jit(solution)/shard_map/ppermute | solution.py:376
  20.4 1.5 %shard_map.89 = (f32[448,128]{1,0:T(8,128)S(1)}, f32[448,128]{1,0:T(8,128)S(1)}, bf16[448,128]{1,0:T(8,128)(2,1)S(1)}, bf16[448,128]{1,0:T(8,128)(2,1)S(1)}) custom-call(bf16[256,1024]{1,0:T(8,128)(2,1)S(1)} %shard_map.88.refs_0_.refs_1_, bf16[2,576,1024]{2,1,0:T(8,128)(2,1)S(1)} %shard_map.86.refs_1_, bf16[64,1024]{1,0:T(8,128)(2,1)S(1)} %collective-permute-done.5.refs_2_, ...), custom_call_target="tpu_custom_call" | custom-call | flops 262144 | bytes 1024 | tf_op jit(solution)/shard_map/pallas_call | solution.py:64
  22.0 0.5 collective-permute-start.8
  22.5 1.5 %collective-permute-start.4 = (bf16[192,256]{1,0:T(8,128)(2,1)S(1)}, bf16[192,256]{1,0:T(8,128)(2,1)S(1)}, u32[]{:S(2)}, u32[]{:S(2)}) collective-permute-start(bf16[192,256]{1,0:T(8,128)(2,1)S(1)} %get-tuple-element.78), channel_id=1, source_target_pairs={{0,16},{8,24},{16,0},{24,8},{1,17},{9,25},{17,1},{25,9},{2,18},{10... | collective-permute-start | bytes 294920 | tf_op jit(solution)/shard_map/ppermute | solution.py:344
  24.0 1.5 %shard_map.90 = (bf16[64,1024]{1,0:T(8,128)(2,1)S(1)}, bf16[64,1024]{1,0:T(8,128)(2,1)S(1)}) custom-call(bf16[1728,128]{1,0:T(8,128)(2,1)S(1)} %bitcast.33, bf16[256,1024]{1,0:T(8,128)(2,1)S(1)} %shard_map.88.refs_0_.refs_1_), custom_call_target="tpu_custom_call" | custom-call | flops 65536 | bytes 1024 | tf_op jit(solution)/shard_map/pallas_call | solution.py:64
  25.6 0.6 collective-permute-start.11
  26.2 1.1 %collective-permute-done.4 = bf16[192,256]{1,0:T(8,128)(2,1)S(1)} collective-permute-done((bf16[192,256]{1,0:T(8,128)(2,1)S(1)}, bf16[192,256]{1,0:T(8,128)(2,1)S(1)}, u32[]{:S(2)}, u32[]{:S(2)}) %collective-permute-start.4) | collective-permute-done | bytes 98336 | tf_op jit(solution)/shard_map/ppermute | solution.py:344
  27.3 0.5 collective-permute-start.9
  27.8 0.9 %collective-permute-done.9.refs_3_ = bf16[128,256]{1,0:T(8,128)(2,1)S(1)} collective-permute-done((bf16[128,256]{1,0:T(8,128)(2,1)S(1)}, bf16[128,256]{1,0:T(8,128)(2,1)S(1)}, u32[]{:S(2)}, u32[]{:S(2)}) %collective-permute-start.9) | collective-permute-done | bytes 65568 | tf_op jit(solution)/shard_map/ppermute | solution.py:344
  28.7 1.1 %shard_map.92.refs_0_ = f32[8,216,128]{2,1,0:T(8,128)S(1)} custom-call(bf16[320,256]{1,0:T(8,128)(2,1)S(1)} %get-tuple-element.75.refs_0_.refs_4_, bf16[320,256]{1,0:T(8,128)(2,1)S(1)} %collective-permute-done.2.refs_1_.refs_5_, bf16[320,256]{1,0:T(8,128)(2,1)S(1)} %collective-permute-done.3.refs_2_.refs_6_, ...), custom_call_target="tpu_custom_call" | custom-call | flops 262144 | bytes 1024 | tf_op jit(solution)/shard_map/pallas_call | solution.py:64
  29.8 1.4 %collective-permute-done.11.refs_2_ = bf16[448,128]{1,0:T(8,128)(2,1)S(1)} collective-permute-done((bf16[448,128]{1,0:T(8,128)(2,1)S(1)}, bf16[448,128]{1,0:T(8,128)(2,1)S(1)}, u32[]{:S(2)}, u32[]{:S(2)}) %collective-permute-start.11) | collective-permute-done | bytes 114720 | tf_op jit(solution)/shard_map/ppermute | solution.py:344
  31.4 0.4 collective-permute-start.13
  31.8 3.0 %collective-permute-start.14 = (bf16[2,272,128]{2,1,0:T(8,128)(2,1)S(1)}, bf16[2,272,128]{2,1,0:T(8,128)(2,1)S(1)}, u32[]{:S(2)}, u32[]{:S(2)}) collective-permute-start(bf16[2,272,128]{2,1,0:T(8,128)(2,1)S(1)} %get-tuple-element.101), channel_id=1, source_target_pairs={{0,3},{1,2},{2,1},{3,0},{4,7},{5,6},{6,5},{7,4},{8,11},{9,10},{10,... | collective-permute-start | bytes 417800 | tf_op jit(solution)/shard_map/ppermute | solution.py:344
  34.8 0.8 %collective-permute-start.15 = (bf16[64,1024]{1,0:T(8,128)(2,1)S(1)}, bf16[64,1024]{1,0:T(8,128)(2,1)S(1)}, u32[]{:S(2)}, u32[]{:S(2)}) collective-permute-start(bf16[64,1024]{1,0:T(8,128)(2,1)S(1)} %get-tuple-element.102), channel_id=1, source_target_pairs={{0,0},{1,2},{2,1},{3,4},{4,3},{5,6},{6,5},{7,7},{8,8},{9,10},{10,9... | collective-permute-start | bytes 393224 | tf_op jit(solution)/shard_map/ppermute | solution.py:457
  35.7 1.5 %shard_map.94 = f32[2,64,1024]{2,1,0:T(8,128)S(1)} custom-call(bf16[1728,128]{1,0:T(8,128)(2,1)S(1)} %bitcast.34, bf16[256,1024]{1,0:T(8,128)(2,1)S(1)} %shard_map.88.refs_0_.refs_1_), custom_call_target="tpu_custom_call" | custom-call | flops 65536 | bytes 1024 | tf_op jit(solution)/shard_map/pallas_call | solution.py:64
  37.2 0.8 %collective-permute-done.13.refs_2_ = bf16[2,272,128]{2,1,0:T(8,128)(2,1)S(1)} collective-permute-done((bf16[2,272,128]{2,1,0:T(8,128)(2,1)S(1)}, bf16[2,272,128]{2,1,0:T(8,128)(2,1)S(1)}, u32[]{:S(2)}, u32[]{:S(2)}) %collective-permute-start.13) | collective-permute-done | bytes 139296 | tf_op jit(solution)/shard_map/ppermute | solution.py:344
  38.0 2.8 %collective-permute-done.14.refs_3_ = bf16[2,272,128]{2,1,0:T(8,128)(2,1)S(1)} collective-permute-done((bf16[2,272,128]{2,1,0:T(8,128)(2,1)S(1)}, bf16[2,272,128]{2,1,0:T(8,128)(2,1)S(1)}, u32[]{:S(2)}, u32[]{:S(2)}) %collective-permute-start.14) | collective-permute-done | bytes 139296 | tf_op jit(solution)/shard_map/ppermute | solution.py:344
  40.9 2.7 %collective-permute-start.16 = (bf16[2,272,128]{2,1,0:T(8,128)(2,1)S(1)}, bf16[2,272,128]{2,1,0:T(8,128)(2,1)S(1)}, u32[]{:S(2)}, u32[]{:S(2)}) collective-permute-start(bf16[2,272,128]{2,1,0:T(8,128)(2,1)S(1)} %shard_map.95.refs_0_), channel_id=1, source_target_pairs={{0,4},{1,5},{2,6},{3,7},{4,0},{5,1},{6,2},{7,3},{8,12},{9,13},{10,... | collective-permute-start | bytes 417800 | tf_op jit(solution)/shard_map/ppermute | solution.py:344
  43.6 1.7 %collective-permute-start.17 = (bf16[64,1024]{1,0:T(8,128)(2,1)S(1)}, bf16[64,1024]{1,0:T(8,128)(2,1)S(1)}, u32[]{:S(2)}, u32[]{:S(2)}) collective-permute-start(bf16[64,1024]{1,0:T(8,128)(2,1)S(1)} %get-tuple-element.109), channel_id=1, source_target_pairs={{0,1},{1,0},{2,3},{3,2},{4,5},{5,4},{6,7},{7,6},{8,9},{9,8},{10,11... | collective-permute-start | bytes 393224 | tf_op jit(solution)/shard_map/ppermute | solution.py:481
  45.3 3.3 %collective-permute-done.17 = bf16[64,1024]{1,0:T(8,128)(2,1)S(1)} collective-permute-done((bf16[64,1024]{1,0:T(8,128)(2,1)S(1)}, bf16[64,1024]{1,0:T(8,128)(2,1)S(1)}, u32[]{:S(2)}, u32[]{:S(2)}) %collective-permute-start.17) | collective-permute-done | bytes 131104 | tf_op jit(solution)/shard_map/ppermute | solution.py:481
  48.6 1.3 %collective-permute-done.16.refs_1_ = bf16[2,272,128]{2,1,0:T(8,128)(2,1)S(1)} collective-permute-done((bf16[2,272,128]{2,1,0:T(8,128)(2,1)S(1)}, bf16[2,272,128]{2,1,0:T(8,128)(2,1)S(1)}, u32[]{:S(2)}, u32[]{:S(2)}) %collective-permute-start.16) | collective-permute-done | bytes 139296 | tf_op jit(solution)/shard_map/ppermute | solution.py:344
  50.0 0.8 %collective-permute-start.18 = (bf16[2,272,128]{2,1,0:T(8,128)(2,1)S(1)}, bf16[2,272,128]{2,1,0:T(8,128)(2,1)S(1)}, u32[]{:S(2)}, u32[]{:S(2)}) collective-permute-start(bf16[2,272,128]{2,1,0:T(8,128)(2,1)S(1)} %get-tuple-element.116.refs_0_), channel_id=1, source_target_pairs={{0,16},{8,24},{16,0},{24,8},{1,17},{9,25},{17,1},{25,9},{2,18},{10... | collective-permute-start | bytes 417800 | tf_op jit(solution)/shard_map/ppermute | solution.py:344
  50.8 3.3 %collective-permute-start.20 = (bf16[2,160,128]{2,1,0:T(8,128)(2,1)S(1)}, bf16[2,160,128]{2,1,0:T(8,128)(2,1)S(1)}, u32[]{:S(2)}, u32[]{:S(2)}) collective-permute-start(bf16[2,160,128]{2,1,0:T(8,128)(2,1)S(1)} %get-tuple-element.112), channel_id=1, source_target_pairs={{0,2},{1,3},{2,0},{3,1},{4,6},{5,7},{6,4},{7,5},{8,10},{9,11},{10,... | collective-permute-start | bytes 245768 | tf_op jit(solution)/shard_map/ppermute | solution.py:344
  54.0 0.2 collective-permute-start.19
  54.2 2.0 %collective-permute-done.21.refs_2_.refs_4_ = bf16[2,160,128]{2,1,0:T(8,128)(2,1)S(1)} collective-permute-done((bf16[2,160,128]{2,1,0:T(8,128)(2,1)S(1)}, bf16[2,160,128]{2,1,0:T(8,128)(2,1)S(1)}, u32[]{:S(2)}, u32[]{:S(2)}) %collective-permute-start.21) | collective-permute-done | bytes 81952 | tf_op jit(solution)/shard_map/ppermute | solution.py:344
  56.2 1.1 %collective-permute-done.20.refs_1_.refs_3_ = bf16[2,160,128]{2,1,0:T(8,128)(2,1)S(1)} collective-permute-done((bf16[2,160,128]{2,1,0:T(8,128)(2,1)S(1)}, bf16[2,160,128]{2,1,0:T(8,128)(2,1)S(1)}, u32[]{:S(2)}, u32[]{:S(2)}) %collective-permute-start.20) | collective-permute-done | bytes 81952 | tf_op jit(solution)/shard_map/ppermute | solution.py:344
  57.3 1.1 %collective-permute-done.19.refs_0_.refs_2_ = bf16[2,160,128]{2,1,0:T(8,128)(2,1)S(1)} collective-permute-done((bf16[2,160,128]{2,1,0:T(8,128)(2,1)S(1)}, bf16[2,160,128]{2,1,0:T(8,128)(2,1)S(1)}, u32[]{:S(2)}, u32[]{:S(2)}) %collective-permute-start.19) | collective-permute-done | bytes 81952 | tf_op jit(solution)/shard_map/ppermute | solution.py:344
  58.6 1.3 %collective-permute-start.22 = (bf16[6,160,128]{2,1,0:T(8,128)(2,1)S(1)}, bf16[6,160,128]{2,1,0:T(8,128)(2,1)S(1)}, u32[]{:S(2)}, u32[]{:S(2)}) collective-permute-start(bf16[6,160,128]{2,1,0:T(8,128)(2,1)S(1)} %shard_map.97), channel_id=1, source_target_pairs={{0,16},{8,24},{16,0},{24,8},{1,17},{9,25},{17,1},{25,9},{2,18},{10... | collective-permute-start | bytes 737288 | tf_op jit(solution)/shard_map/ppermute | solution.py:344
  60.1 1.7 %collective-permute-start.24 = (bf16[4,112,128]{2,1,0:T(8,128)(2,1)S(1)}, bf16[4,112,128]{2,1,0:T(8,128)(2,1)S(1)}, u32[]{:S(2)}, u32[]{:S(2)}) collective-permute-start(bf16[4,112,128]{2,1,0:T(8,128)(2,1)S(1)} %shard_map.98), channel_id=1, source_target_pairs={{0,2},{1,3},{2,0},{3,1},{4,6},{5,7},{6,4},{7,5},{8,10},{9,11},{10,... | collective-permute-start | bytes 344072 | tf_op jit(solution)/shard_map/ppermute | solution.py:344
  61.9 1.7 %collective-permute-start.23 = (bf16[4,112,128]{2,1,0:T(8,128)(2,1)S(1)}, bf16[4,112,128]{2,1,0:T(8,128)(2,1)S(1)}, u32[]{:S(2)}, u32[]{:S(2)}) collective-permute-start(bf16[4,112,128]{2,1,0:T(8,128)(2,1)S(1)} %shard_map.98), channel_id=1, source_target_pairs={{0,1},{1,0},{2,3},{3,2},{4,5},{5,4},{6,7},{7,6},{8,9},{9,8},{10,11... | collective-permute-start | bytes 344072 | tf_op jit(solution)/shard_map/ppermute | solution.py:344
  63.6 3.3 %collective-permute-done.25.refs_4_ = bf16[4,112,128]{2,1,0:T(8,128)(2,1)S(1)} collective-permute-done((bf16[4,112,128]{2,1,0:T(8,128)(2,1)S(1)}, bf16[4,112,128]{2,1,0:T(8,128)(2,1)S(1)}, u32[]{:S(2)}, u32[]{:S(2)}) %collective-permute-start.25) | collective-permute-done | bytes 114720 | tf_op jit(solution)/shard_map/ppermute | solution.py:344
  67.0 0.6 collective-permute-done.24.refs_3_
  67.6 1.1 %collective-permute-done.23.refs_2_ = bf16[4,112,128]{2,1,0:T(8,128)(2,1)S(1)} collective-permute-done((bf16[4,112,128]{2,1,0:T(8,128)(2,1)S(1)}, bf16[4,112,128]{2,1,0:T(8,128)(2,1)S(1)}, u32[]{:S(2)}, u32[]{:S(2)}) %collective-permute-start.23) | collective-permute-done | bytes 114720 | tf_op jit(solution)/shard_map/ppermute | solution.py:344
  68.7 0.5 collective-permute-start.28
  69.3 0.4 collective-permute-start.30
  69.7 1.0 %copy.11 = bf16[1,64,2,1024]{3,2,1,0:T(2,128)(2,1)} copy(bf16[1,64,2,1024]{3,1,2,0:T(8,128)(2,1)S(1)} %fusion) | data formatting | bytes 524288
  70.7 2.6 %shard_map.100 = (f32[1728,128]{1,0:T(8,128)}, f32[3456,256]{1,0:T(8,128)}) custom-call(bf16[2048,128]{1,0:T(8,128)(2,1)S(1)} %shard_map.99.refs_0_, bf16[6,160,128]{2,1,0:T(8,128)(2,1)S(1)} %collective-permute-done.22.refs_1_, bf16[4,112,128]{2,1,0:T(8,128)(2,1)S(1)} %collective-permute-done.23.refs_2_, ...), custom_call_target="tpu_custom_call" | custom-call | flops 256 | bytes 1024 | tf_op jit(solution)/shard_map/pallas_call | solution.py:64
  (42 shorter events, 1.0 us)
Async XLA Ops:
  1.7 11.8 %collective-permute-start.1 = (bf16[256,256]{1,0:T(8,128)(2,1)S(1)}, bf16[256,256]{1,0:T(8,128)(2,1)S(1)}, u32[]{:S(2)}, u32[]{:S(2)}) collective-permute-start(bf16[256,256]{1,0:T(8,128)(2,1)S(1)} %fusion.1.refs_1_), channel_id=1, source_target_pairs={{0,7},{1,2},{2,1},{3,4},{4,3},{5,6},{6,5},{7,0},{8,15},{9,10},{10,... | collective-permute-start | bytes 393224 | tf_op jit(solution)/shard_map/ppermute | solution.py:360
  7.7 6.4 %collective-permute-start = (bf16[256,256]{1,0:T(8,128)(2,1)S(1)}, bf16[256,256]{1,0:T(8,128)(2,1)S(1)}, u32[]{:S(2)}, u32[]{:S(2)}) collective-permute-start(bf16[256,256]{1,0:T(8,128)(2,1)S(1)} %fusion.1.refs_1_), channel_id=1, source_target_pairs={{0,1},{1,0},{2,3},{3,2},{4,5},{5,4},{6,7},{7,6},{8,9},{9,8},{10,11... | collective-permute-start | bytes 393224 | tf_op jit(solution)/shard_map/ppermute | solution.py:360
  8.7 7.0 %copy-start = (bf16[27,128,256]{2,1,0:T(8,128)(2,1)S(1)}, bf16[27,128,256]{2,1,0:T(8,128)(2,1)}, u32[]{:S(2)}) copy-start(bf16[27,128,256]{2,1,0:T(8,128)(2,1)} %param.11) | copy-start | bytes 5308420
  10.6 7.1 %collective-permute-start.5 = (bf16[64,1024]{1,0:T(8,128)(2,1)S(1)}, bf16[64,1024]{1,0:T(8,128)(2,1)S(1)}, u32[]{:S(2)}, u32[]{:S(2)}) collective-permute-start(bf16[64,1024]{1,0:T(8,128)(2,1)S(1)} %get-tuple-element.83), channel_id=1, source_target_pairs={{0,1},{1,0},{2,3},{3,2},{4,5},{5,4},{6,7},{7,6},{8,9},{9,8},{10,11... | collective-permute-start | bytes 393224 | tf_op jit(solution)/shard_map/ppermute | solution.py:376
  12.7 7.7 %collective-permute-start.6 = (bf16[64,1024]{1,0:T(8,128)(2,1)S(1)}, bf16[64,1024]{1,0:T(8,128)(2,1)S(1)}, u32[]{:S(2)}, u32[]{:S(2)}) collective-permute-start(bf16[64,1024]{1,0:T(8,128)(2,1)S(1)} %get-tuple-element.84), channel_id=1, source_target_pairs={{0,7},{1,2},{2,1},{3,4},{4,3},{5,6},{6,5},{7,0},{8,15},{9,10},{10,... | collective-permute-start | bytes 393224 | tf_op jit(solution)/shard_map/ppermute | solution.py:376
  14.2 13.1 %collective-permute-start.3 = (bf16[320,256]{1,0:T(8,128)(2,1)S(1)}, bf16[320,256]{1,0:T(8,128)(2,1)S(1)}, u32[]{:S(2)}, u32[]{:S(2)}) collective-permute-start(bf16[320,256]{1,0:T(8,128)(2,1)S(1)} %get-tuple-element.77), channel_id=1, source_target_pairs={{0,16},{8,24},{16,0},{24,8},{1,17},{9,25},{17,1},{25,9},{2,18},{10... | collective-permute-start | bytes 491528 | tf_op jit(solution)/shard_map/ppermute | solution.py:344
  17.4 6.6 %copy-start.1 = (bf16[27,64,128]{2,1,0:T(8,128)(2,1)S(1)}, bf16[27,64,128]{2,1,0:T(8,128)(2,1)}, u32[]{:S(2)}) copy-start(bf16[27,64,128]{2,1,0:T(8,128)(2,1)} %param.10) | copy-start | bytes 1327108
  21.9 3.6 %collective-permute-start.7 = (bf16[448,128]{1,0:T(8,128)(2,1)S(1)}, bf16[448,128]{1,0:T(8,128)(2,1)S(1)}, u32[]{:S(2)}, u32[]{:S(2)}) collective-permute-start(bf16[448,128]{1,0:T(8,128)(2,1)S(1)} %get-tuple-element.87), channel_id=1, source_target_pairs={{0,8},{8,0},{16,24},{24,16},{1,9},{9,1},{17,25},{25,17},{2,10},{10... | collective-permute-start | bytes 344072 | tf_op jit(solution)/shard_map/ppermute | solution.py:344
  22.0 3.6 %collective-permute-start.8 = (bf16[448,128]{1,0:T(8,128)(2,1)S(1)}, bf16[448,128]{1,0:T(8,128)(2,1)S(1)}, u32[]{:S(2)}, u32[]{:S(2)}) collective-permute-start(bf16[448,128]{1,0:T(8,128)(2,1)S(1)} %get-tuple-element.88), channel_id=1, source_target_pairs={{0,8},{8,0},{16,24},{24,16},{1,9},{9,1},{17,25},{25,17},{2,10},{10... | collective-permute-start | bytes 344072 | tf_op jit(solution)/shard_map/ppermute | solution.py:344
  22.5 4.8 %collective-permute-start.4 = (bf16[192,256]{1,0:T(8,128)(2,1)S(1)}, bf16[192,256]{1,0:T(8,128)(2,1)S(1)}, u32[]{:S(2)}, u32[]{:S(2)}) collective-permute-start(bf16[192,256]{1,0:T(8,128)(2,1)S(1)} %get-tuple-element.78), channel_id=1, source_target_pairs={{0,16},{8,24},{16,0},{24,8},{1,17},{9,25},{17,1},{25,9},{2,18},{10... | collective-permute-start | bytes 294920 | tf_op jit(solution)/shard_map/ppermute | solution.py:344
  23.9 3.8 %collective-permute-start.2 = (bf16[320,256]{1,0:T(8,128)(2,1)S(1)}, bf16[320,256]{1,0:T(8,128)(2,1)S(1)}, u32[]{:S(2)}, u32[]{:S(2)}) collective-permute-start(bf16[320,256]{1,0:T(8,128)(2,1)S(1)} %get-tuple-element.76), channel_id=1, source_target_pairs={{0,8},{8,0},{16,24},{24,16},{1,9},{9,1},{17,25},{25,17},{2,10},{10... | collective-permute-start | bytes 491528 | tf_op jit(solution)/shard_map/ppermute | solution.py:344
  25.6 5.6 %collective-permute-start.11 = (bf16[448,128]{1,0:T(8,128)(2,1)S(1)}, bf16[448,128]{1,0:T(8,128)(2,1)S(1)}, u32[]{:S(2)}, u32[]{:S(2)}) collective-permute-start(bf16[448,128]{1,0:T(8,128)(2,1)S(1)} %get-tuple-element.97), channel_id=1, source_target_pairs={{0,16},{8,24},{16,0},{24,8},{1,17},{9,25},{17,1},{25,9},{2,18},{10... | collective-permute-start | bytes 344072 | tf_op jit(solution)/shard_map/ppermute | solution.py:344
  27.3 1.4 %collective-permute-start.10 = (bf16[192,256]{1,0:T(8,128)(2,1)S(1)}, bf16[192,256]{1,0:T(8,128)(2,1)S(1)}, u32[]{:S(2)}, u32[]{:S(2)}) collective-permute-start(bf16[192,256]{1,0:T(8,128)(2,1)S(1)} %collective-permute-done.4), channel_id=1, source_target_pairs={{0,8},{8,0},{16,24},{24,16},{1,9},{9,1},{17,25},{25,17},{2,10},{10... | collective-permute-start | bytes 294920 | tf_op jit(solution)/shard_map/ppermute | solution.py:344
  27.3 1.4 %collective-permute-start.9 = (bf16[128,256]{1,0:T(8,128)(2,1)S(1)}, bf16[128,256]{1,0:T(8,128)(2,1)S(1)}, u32[]{:S(2)}, u32[]{:S(2)}) collective-permute-start(bf16[128,256]{1,0:T(8,128)(2,1)S(1)} %slice.11), channel_id=1, source_target_pairs={{0,8},{8,0},{16,24},{24,16},{1,9},{9,1},{17,25},{25,17},{2,10},{10... | collective-permute-start | bytes 196616 | tf_op jit(solution)/shard_map/ppermute | solution.py:344
  31.3 5.9 %collective-permute-start.12 = (bf16[2,272,128]{2,1,0:T(8,128)(2,1)S(1)}, bf16[2,272,128]{2,1,0:T(8,128)(2,1)S(1)}, u32[]{:S(2)}, u32[]{:S(2)}) collective-permute-start(bf16[2,272,128]{2,1,0:T(8,128)(2,1)S(1)} %get-tuple-element.99), channel_id=1, source_target_pairs={{0,1},{1,0},{2,3},{3,2},{4,5},{5,4},{6,7},{7,6},{8,9},{9,8},{10,11... | collective-permute-start | bytes 417800 | tf_op jit(solution)/shard_map/ppermute | solution.py:344
  31.4 6.6 %collective-permute-start.13 = (bf16[2,272,128]{2,1,0:T(8,128)(2,1)S(1)}, bf16[2,272,128]{2,1,0:T(8,128)(2,1)S(1)}, u32[]{:S(2)}, u32[]{:S(2)}) collective-permute-start(bf16[2,272,128]{2,1,0:T(8,128)(2,1)S(1)} %get-tuple-element.100), channel_id=1, source_target_pairs={{0,2},{1,3},{2,0},{3,1},{4,6},{5,7},{6,4},{7,5},{8,10},{9,11},{10,... | collective-permute-start | bytes 417800 | tf_op jit(solution)/shard_map/ppermute | solution.py:344
  31.8 9.0 %collective-permute-start.14 = (bf16[2,272,128]{2,1,0:T(8,128)(2,1)S(1)}, bf16[2,272,128]{2,1,0:T(8,128)(2,1)S(1)}, u32[]{:S(2)}, u32[]{:S(2)}) collective-permute-start(bf16[2,272,128]{2,1,0:T(8,128)(2,1)S(1)} %get-tuple-element.101), channel_id=1, source_target_pairs={{0,3},{1,2},{2,1},{3,0},{4,7},{5,6},{6,5},{7,4},{8,11},{9,10},{10,... | collective-permute-start | bytes 417800 | tf_op jit(solution)/shard_map/ppermute | solution.py:344
  34.8 2.4 %collective-permute-start.15 = (bf16[64,1024]{1,0:T(8,128)(2,1)S(1)}, bf16[64,1024]{1,0:T(8,128)(2,1)S(1)}, u32[]{:S(2)}, u32[]{:S(2)}) collective-permute-start(bf16[64,1024]{1,0:T(8,128)(2,1)S(1)} %get-tuple-element.102), channel_id=1, source_target_pairs={{0,0},{1,2},{2,1},{3,4},{4,3},{5,6},{6,5},{7,7},{8,8},{9,10},{10,9... | collective-permute-start | bytes 393224 | tf_op jit(solution)/shard_map/ppermute | solution.py:457
  40.9 9.0 %collective-permute-start.16 = (bf16[2,272,128]{2,1,0:T(8,128)(2,1)S(1)}, bf16[2,272,128]{2,1,0:T(8,128)(2,1)S(1)}, u32[]{:S(2)}, u32[]{:S(2)}) collective-permute-start(bf16[2,272,128]{2,1,0:T(8,128)(2,1)S(1)} %shard_map.95.refs_0_), channel_id=1, source_target_pairs={{0,4},{1,5},{2,6},{3,7},{4,0},{5,1},{6,2},{7,3},{8,12},{9,13},{10,... | collective-permute-start | bytes 417800 | tf_op jit(solution)/shard_map/ppermute | solution.py:344
  43.6 5.0 %collective-permute-start.17 = (bf16[64,1024]{1,0:T(8,128)(2,1)S(1)}, bf16[64,1024]{1,0:T(8,128)(2,1)S(1)}, u32[]{:S(2)}, u32[]{:S(2)}) collective-permute-start(bf16[64,1024]{1,0:T(8,128)(2,1)S(1)} %get-tuple-element.109), channel_id=1, source_target_pairs={{0,1},{1,0},{2,3},{3,2},{4,5},{5,4},{6,7},{7,6},{8,9},{9,8},{10,11... | collective-permute-start | bytes 393224 | tf_op jit(solution)/shard_map/ppermute | solution.py:481
  50.0 8.5 %collective-permute-start.18 = (bf16[2,272,128]{2,1,0:T(8,128)(2,1)S(1)}, bf16[2,272,128]{2,1,0:T(8,128)(2,1)S(1)}, u32[]{:S(2)}, u32[]{:S(2)}) collective-permute-start(bf16[2,272,128]{2,1,0:T(8,128)(2,1)S(1)} %get-tuple-element.116.refs_0_), channel_id=1, source_target_pairs={{0,16},{8,24},{16,0},{24,8},{1,17},{9,25},{17,1},{25,9},{2,18},{10... | collective-permute-start | bytes 417800 | tf_op jit(solution)/shard_map/ppermute | solution.py:344
  50.8 5.4 %collective-permute-start.21 = (bf16[2,160,128]{2,1,0:T(8,128)(2,1)S(1)}, bf16[2,160,128]{2,1,0:T(8,128)(2,1)S(1)}, u32[]{:S(2)}, u32[]{:S(2)}) collective-permute-start(bf16[2,160,128]{2,1,0:T(8,128)(2,1)S(1)} %get-tuple-element.112), channel_id=1, source_target_pairs={{0,3},{1,2},{2,1},{3,0},{4,7},{5,6},{6,5},{7,4},{8,11},{9,10},{10,... | collective-permute-start | bytes 245768 | tf_op jit(solution)/shard_map/ppermute | solution.py:344
  50.8 6.6 %collective-permute-start.20 = (bf16[2,160,128]{2,1,0:T(8,128)(2,1)S(1)}, bf16[2,160,128]{2,1,0:T(8,128)(2,1)S(1)}, u32[]{:S(2)}, u32[]{:S(2)}) collective-permute-start(bf16[2,160,128]{2,1,0:T(8,128)(2,1)S(1)} %get-tuple-element.112), channel_id=1, source_target_pairs={{0,2},{1,3},{2,0},{3,1},{4,6},{5,7},{6,4},{7,5},{8,10},{9,11},{10,... | collective-permute-start | bytes 245768 | tf_op jit(solution)/shard_map/ppermute | solution.py:344
  54.0 4.4 %collective-permute-start.19 = (bf16[2,160,128]{2,1,0:T(8,128)(2,1)S(1)}, bf16[2,160,128]{2,1,0:T(8,128)(2,1)S(1)}, u32[]{:S(2)}, u32[]{:S(2)}) collective-permute-start(bf16[2,160,128]{2,1,0:T(8,128)(2,1)S(1)} %get-tuple-element.112), channel_id=1, source_target_pairs={{0,1},{1,0},{2,3},{3,2},{4,5},{5,4},{6,7},{7,6},{8,9},{9,8},{10,11... | collective-permute-start | bytes 245768 | tf_op jit(solution)/shard_map/ppermute | solution.py:344
  58.5 10.2 %collective-permute-start.26 = (bf16[2048,128]{1,0:T(8,128)(2,1)S(1)}, bf16[2048,128]{1,0:T(8,128)(2,1)S(1)}, u32[]{:S(2)}, u32[]{:S(2)}) collective-permute-start(bf16[2048,128]{1,0:T(8,128)(2,1)S(1)} %shard_map.99.refs_0_), channel_id=1, source_target_pairs={{0,8},{8,0},{16,24},{24,16},{1,9},{9,1},{17,25},{25,17},{2,10},{10... | collective-permute-start | bytes 1572872 | tf_op jit(solution)/shard_map/ppermute | solution.py:344
  58.6 10.1 %collective-permute-start.22 = (bf16[6,160,128]{2,1,0:T(8,128)(2,1)S(1)}, bf16[6,160,128]{2,1,0:T(8,128)(2,1)S(1)}, u32[]{:S(2)}, u32[]{:S(2)}) collective-permute-start(bf16[6,160,128]{2,1,0:T(8,128)(2,1)S(1)} %shard_map.97), channel_id=1, source_target_pairs={{0,16},{8,24},{16,0},{24,8},{1,17},{9,25},{17,1},{25,9},{2,18},{10... | collective-permute-start | bytes 737288 | tf_op jit(solution)/shard_map/ppermute | solution.py:344
  60.0 6.9 %collective-permute-start.25 = (bf16[4,112,128]{2,1,0:T(8,128)(2,1)S(1)}, bf16[4,112,128]{2,1,0:T(8,128)(2,1)S(1)}, u32[]{:S(2)}, u32[]{:S(2)}) collective-permute-start(bf16[4,112,128]{2,1,0:T(8,128)(2,1)S(1)} %shard_map.98), channel_id=1, source_target_pairs={{0,3},{1,2},{2,1},{3,0},{4,7},{5,6},{6,5},{7,4},{8,11},{9,10},{10,... | collective-permute-start | bytes 344072 | tf_op jit(solution)/shard_map/ppermute | solution.py:344
  60.1 7.4 %collective-permute-start.24 = (bf16[4,112,128]{2,1,0:T(8,128)(2,1)S(1)}, bf16[4,112,128]{2,1,0:T(8,128)(2,1)S(1)}, u32[]{:S(2)}, u32[]{:S(2)}) collective-permute-start(bf16[4,112,128]{2,1,0:T(8,128)(2,1)S(1)} %shard_map.98), channel_id=1, source_target_pairs={{0,2},{1,3},{2,0},{3,1},{4,6},{5,7},{6,4},{7,5},{8,10},{9,11},{10,... | collective-permute-start | bytes 344072 | tf_op jit(solution)/shard_map/ppermute | solution.py:344
  61.9 6.8 %collective-permute-start.23 = (bf16[4,112,128]{2,1,0:T(8,128)(2,1)S(1)}, bf16[4,112,128]{2,1,0:T(8,128)(2,1)S(1)}, u32[]{:S(2)}, u32[]{:S(2)}) collective-permute-start(bf16[4,112,128]{2,1,0:T(8,128)(2,1)S(1)} %shard_map.98), channel_id=1, source_target_pairs={{0,1},{1,0},{2,3},{3,2},{4,5},{5,4},{6,7},{7,6},{8,9},{9,8},{10,11... | collective-permute-start | bytes 344072 | tf_op jit(solution)/shard_map/ppermute | solution.py:344
  68.7 2.0 %collective-permute-start.27 = (bf16[6,160,128]{2,1,0:T(8,128)(2,1)S(1)}, bf16[6,160,128]{2,1,0:T(8,128)(2,1)S(1)}, u32[]{:S(2)}, u32[]{:S(2)}) collective-permute-start(bf16[6,160,128]{2,1,0:T(8,128)(2,1)S(1)} %collective-permute-done.22.refs_1_), channel_id=1, source_target_pairs={{0,8},{8,0},{16,24},{24,16},{1,9},{9,1},{17,25},{25,17},{2,10},{10... | collective-permute-start | bytes 737288 | tf_op jit(solution)/shard_map/ppermute | solution.py:344
  68.7 2.0 %collective-permute-start.28 = (bf16[4,112,128]{2,1,0:T(8,128)(2,1)S(1)}, bf16[4,112,128]{2,1,0:T(8,128)(2,1)S(1)}, u32[]{:S(2)}, u32[]{:S(2)}) collective-permute-start(bf16[4,112,128]{2,1,0:T(8,128)(2,1)S(1)} %collective-permute-done.23.refs_2_), channel_id=1, source_target_pairs={{0,8},{8,0},{16,24},{24,16},{1,9},{9,1},{17,25},{25,17},{2,10},{10... | collective-permute-start | bytes 344072 | tf_op jit(solution)/shard_map/ppermute | solution.py:344
  69.2 1.5 %collective-permute-start.29 = (bf16[4,112,128]{2,1,0:T(8,128)(2,1)S(1)}, bf16[4,112,128]{2,1,0:T(8,128)(2,1)S(1)}, u32[]{:S(2)}, u32[]{:S(2)}) collective-permute-start(bf16[4,112,128]{2,1,0:T(8,128)(2,1)S(1)} %collective-permute-done.24.refs_3_), channel_id=1, source_target_pairs={{0,8},{8,0},{16,24},{24,16},{1,9},{9,1},{17,25},{25,17},{2,10},{10... | collective-permute-start | bytes 344072 | tf_op jit(solution)/shard_map/ppermute | solution.py:344
  69.3 1.4 %collective-permute-start.30 = (bf16[4,112,128]{2,1,0:T(8,128)(2,1)S(1)}, bf16[4,112,128]{2,1,0:T(8,128)(2,1)S(1)}, u32[]{:S(2)}, u32[]{:S(2)}) collective-permute-start(bf16[4,112,128]{2,1,0:T(8,128)(2,1)S(1)} %collective-permute-done.25.refs_4_), channel_id=1, source_target_pairs={{0,8},{8,0},{16,24},{24,16},{1,9},{9,1},{17,25},{25,17},{2,10},{10... | collective-permute-start | bytes 344072 | tf_op jit(solution)/shard_map/ppermute | solution.py:344
where the time goes:
time: 73.7 us; the launch traced here: 73.5 us
  starting transfers between devices  32 us (43%)
  waiting for transfers between devices  24.5 us (33%)
  Pallas kernels  11.5 us (16%)
  local copies, waits for them, and re-layouts  3.27 us (4%)
  other arithmetic  1.12 us (2%)
  between operations  1.06 us (1%)
    ppermute x25, starting transfers between devices, swapped(): lax.ppermute(part, axis, [(i, i ^ distance) for i in range(lax.axis_size(...  21.2 us
    ppermute x25, waiting for transfers between devices, swapped(): lax.ppermute(part, axis, [(i, i ^ distance) for i in range(lax.axis_size(...  17.6 us
    pallas_call x16, Pallas kernels, call(): pl.pallas_call(kernel, out_shape=out_shape, in_specs=[vmem] * len(args),...  11.5 us
    ppermute x2, starting transfers between devices, per_device(): grad_sides = [lax.ppermute(grad, 'space', pairs) for pairs in (even, odd)]  6.07 us
    ppermute x1, waiting for transfers between devices, per_device(): from_even = lax.ppermute(even_edge, 'space', even)  3.29 us
    ppermute x2, waiting for transfers between devices, per_device(): lax.ppermute(part, 'space', pairs)  2.98 us
    optimization_barrier x2, local copies, waits for them, and re-layouts, per_device(): lax.optimization_barrier((grad, layer_input, hidden_pre))  2.28 us
    ppermute x2, starting transfers between devices, per_device(): lax.ppermute(part, 'space', pairs)  2.17 us
  transfers between devices with their start and end apart: 31, of which 16 were waited for; matrix products, arithmetic and copies ran while one was open for 5% of the time, Pallas kernels for 12%

commit v1 on v0

--- a/solution.py
+++ b/solution.py
@@ -352,7 +352,6 @@
     samples, slabs = lax.axis_size("dp"), lax.axis_size("space")
     even = [(i, i ^ 1) for i in range(slabs)]
     odd = [(i, ((i + 1 ^ 1) - 1) % slabs) for i in range(slabs)]
-    odd_inside = [(i, k) if abs(i - k) == 1 else (i, i) for i, k in odd]
     shape = jax.ShapeDtypeStruct
     outer = output_pre[0, :, 0].astype(f32)
     grad = (output_grad[0, :, 0].astype(f32) * jnp.where(outer > 0, 1.0, negative_slope)).astype(bf16)
@@ -404,6 +403,15 @@
         hidden,
         matrix,
     )
+    edges = call(
+        lambda *refs: edges_kernel(side, *refs),
+        [shape((chan, size), bf16)] * 2,
+        [pltpu.VMEM((9 * chan, size), f32)],
+        1 << 28,
+        weight_a.reshape(27 * chan, width_a),
+        grad_hidden,
+    )
+    edges, source_sides = lax.optimization_barrier((edges, source_sides))
     halves = call(
         lambda *refs: sums_a_kernel(side, plan, *refs),
         [shape((plan.rows_a * slabs, width_a), kind) for kind in (f32, bf16) for _ in range(samples // 2)],
@@ -417,15 +425,7 @@
         *source_sides,
     )
     keep, send = halves[: samples // 2], halves[samples // 2 :]
-    edges = call(
-        lambda *refs: edges_kernel(side, *refs),
-        [shape((chan, size), bf16)] * 2,
-        [pltpu.VMEM((9 * chan, size), f32)],
-        1 << 28,
-        weight_a.reshape(27 * chan, width_a),
-        grad_hidden,
-    )
-    got_a, edges = lax.optimization_barrier(([swapped(part, "dp", 1) for part in send], edges))
+    got_a = [swapped(part, "dp", 1) for part in send]
     for stride in [1 << k for k in range(1, samples.bit_length() - 1)]:
         count = len(keep) // 2
         halves = call(
@@ -454,8 +454,9 @@
         *pooled_parts,
         *channel_parts,
     )
-    from_odd = lax.ppermute(edges[1], "space", odd_inside)
+    from_odd = lax.ppermute(edges[1], "space", odd)
     far = plan.far
+    totals, from_odd = lax.optimization_barrier((totals, from_odd))
     blocks = call(
         lambda *refs: blocks_kernel(plan, *refs),
         [shape((2, plan.block, 128), bf16)] * far,
@@ -474,7 +475,7 @@
         weight_a.reshape(27 * chan, width_a),
         grad_hidden,
     )
-    parts, from_odd, own = lax.optimization_barrier((parts, from_odd, own))
+    parts, own = lax.optimization_barrier((parts, own))
     both = call(near_kernel, shape((2, plan.block, 128), bf16), [], 1 << 20, *parts)
     there = swapped(both, "space", far)
     both, even_edge = lax.optimization_barrier((both, edges[0]))

time: 73.7 us -> 72.5 us (0.984)
  starting transfers between devices: 32 us -> 30.2 us
    ppermute x1, waiting for transfers between devices: 0.01 us -> 2.75 us  [per_device(): from_odd = lax.ppermute(edges[1], 'space', odd)]
    ppermute x25, starting transfers between devices: 21.2 us -> 19.3 us  [swapped(): lax.ppermute(part, axis, [(i, i ^ distance) for i in range(lax.axis_size(...]
    ppermute x2, waiting for transfers between devices: 2.98 us -> 1.41 us  [per_device(): lax.ppermute(part, 'space', pairs)]
    ppermute x25, waiting for transfers between devices: 17.6 us -> 16.1 us  [swapped(): lax.ppermute(part, axis, [(i, i ^ distance) for i in range(lax.axis_size(...]
    ppermute x1, starting transfers between devices: 0.84 us -> 1.94 us  [per_device(): from_odd = lax.ppermute(edges[1], 'space', odd)]
    ppermute x1, waiting for transfers between devices: 3.29 us -> 4.33 us  [per_device(): from_even = lax.ppermute(even_edge, 'space', even)]
    ppermute x1, starting transfers between devices: 1.68 us -> 0.7 us  [per_device(): from_even = lax.ppermute(even_edge, 'space', even)]
  transfers between devices with their start and end apart: 31 -> 31, of which waited for: 16 -> 13; matrix products, arithmetic and copies ran while one was open for 5% -> 5% of each run, Pallas kernels for 12% -> 12%
where the time goes in v1:
time: 72.5 us; the launch traced here: 72.3 us
  starting transfers between devices  30.2 us (42%)
  waiting for transfers between devices  25.2 us (35%)
  Pallas kernels  11.5 us (16%)
  local copies, waits for them, and re-layouts  3.27 us (5%)
  other arithmetic  1.12 us (2%)
  between operations  0.91 us (1%)
    ppermute x25, starting transfers between devices, swapped(): lax.ppermute(part, axis, [(i, i ^ distance) for i in range(lax.axis_size(...  19.3 us
    ppermute x25, waiting for transfers between devices, swapped(): lax.ppermute(part, axis, [(i, i ^ distance) for i in range(lax.axis_size(...  16.1 us
    pallas_call x16, Pallas kernels, call(): pl.pallas_call(kernel, out_shape=out_shape, in_specs=[vmem] * len(args),...  11.5 us
    ppermute x2, starting transfers between devices, per_device(): grad_sides = [lax.ppermute(grad, 'space', pairs) for pairs in (even, odd)]  6.07 us
    ppermute x1, waiting for transfers between devices, per_device(): from_even = lax.ppermute(even_edge, 'space', even)  4.33 us
    ppermute x1, waiting for transfers between devices, per_device(): from_odd = lax.ppermute(edges[1], 'space', odd)  2.75 us
    optimization_barrier x2, local copies, waits for them, and re-layouts, per_device(): lax.optimization_barrier((grad, layer_input, hidden_pre))  2.28 us
    ppermute x2, starting transfers between devices, per_device(): lax.ppermute(part, 'space', pairs)  2.17 us
  transfers between devices with their start and end apart: 31, of which 13 were waited for; matrix products, arithmetic and copies ran while one was open for 5% of the time, Pallas kernels for 12%

profile of v1, /device:TPU:0, one launch (start us, length us, event | category | flops | bytes accessed | tf_op | source)
XLA Modules:
  0.0 72.3 jit_solution(6950694586476277318)
XLA Ops:
  0.6 1.0 %fusion.1.refs_1_ = bf16[256,256]{1,0:T(8,128)(2,1)S(1)} fusion(bf16[1,256,1,256]{3,1,2,0:T(8,128)(2,1)} %param.8, bf16[1,256,1,256]{3,1,2,0:T(8,128)(2,1)} %param.9), kind=kLoop, calls=%fused_computation.6 | loop fusion | flops 393216 | bytes 393216 | tf_op jit(solution)/shard_map/mul | solution.py:357
  1.7 6.1 %collective-permute-start.1 = (bf16[256,256]{1,0:T(8,128)(2,1)S(1)}, bf16[256,256]{1,0:T(8,128)(2,1)S(1)}, u32[]{:S(2)}, u32[]{:S(2)}) collective-permute-start(bf16[256,256]{1,0:T(8,128)(2,1)S(1)} %fusion.1.refs_1_), channel_id=1, source_target_pairs={{0,7},{1,2},{2,1},{3,4},{4,3},{5,6},{6,5},{7,0},{8,15},{9,10},{10,... | collective-permute-start | bytes 393224 | tf_op jit(solution)/shard_map/ppermute | solution.py:359
  7.7 1.0 %copy.15 = bf16[1,64,2,1024]{3,1,2,0:T(8,128)(2,1)S(1)} copy(bf16[1,64,2,1024]{3,2,1,0:T(2,128)(2,1)} %param.6) | data formatting | bytes 524288 | tf_op jit(solution)/shard_map/optimization_barrier | solution.py:358
  8.7 1.3 %copy.14 = bf16[1,128,2,1024]{3,1,2,0:T(8,128)(2,1)S(1)} copy(bf16[1,128,2,1024]{3,2,1,0:T(2,128)(2,1)} %param.7) | data formatting | bytes 1048576 | tf_op jit(solution)/shard_map/optimization_barrier | solution.py:358
  10.0 0.5 shard_map.85
  10.6 2.1 %collective-permute-start.5 = (bf16[64,1024]{1,0:T(8,128)(2,1)S(1)}, bf16[64,1024]{1,0:T(8,128)(2,1)S(1)}, u32[]{:S(2)}, u32[]{:S(2)}) collective-permute-start(bf16[64,1024]{1,0:T(8,128)(2,1)S(1)} %get-tuple-element.86), channel_id=1, source_target_pairs={{0,1},{1,0},{2,3},{3,2},{4,5},{5,4},{6,7},{7,6},{8,9},{9,8},{10,11... | collective-permute-start | bytes 393224 | tf_op jit(solution)/shard_map/ppermute | solution.py:375
  12.7 0.1 collective-permute-start.6
  12.8 0.7 shard_map.86.refs_1_
  13.5 0.6 collective-permute-done.refs_2_
  14.2 1.6 %collective-permute-start.3 = (bf16[320,256]{1,0:T(8,128)(2,1)S(1)}, bf16[320,256]{1,0:T(8,128)(2,1)S(1)}, u32[]{:S(2)}, u32[]{:S(2)}) collective-permute-start(bf16[320,256]{1,0:T(8,128)(2,1)S(1)} %get-tuple-element.78), channel_id=1, source_target_pairs={{0,16},{8,24},{16,0},{24,8},{1,17},{9,25},{17,1},{25,9},{2,18},{10... | collective-permute-start | bytes 491528 | tf_op jit(solution)/shard_map/ppermute | solution.py:344
  15.8 1.6 %shard_map.88.refs_1_.refs_0_ = bf16[256,1024]{1,0:T(8,128)(2,1)S(1)} custom-call(bf16[3456,256]{1,0:T(8,128)(2,1)S(1)} %bitcast.32, bf16[256,256]{1,0:T(8,128)(2,1)S(1)} %fusion.1.refs_1_, bf16[256,256]{1,0:T(8,128)(2,1)S(1)} %get-tuple-element.80.refs_2_, bf16[256,256]{1,0:T(8,128)(2,1)S(1)} %get-tuple-element.81.refs_3_, ...), custom_call_target="tpu_custom_call" | custom-call | flops 262144 | bytes 1024 | tf_op jit(solution)/shard_map/pallas_call | solution.py:64
  17.4 1.6 %shard_map.89 = (bf16[64,1024]{1,0:T(8,128)(2,1)S(1)}, bf16[64,1024]{1,0:T(8,128)(2,1)S(1)}) custom-call(bf16[1728,128]{1,0:T(8,128)(2,1)S(1)} %bitcast.33, bf16[256,1024]{1,0:T(8,128)(2,1)S(1)} %shard_map.88.refs_1_.refs_0_), custom_call_target="tpu_custom_call" | custom-call | flops 65536 | bytes 1024 | tf_op jit(solution)/shard_map/pallas_call | solution.py:64
  19.0 1.4 %collective-permute-done.6.refs_3_ = bf16[64,1024]{1,0:T(8,128)(2,1)S(1)} collective-permute-done((bf16[64,1024]{1,0:T(8,128)(2,1)S(1)}, bf16[64,1024]{1,0:T(8,128)(2,1)S(1)}, u32[]{:S(2)}, u32[]{:S(2)}) %collective-permute-start.6) | collective-permute-done | bytes 131104 | tf_op jit(solution)/shard_map/ppermute | solution.py:375
  20.4 1.5 %shard_map.90 = (f32[448,128]{1,0:T(8,128)S(1)}, f32[448,128]{1,0:T(8,128)S(1)}, bf16[448,128]{1,0:T(8,128)(2,1)S(1)}, bf16[448,128]{1,0:T(8,128)(2,1)S(1)}) custom-call(bf16[256,1024]{1,0:T(8,128)(2,1)S(1)} %shard_map.88.refs_1_.refs_0_, bf16[2,576,1024]{2,1,0:T(8,128)(2,1)S(1)} %shard_map.86.refs_1_, bf16[64,1024]{1,0:T(8,128)(2,1)S(1)} %collective-permute-done.5.refs_2_, ...), custom_call_target="tpu_custom_call" | custom-call | flops 262144 | bytes 1024 | tf_op jit(solution)/shard_map/pallas_call | solution.py:64
  22.0 0.5 collective-permute-start.8
  22.5 1.5 %collective-permute-start.4 = (bf16[192,256]{1,0:T(8,128)(2,1)S(1)}, bf16[192,256]{1,0:T(8,128)(2,1)S(1)}, u32[]{:S(2)}, u32[]{:S(2)}) collective-permute-start(bf16[192,256]{1,0:T(8,128)(2,1)S(1)} %get-tuple-element.79), channel_id=1, source_target_pairs={{0,16},{8,24},{16,0},{24,8},{1,17},{9,25},{17,1},{25,9},{2,18},{10... | collective-permute-start | bytes 294920 | tf_op jit(solution)/shard_map/ppermute | solution.py:344
  24.0 1.9 %collective-permute-start.11 = (bf16[64,1024]{1,0:T(8,128)(2,1)S(1)}, bf16[64,1024]{1,0:T(8,128)(2,1)S(1)}, u32[]{:S(2)}, u32[]{:S(2)}) collective-permute-start(bf16[64,1024]{1,0:T(8,128)(2,1)S(1)} %get-tuple-element.97), channel_id=1, source_target_pairs={{0,7},{1,2},{2,1},{3,4},{4,3},{5,6},{6,5},{7,0},{8,15},{9,10},{10,... | collective-permute-start | bytes 393224 | tf_op jit(solution)/shard_map/ppermute | solution.py:457
  26.0 1.3 %collective-permute-start.12 = (bf16[448,128]{1,0:T(8,128)(2,1)S(1)}, bf16[448,128]{1,0:T(8,128)(2,1)S(1)}, u32[]{:S(2)}, u32[]{:S(2)}) collective-permute-start(bf16[448,128]{1,0:T(8,128)(2,1)S(1)} %get-tuple-element.100), channel_id=1, source_target_pairs={{0,16},{8,24},{16,0},{24,8},{1,17},{9,25},{17,1},{25,9},{2,18},{10... | collective-permute-start | bytes 344072 | tf_op jit(solution)/shard_map/ppermute | solution.py:344
  27.3 0.5 collective-permute-start.9
  27.8 0.9 %collective-permute-done.9.refs_3_ = bf16[128,256]{1,0:T(8,128)(2,1)S(1)} collective-permute-done((bf16[128,256]{1,0:T(8,128)(2,1)S(1)}, bf16[128,256]{1,0:T(8,128)(2,1)S(1)}, u32[]{:S(2)}, u32[]{:S(2)}) %collective-permute-start.9) | collective-permute-done | bytes 65568 | tf_op jit(solution)/shard_map/ppermute | solution.py:344
  28.7 1.1 %shard_map.92.refs_0_ = f32[8,216,128]{2,1,0:T(8,128)S(1)} custom-call(bf16[320,256]{1,0:T(8,128)(2,1)S(1)} %get-tuple-element.76.refs_0_.refs_4_, bf16[320,256]{1,0:T(8,128)(2,1)S(1)} %collective-permute-done.2.refs_1_.refs_5_, bf16[320,256]{1,0:T(8,128)(2,1)S(1)} %collective-permute-done.3.refs_2_.refs_6_, ...), custom_call_target="tpu_custom_call" | custom-call | flops 262144 | bytes 1024 | tf_op jit(solution)/shard_map/pallas_call | solution.py:64
  29.8 2.8 %collective-permute-done.11 = bf16[64,1024]{1,0:T(8,128)(2,1)S(1)} collective-permute-done((bf16[64,1024]{1,0:T(8,128)(2,1)S(1)}, bf16[64,1024]{1,0:T(8,128)(2,1)S(1)}, u32[]{:S(2)}, u32[]{:S(2)}) %collective-permute-start.11) | collective-permute-done | bytes 131104 | tf_op jit(solution)/shard_map/ppermute | solution.py:457
  32.6 0.1 shard_map.93
  32.8 3.4 %collective-permute-start.15 = (bf16[2,272,128]{2,1,0:T(8,128)(2,1)S(1)}, bf16[2,272,128]{2,1,0:T(8,128)(2,1)S(1)}, u32[]{:S(2)}, u32[]{:S(2)}) collective-permute-start(bf16[2,272,128]{2,1,0:T(8,128)(2,1)S(1)} %get-tuple-element.104), channel_id=1, source_target_pairs={{0,3},{1,2},{2,1},{3,0},{4,7},{5,6},{6,5},{7,4},{8,11},{9,10},{10,... | collective-permute-start | bytes 417800 | tf_op jit(solution)/shard_map/ppermute | solution.py:344
  36.2 1.5 %shard_map.94 = f32[2,64,1024]{2,1,0:T(8,128)S(1)} custom-call(bf16[1728,128]{1,0:T(8,128)(2,1)S(1)} %bitcast.34, bf16[256,1024]{1,0:T(8,128)(2,1)S(1)} %shard_map.88.refs_1_.refs_0_), custom_call_target="tpu_custom_call" | custom-call | flops 65536 | bytes 1024 | tf_op jit(solution)/shard_map/pallas_call | solution.py:64
  37.7 0.7 collective-permute-done.13.refs_1_
  38.4 1.0 %collective-permute-done.14.refs_2_ = bf16[2,272,128]{2,1,0:T(8,128)(2,1)S(1)} collective-permute-done((bf16[2,272,128]{2,1,0:T(8,128)(2,1)S(1)}, bf16[2,272,128]{2,1,0:T(8,128)(2,1)S(1)}, u32[]{:S(2)}, u32[]{:S(2)}) %collective-permute-start.14) | collective-permute-done | bytes 139296 | tf_op jit(solution)/shard_map/ppermute | solution.py:344
  39.4 2.8 %collective-permute-done.15.refs_3_ = bf16[2,272,128]{2,1,0:T(8,128)(2,1)S(1)} collective-permute-done((bf16[2,272,128]{2,1,0:T(8,128)(2,1)S(1)}, bf16[2,272,128]{2,1,0:T(8,128)(2,1)S(1)}, u32[]{:S(2)}, u32[]{:S(2)}) %collective-permute-start.15) | collective-permute-done | bytes 139296 | tf_op jit(solution)/shard_map/ppermute | solution.py:344
  42.2 0.1 shard_map.95.refs_0_
  42.3 0.7 collective-permute-start.17
  43.0 4.3 %collective-permute-done.17 = bf16[64,1024]{1,0:T(8,128)(2,1)S(1)} collective-permute-done((bf16[64,1024]{1,0:T(8,128)(2,1)S(1)}, bf16[64,1024]{1,0:T(8,128)(2,1)S(1)}, u32[]{:S(2)}, u32[]{:S(2)}) %collective-permute-start.17) | collective-permute-done | bytes 131104 | tf_op jit(solution)/shard_map/ppermute | solution.py:482
  47.4 2.6 %collective-permute-done.16.refs_1_ = bf16[2,272,128]{2,1,0:T(8,128)(2,1)S(1)} collective-permute-done((bf16[2,272,128]{2,1,0:T(8,128)(2,1)S(1)}, bf16[2,272,128]{2,1,0:T(8,128)(2,1)S(1)}, u32[]{:S(2)}, u32[]{:S(2)}) %collective-permute-start.16) | collective-permute-done | bytes 139296 | tf_op jit(solution)/shard_map/ppermute | solution.py:344
  50.1 1.0 %collective-permute-start.21 = (bf16[2,160,128]{2,1,0:T(8,128)(2,1)S(1)}, bf16[2,160,128]{2,1,0:T(8,128)(2,1)S(1)}, u32[]{:S(2)}, u32[]{:S(2)}) collective-permute-start(bf16[2,160,128]{2,1,0:T(8,128)(2,1)S(1)} %get-tuple-element.114), channel_id=1, source_target_pairs={{0,3},{1,2},{2,1},{3,0},{4,7},{5,6},{6,5},{7,4},{8,11},{9,10},{10,... | collective-permute-start | bytes 245768 | tf_op jit(solution)/shard_map/ppermute | solution.py:344
  51.1 1.0 %collective-permute-start.20 = (bf16[2,160,128]{2,1,0:T(8,128)(2,1)S(1)}, bf16[2,160,128]{2,1,0:T(8,128)(2,1)S(1)}, u32[]{:S(2)}, u32[]{:S(2)}) collective-permute-start(bf16[2,160,128]{2,1,0:T(8,128)(2,1)S(1)} %get-tuple-element.114), channel_id=1, source_target_pairs={{0,2},{1,3},{2,0},{3,1},{4,6},{5,7},{6,4},{7,5},{8,10},{9,11},{10,... | collective-permute-start | bytes 245768 | tf_op jit(solution)/shard_map/ppermute | solution.py:344
  52.2 1.5 %collective-permute-start.19 = (bf16[2,160,128]{2,1,0:T(8,128)(2,1)S(1)}, bf16[2,160,128]{2,1,0:T(8,128)(2,1)S(1)}, u32[]{:S(2)}, u32[]{:S(2)}) collective-permute-start(bf16[2,160,128]{2,1,0:T(8,128)(2,1)S(1)} %get-tuple-element.114), channel_id=1, source_target_pairs={{0,1},{1,0},{2,3},{3,2},{4,5},{5,4},{6,7},{7,6},{8,9},{9,8},{10,11... | collective-permute-start | bytes 245768 | tf_op jit(solution)/shard_map/ppermute | solution.py:344
  53.7 1.9 %collective-permute-done.21.refs_2_.refs_4_ = bf16[2,160,128]{2,1,0:T(8,128)(2,1)S(1)} collective-permute-done((bf16[2,160,128]{2,1,0:T(8,128)(2,1)S(1)}, bf16[2,160,128]{2,1,0:T(8,128)(2,1)S(1)}, u32[]{:S(2)}, u32[]{:S(2)}) %collective-permute-start.21) | collective-permute-done | bytes 81952 | tf_op jit(solution)/shard_map/ppermute | solution.py:344
  55.6 1.0 %collective-permute-done.19.refs_0_.refs_2_ = bf16[2,160,128]{2,1,0:T(8,128)(2,1)S(1)} collective-permute-done((bf16[2,160,128]{2,1,0:T(8,128)(2,1)S(1)}, bf16[2,160,128]{2,1,0:T(8,128)(2,1)S(1)}, u32[]{:S(2)}, u32[]{:S(2)}) %collective-permute-start.19) | collective-permute-done | bytes 81952 | tf_op jit(solution)/shard_map/ppermute | solution.py:344
  56.8 2.0 %collective-permute-start.22 = (bf16[6,160,128]{2,1,0:T(8,128)(2,1)S(1)}, bf16[6,160,128]{2,1,0:T(8,128)(2,1)S(1)}, u32[]{:S(2)}, u32[]{:S(2)}) collective-permute-start(bf16[6,160,128]{2,1,0:T(8,128)(2,1)S(1)} %shard_map.97), channel_id=1, source_target_pairs={{0,16},{8,24},{16,0},{24,8},{1,17},{9,25},{17,1},{25,9},{2,18},{10... | collective-permute-start | bytes 737288 | tf_op jit(solution)/shard_map/ppermute | solution.py:344
  58.8 1.0 %collective-permute-start.25 = (bf16[4,112,128]{2,1,0:T(8,128)(2,1)S(1)}, bf16[4,112,128]{2,1,0:T(8,128)(2,1)S(1)}, u32[]{:S(2)}, u32[]{:S(2)}) collective-permute-start(bf16[4,112,128]{2,1,0:T(8,128)(2,1)S(1)} %shard_map.98), channel_id=1, source_target_pairs={{0,3},{1,2},{2,1},{3,0},{4,7},{5,6},{6,5},{7,4},{8,11},{9,10},{10,... | collective-permute-start | bytes 344072 | tf_op jit(solution)/shard_map/ppermute | solution.py:344
  59.9 2.0 %collective-permute-start.24 = (bf16[4,112,128]{2,1,0:T(8,128)(2,1)S(1)}, bf16[4,112,128]{2,1,0:T(8,128)(2,1)S(1)}, u32[]{:S(2)}, u32[]{:S(2)}) collective-permute-start(bf16[4,112,128]{2,1,0:T(8,128)(2,1)S(1)} %shard_map.98), channel_id=1, source_target_pairs={{0,2},{1,3},{2,0},{3,1},{4,6},{5,7},{6,4},{7,5},{8,10},{9,11},{10,... | collective-permute-start | bytes 344072 | tf_op jit(solution)/shard_map/ppermute | solution.py:344
  61.9 0.5 collective-permute-start.23
  62.5 3.3 %collective-permute-done.25.refs_4_ = bf16[4,112,128]{2,1,0:T(8,128)(2,1)S(1)} collective-permute-done((bf16[4,112,128]{2,1,0:T(8,128)(2,1)S(1)}, bf16[4,112,128]{2,1,0:T(8,128)(2,1)S(1)}, u32[]{:S(2)}, u32[]{:S(2)}) %collective-permute-start.25) | collective-permute-done | bytes 114720 | tf_op jit(solution)/shard_map/ppermute | solution.py:344
  65.8 1.8 %collective-permute-done.24.refs_3_ = bf16[4,112,128]{2,1,0:T(8,128)(2,1)S(1)} collective-permute-done((bf16[4,112,128]{2,1,0:T(8,128)(2,1)S(1)}, bf16[4,112,128]{2,1,0:T(8,128)(2,1)S(1)}, u32[]{:S(2)}, u32[]{:S(2)}) %collective-permute-start.24) | collective-permute-done | bytes 114720 | tf_op jit(solution)/shard_map/ppermute | solution.py:344
  67.7 0.5 collective-permute-start.28
  68.2 0.1 collective-permute-start.29
  68.2 0.4 collective-permute-start.30
  68.7 1.0 %copy.11 = bf16[1,64,2,1024]{3,2,1,0:T(2,128)(2,1)} copy(bf16[1,64,2,1024]{3,1,2,0:T(8,128)(2,1)S(1)} %fusion) | data formatting | bytes 524288
  69.7 2.6 %shard_map.100 = (f32[1728,128]{1,0:T(8,128)}, f32[3456,256]{1,0:T(8,128)}) custom-call(bf16[2048,128]{1,0:T(8,128)(2,1)S(1)} %shard_map.99.refs_0_, bf16[6,160,128]{2,1,0:T(8,128)(2,1)S(1)} %collective-permute-done.22.refs_1_, bf16[4,112,128]{2,1,0:T(8,128)(2,1)S(1)} %collective-permute-done.23.refs_2_, ...), custom_call_target="tpu_custom_call" | custom-call | flops 256 | bytes 1024 | tf_op jit(solution)/shard_map/pallas_call | solution.py:64
  (42 shorter events, 0.9 us)
Async XLA Ops:
  1.7 11.8 %collective-permute-start.1 = (bf16[256,256]{1,0:T(8,128)(2,1)S(1)}, bf16[256,256]{1,0:T(8,128)(2,1)S(1)}, u32[]{:S(2)}, u32[]{:S(2)}) collective-permute-start(bf16[256,256]{1,0:T(8,128)(2,1)S(1)} %fusion.1.refs_1_), channel_id=1, source_target_pairs={{0,7},{1,2},{2,1},{3,4},{4,3},{5,6},{6,5},{7,0},{8,15},{9,10},{10,... | collective-permute-start | bytes 393224 | tf_op jit(solution)/shard_map/ppermute | solution.py:359
  7.7 6.4 %collective-permute-start = (bf16[256,256]{1,0:T(8,128)(2,1)S(1)}, bf16[256,256]{1,0:T(8,128)(2,1)S(1)}, u32[]{:S(2)}, u32[]{:S(2)}) collective-permute-start(bf16[256,256]{1,0:T(8,128)(2,1)S(1)} %fusion.1.refs_1_), channel_id=1, source_target_pairs={{0,1},{1,0},{2,3},{3,2},{4,5},{5,4},{6,7},{7,6},{8,9},{9,8},{10,11... | collective-permute-start | bytes 393224 | tf_op jit(solution)/shard_map/ppermute | solution.py:359
  8.7 7.0 %copy-start = (bf16[27,128,256]{2,1,0:T(8,128)(2,1)S(1)}, bf16[27,128,256]{2,1,0:T(8,128)(2,1)}, u32[]{:S(2)}) copy-start(bf16[27,128,256]{2,1,0:T(8,128)(2,1)} %param.11) | copy-start | bytes 5308420
  10.6 8.3 %collective-permute-start.5 = (bf16[64,1024]{1,0:T(8,128)(2,1)S(1)}, bf16[64,1024]{1,0:T(8,128)(2,1)S(1)}, u32[]{:S(2)}, u32[]{:S(2)}) collective-permute-start(bf16[64,1024]{1,0:T(8,128)(2,1)S(1)} %get-tuple-element.86), channel_id=1, source_target_pairs={{0,1},{1,0},{2,3},{3,2},{4,5},{5,4},{6,7},{7,6},{8,9},{9,8},{10,11... | collective-permute-start | bytes 393224 | tf_op jit(solution)/shard_map/ppermute | solution.py:375
  12.7 7.7 %collective-permute-start.6 = (bf16[64,1024]{1,0:T(8,128)(2,1)S(1)}, bf16[64,1024]{1,0:T(8,128)(2,1)S(1)}, u32[]{:S(2)}, u32[]{:S(2)}) collective-permute-start(bf16[64,1024]{1,0:T(8,128)(2,1)S(1)} %get-tuple-element.87), channel_id=1, source_target_pairs={{0,7},{1,2},{2,1},{3,4},{4,3},{5,6},{6,5},{7,0},{8,15},{9,10},{10,... | collective-permute-start | bytes 393224 | tf_op jit(solution)/shard_map/ppermute | solution.py:375
  13.5 3.9 %copy-start.1 = (bf16[27,64,128]{2,1,0:T(8,128)(2,1)S(1)}, bf16[27,64,128]{2,1,0:T(8,128)(2,1)}, u32[]{:S(2)}) copy-start(bf16[27,64,128]{2,1,0:T(8,128)(2,1)} %param.10) | copy-start | bytes 1327108
  14.2 13.1 %collective-permute-start.3 = (bf16[320,256]{1,0:T(8,128)(2,1)S(1)}, bf16[320,256]{1,0:T(8,128)(2,1)S(1)}, u32[]{:S(2)}, u32[]{:S(2)}) collective-permute-start(bf16[320,256]{1,0:T(8,128)(2,1)S(1)} %get-tuple-element.78), channel_id=1, source_target_pairs={{0,16},{8,24},{16,0},{24,8},{1,17},{9,25},{17,1},{25,9},{2,18},{10... | collective-permute-start | bytes 491528 | tf_op jit(solution)/shard_map/ppermute | solution.py:344
  21.9 2.1 %collective-permute-start.7 = (bf16[448,128]{1,0:T(8,128)(2,1)S(1)}, bf16[448,128]{1,0:T(8,128)(2,1)S(1)}, u32[]{:S(2)}, u32[]{:S(2)}) collective-permute-start(bf16[448,128]{1,0:T(8,128)(2,1)S(1)} %get-tuple-element.92), channel_id=1, source_target_pairs={{0,8},{8,0},{16,24},{24,16},{1,9},{9,1},{17,25},{25,17},{2,10},{10... | collective-permute-start | bytes 344072 | tf_op jit(solution)/shard_map/ppermute | solution.py:344
  22.0 3.9 %collective-permute-start.8 = (bf16[448,128]{1,0:T(8,128)(2,1)S(1)}, bf16[448,128]{1,0:T(8,128)(2,1)S(1)}, u32[]{:S(2)}, u32[]{:S(2)}) collective-permute-start(bf16[448,128]{1,0:T(8,128)(2,1)S(1)} %get-tuple-element.93), channel_id=1, source_target_pairs={{0,8},{8,0},{16,24},{24,16},{1,9},{9,1},{17,25},{25,17},{2,10},{10... | collective-permute-start | bytes 344072 | tf_op jit(solution)/shard_map/ppermute | solution.py:344
  22.5 4.8 %collective-permute-start.4 = (bf16[192,256]{1,0:T(8,128)(2,1)S(1)}, bf16[192,256]{1,0:T(8,128)(2,1)S(1)}, u32[]{:S(2)}, u32[]{:S(2)}) collective-permute-start(bf16[192,256]{1,0:T(8,128)(2,1)S(1)} %get-tuple-element.79), channel_id=1, source_target_pairs={{0,16},{8,24},{16,0},{24,8},{1,17},{9,25},{17,1},{25,9},{2,18},{10... | collective-permute-start | bytes 294920 | tf_op jit(solution)/shard_map/ppermute | solution.py:344
  24.0 3.8 %collective-permute-start.2 = (bf16[320,256]{1,0:T(8,128)(2,1)S(1)}, bf16[320,256]{1,0:T(8,128)(2,1)S(1)}, u32[]{:S(2)}, u32[]{:S(2)}) collective-permute-start(bf16[320,256]{1,0:T(8,128)(2,1)S(1)} %get-tuple-element.77), channel_id=1, source_target_pairs={{0,8},{8,0},{16,24},{24,16},{1,9},{9,1},{17,25},{25,17},{2,10},{10... | collective-permute-start | bytes 491528 | tf_op jit(solution)/shard_map/ppermute | solution.py:344
  24.0 8.6 %collective-permute-start.11 = (bf16[64,1024]{1,0:T(8,128)(2,1)S(1)}, bf16[64,1024]{1,0:T(8,128)(2,1)S(1)}, u32[]{:S(2)}, u32[]{:S(2)}) collective-permute-start(bf16[64,1024]{1,0:T(8,128)(2,1)S(1)} %get-tuple-element.97), channel_id=1, source_target_pairs={{0,7},{1,2},{2,1},{3,4},{4,3},{5,6},{6,5},{7,0},{8,15},{9,10},{10,... | collective-permute-start | bytes 393224 | tf_op jit(solution)/shard_map/ppermute | solution.py:457
  26.0 6.6 %collective-permute-start.12 = (bf16[448,128]{1,0:T(8,128)(2,1)S(1)}, bf16[448,128]{1,0:T(8,128)(2,1)S(1)}, u32[]{:S(2)}, u32[]{:S(2)}) collective-permute-start(bf16[448,128]{1,0:T(8,128)(2,1)S(1)} %get-tuple-element.100), channel_id=1, source_target_pairs={{0,16},{8,24},{16,0},{24,8},{1,17},{9,25},{17,1},{25,9},{2,18},{10... | collective-permute-start | bytes 344072 | tf_op jit(solution)/shard_map/ppermute | solution.py:344
  27.2 1.4 %collective-permute-start.10 = (bf16[192,256]{1,0:T(8,128)(2,1)S(1)}, bf16[192,256]{1,0:T(8,128)(2,1)S(1)}, u32[]{:S(2)}, u32[]{:S(2)}) collective-permute-start(bf16[192,256]{1,0:T(8,128)(2,1)S(1)} %collective-permute-done.4), channel_id=1, source_target_pairs={{0,8},{8,0},{16,24},{24,16},{1,9},{9,1},{17,25},{25,17},{2,10},{10... | collective-permute-start | bytes 294920 | tf_op jit(solution)/shard_map/ppermute | solution.py:344
  27.3 1.4 %collective-permute-start.9 = (bf16[128,256]{1,0:T(8,128)(2,1)S(1)}, bf16[128,256]{1,0:T(8,128)(2,1)S(1)}, u32[]{:S(2)}, u32[]{:S(2)}) collective-permute-start(bf16[128,256]{1,0:T(8,128)(2,1)S(1)} %slice.11), channel_id=1, source_target_pairs={{0,8},{8,0},{16,24},{24,16},{1,9},{9,1},{17,25},{25,17},{2,10},{10... | collective-permute-start | bytes 196616 | tf_op jit(solution)/shard_map/ppermute | solution.py:344
  32.7 5.8 %collective-permute-start.13 = (bf16[2,272,128]{2,1,0:T(8,128)(2,1)S(1)}, bf16[2,272,128]{2,1,0:T(8,128)(2,1)S(1)}, u32[]{:S(2)}, u32[]{:S(2)}) collective-permute-start(bf16[2,272,128]{2,1,0:T(8,128)(2,1)S(1)} %get-tuple-element.102), channel_id=1, source_target_pairs={{0,1},{1,0},{2,3},{3,2},{4,5},{5,4},{6,7},{7,6},{8,9},{9,8},{10,11... | collective-permute-start | bytes 417800 | tf_op jit(solution)/shard_map/ppermute | solution.py:344
  32.7 6.6 %collective-permute-start.14 = (bf16[2,272,128]{2,1,0:T(8,128)(2,1)S(1)}, bf16[2,272,128]{2,1,0:T(8,128)(2,1)S(1)}, u32[]{:S(2)}, u32[]{:S(2)}) collective-permute-start(bf16[2,272,128]{2,1,0:T(8,128)(2,1)S(1)} %get-tuple-element.103), channel_id=1, source_target_pairs={{0,2},{1,3},{2,0},{3,1},{4,6},{5,7},{6,4},{7,5},{8,10},{9,11},{10,... | collective-permute-start | bytes 417800 | tf_op jit(solution)/shard_map/ppermute | solution.py:344
  32.8 9.4 %collective-permute-start.15 = (bf16[2,272,128]{2,1,0:T(8,128)(2,1)S(1)}, bf16[2,272,128]{2,1,0:T(8,128)(2,1)S(1)}, u32[]{:S(2)}, u32[]{:S(2)}) collective-permute-start(bf16[2,272,128]{2,1,0:T(8,128)(2,1)S(1)} %get-tuple-element.104), channel_id=1, source_target_pairs={{0,3},{1,2},{2,1},{3,0},{4,7},{5,6},{6,5},{7,4},{8,11},{9,10},{10,... | collective-permute-start | bytes 417800 | tf_op jit(solution)/shard_map/ppermute | solution.py:344
  42.3 7.8 %collective-permute-start.16 = (bf16[2,272,128]{2,1,0:T(8,128)(2,1)S(1)}, bf16[2,272,128]{2,1,0:T(8,128)(2,1)S(1)}, u32[]{:S(2)}, u32[]{:S(2)}) collective-permute-start(bf16[2,272,128]{2,1,0:T(8,128)(2,1)S(1)} %shard_map.95.refs_0_), channel_id=1, source_target_pairs={{0,4},{1,5},{2,6},{3,7},{4,0},{5,1},{6,2},{7,3},{8,12},{9,13},{10,... | collective-permute-start | bytes 417800 | tf_op jit(solution)/shard_map/ppermute | solution.py:344
  42.3 5.0 %collective-permute-start.17 = (bf16[64,1024]{1,0:T(8,128)(2,1)S(1)}, bf16[64,1024]{1,0:T(8,128)(2,1)S(1)}, u32[]{:S(2)}, u32[]{:S(2)}) collective-permute-start(bf16[64,1024]{1,0:T(8,128)(2,1)S(1)} %get-tuple-element.111), channel_id=1, source_target_pairs={{0,1},{1,0},{2,3},{3,2},{4,5},{5,4},{6,7},{7,6},{8,9},{9,8},{10,11... | collective-permute-start | bytes 393224 | tf_op jit(solution)/shard_map/ppermute | solution.py:482
  50.1 6.6 %collective-permute-start.18 = (bf16[2,272,128]{2,1,0:T(8,128)(2,1)S(1)}, bf16[2,272,128]{2,1,0:T(8,128)(2,1)S(1)}, u32[]{:S(2)}, u32[]{:S(2)}) collective-permute-start(bf16[2,272,128]{2,1,0:T(8,128)(2,1)S(1)} %get-tuple-element.118.refs_0_), channel_id=1, source_target_pairs={{0,16},{8,24},{16,0},{24,8},{1,17},{9,25},{17,1},{25,9},{2,18},{10... | collective-permute-start | bytes 417800 | tf_op jit(solution)/shard_map/ppermute | solution.py:344
  50.1 5.4 %collective-permute-start.21 = (bf16[2,160,128]{2,1,0:T(8,128)(2,1)S(1)}, bf16[2,160,128]{2,1,0:T(8,128)(2,1)S(1)}, u32[]{:S(2)}, u32[]{:S(2)}) collective-permute-start(bf16[2,160,128]{2,1,0:T(8,128)(2,1)S(1)} %get-tuple-element.114), channel_id=1, source_target_pairs={{0,3},{1,2},{2,1},{3,0},{4,7},{5,6},{6,5},{7,4},{8,11},{9,10},{10,... | collective-permute-start | bytes 245768 | tf_op jit(solution)/shard_map/ppermute | solution.py:344
  51.1 4.4 %collective-permute-start.20 = (bf16[2,160,128]{2,1,0:T(8,128)(2,1)S(1)}, bf16[2,160,128]{2,1,0:T(8,128)(2,1)S(1)}, u32[]{:S(2)}, u32[]{:S(2)}) collective-permute-start(bf16[2,160,128]{2,1,0:T(8,128)(2,1)S(1)} %get-tuple-element.114), channel_id=1, source_target_pairs={{0,2},{1,3},{2,0},{3,1},{4,6},{5,7},{6,4},{7,5},{8,10},{9,11},{10,... | collective-permute-start | bytes 245768 | tf_op jit(solution)/shard_map/ppermute | solution.py:344
  52.2 4.4 %collective-permute-start.19 = (bf16[2,160,128]{2,1,0:T(8,128)(2,1)S(1)}, bf16[2,160,128]{2,1,0:T(8,128)(2,1)S(1)}, u32[]{:S(2)}, u32[]{:S(2)}) collective-permute-start(bf16[2,160,128]{2,1,0:T(8,128)(2,1)S(1)} %get-tuple-element.114), channel_id=1, source_target_pairs={{0,1},{1,0},{2,3},{3,2},{4,5},{5,4},{6,7},{7,6},{8,9},{9,8},{10,11... | collective-permute-start | bytes 245768 | tf_op jit(solution)/shard_map/ppermute | solution.py:344
  56.7 10.9 %collective-permute-start.26 = (bf16[2048,128]{1,0:T(8,128)(2,1)S(1)}, bf16[2048,128]{1,0:T(8,128)(2,1)S(1)}, u32[]{:S(2)}, u32[]{:S(2)}) collective-permute-start(bf16[2048,128]{1,0:T(8,128)(2,1)S(1)} %shard_map.99.refs_0_), channel_id=1, source_target_pairs={{0,8},{8,0},{16,24},{24,16},{1,9},{9,1},{17,25},{25,17},{2,10},{10... | collective-permute-start | bytes 1572872 | tf_op jit(solution)/shard_map/ppermute | solution.py:344
  56.8 10.8 %collective-permute-start.22 = (bf16[6,160,128]{2,1,0:T(8,128)(2,1)S(1)}, bf16[6,160,128]{2,1,0:T(8,128)(2,1)S(1)}, u32[]{:S(2)}, u32[]{:S(2)}) collective-permute-start(bf16[6,160,128]{2,1,0:T(8,128)(2,1)S(1)} %shard_map.97), channel_id=1, source_target_pairs={{0,16},{8,24},{16,0},{24,8},{1,17},{9,25},{17,1},{25,9},{2,18},{10... | collective-permute-start | bytes 737288 | tf_op jit(solution)/shard_map/ppermute | solution.py:344
  58.8 6.9 %collective-permute-start.25 = (bf16[4,112,128]{2,1,0:T(8,128)(2,1)S(1)}, bf16[4,112,128]{2,1,0:T(8,128)(2,1)S(1)}, u32[]{:S(2)}, u32[]{:S(2)}) collective-permute-start(bf16[4,112,128]{2,1,0:T(8,128)(2,1)S(1)} %shard_map.98), channel_id=1, source_target_pairs={{0,3},{1,2},{2,1},{3,0},{4,7},{5,6},{6,5},{7,4},{8,11},{9,10},{10,... | collective-permute-start | bytes 344072 | tf_op jit(solution)/shard_map/ppermute | solution.py:344
  59.9 7.7 %collective-permute-start.24 = (bf16[4,112,128]{2,1,0:T(8,128)(2,1)S(1)}, bf16[4,112,128]{2,1,0:T(8,128)(2,1)S(1)}, u32[]{:S(2)}, u32[]{:S(2)}) collective-permute-start(bf16[4,112,128]{2,1,0:T(8,128)(2,1)S(1)} %shard_map.98), channel_id=1, source_target_pairs={{0,2},{1,3},{2,0},{3,1},{4,6},{5,7},{6,4},{7,5},{8,10},{9,11},{10,... | collective-permute-start | bytes 344072 | tf_op jit(solution)/shard_map/ppermute | solution.py:344
  61.9 5.7 %collective-permute-start.23 = (bf16[4,112,128]{2,1,0:T(8,128)(2,1)S(1)}, bf16[4,112,128]{2,1,0:T(8,128)(2,1)S(1)}, u32[]{:S(2)}, u32[]{:S(2)}) collective-permute-start(bf16[4,112,128]{2,1,0:T(8,128)(2,1)S(1)} %shard_map.98), channel_id=1, source_target_pairs={{0,1},{1,0},{2,3},{3,2},{4,5},{5,4},{6,7},{7,6},{8,9},{9,8},{10,11... | collective-permute-start | bytes 344072 | tf_op jit(solution)/shard_map/ppermute | solution.py:344
  67.6 2.1 %collective-permute-start.27 = (bf16[6,160,128]{2,1,0:T(8,128)(2,1)S(1)}, bf16[6,160,128]{2,1,0:T(8,128)(2,1)S(1)}, u32[]{:S(2)}, u32[]{:S(2)}) collective-permute-start(bf16[6,160,128]{2,1,0:T(8,128)(2,1)S(1)} %collective-permute-done.22.refs_1_), channel_id=1, source_target_pairs={{0,8},{8,0},{16,24},{24,16},{1,9},{9,1},{17,25},{25,17},{2,10},{10... | collective-permute-start | bytes 737288 | tf_op jit(solution)/shard_map/ppermute | solution.py:344
  67.7 2.0 %collective-permute-start.28 = (bf16[4,112,128]{2,1,0:T(8,128)(2,1)S(1)}, bf16[4,112,128]{2,1,0:T(8,128)(2,1)S(1)}, u32[]{:S(2)}, u32[]{:S(2)}) collective-permute-start(bf16[4,112,128]{2,1,0:T(8,128)(2,1)S(1)} %collective-permute-done.23.refs_2_), channel_id=1, source_target_pairs={{0,8},{8,0},{16,24},{24,16},{1,9},{9,1},{17,25},{25,17},{2,10},{10... | collective-permute-start | bytes 344072 | tf_op jit(solution)/shard_map/ppermute | solution.py:344
  68.2 1.5 %collective-permute-start.29 = (bf16[4,112,128]{2,1,0:T(8,128)(2,1)S(1)}, bf16[4,112,128]{2,1,0:T(8,128)(2,1)S(1)}, u32[]{:S(2)}, u32[]{:S(2)}) collective-permute-start(bf16[4,112,128]{2,1,0:T(8,128)(2,1)S(1)} %collective-permute-done.24.refs_3_), channel_id=1, source_target_pairs={{0,8},{8,0},{16,24},{24,16},{1,9},{9,1},{17,25},{25,17},{2,10},{10... | collective-permute-start | bytes 344072 | tf_op jit(solution)/shard_map/ppermute | solution.py:344
  68.2 1.4 %collective-permute-start.30 = (bf16[4,112,128]{2,1,0:T(8,128)(2,1)S(1)}, bf16[4,112,128]{2,1,0:T(8,128)(2,1)S(1)}, u32[]{:S(2)}, u32[]{:S(2)}) collective-permute-start(bf16[4,112,128]{2,1,0:T(8,128)(2,1)S(1)} %collective-permute-done.25.refs_4_), channel_id=1, source_target_pairs={{0,8},{8,0},{16,24},{24,16},{1,9},{9,1},{17,25},{25,17},{2,10},{10... | collective-permute-start | bytes 344072 | tf_op jit(solution)/shard_map/ppermute | solution.py:344

commit v2 on v1

--- a/solution.py
+++ b/solution.py
@@ -231,7 +231,7 @@
         self.rows_b = -(-3 * self.tall // (8 * slabs)) * 8
         self.rows_a = -(-27 * chan // (8 * samples * slabs)) * 8
         self.block = -(-(self.rows_b + self.rows_a) // 16) * 16
-        self.low = -(-self.block * 4 // 112) * 16
+        self.low = -(-self.block * 5 // 128) * 16
         self.far = slabs // 2
 
 

time: 72.5 us -> 71.8 us (level)
  transfers between devices with their start and end apart: 31 -> 31, of which waited for: 13 -> 14; matrix products, arithmetic and copies ran while one was open for 5% -> 5% of each run, Pallas kernels for 12% -> 12%
where the time goes in v2:
time: 71.8 us; the launch traced here: 71.7 us
  starting transfers between devices  30.2 us (42%)
  waiting for transfers between devices  24.6 us (34%)
  Pallas kernels  11.5 us (16%)
  local copies, waits for them, and re-layouts  3.27 us (5%)
  other arithmetic  1.12 us (2%)
  between operations  0.91 us (1%)
    ppermute x25, starting transfers between devices, swapped(): lax.ppermute(part, axis, [(i, i ^ distance) for i in range(lax.axis_size(...  19.3 us
    ppermute x25, waiting for transfers between devices, swapped(): lax.ppermute(part, axis, [(i, i ^ distance) for i in range(lax.axis_size(...  15.5 us
    pallas_call x16, Pallas kernels, call(): pl.pallas_call(kernel, out_shape=out_shape, in_specs=[vmem] * len(args),...  11.5 us
    ppermute x2, starting transfers between devices, per_device(): grad_sides = [lax.ppermute(grad, 'space', pairs) for pairs in (even, odd)]  6.07 us
    ppermute x1, waiting for transfers between devices, per_device(): from_even = lax.ppermute(even_edge, 'space', even)  4.33 us
    ppermute x1, waiting for transfers between devices, per_device(): from_odd = lax.ppermute(edges[1], 'space', odd)  2.75 us
    optimization_barrier x2, local copies, waits for them, and re-layouts, per_device(): lax.optimization_barrier((grad, layer_input, hidden_pre))  2.28 us
    ppermute x2, starting transfers between devices, per_device(): lax.ppermute(part, 'space', pairs)  2.17 us
  transfers between devices with their start and end apart: 31, of which 14 were waited for; matrix products, arithmetic and copies ran while one was open for 5% of the time, Pallas kernels for 12%

profile of v2, /device:TPU:0, one launch (start us, length us, event | category | flops | bytes accessed | tf_op | source)
XLA Modules:
  0.0 71.7 jit_solution(10846549031850158521)
XLA Ops:
  0.6 1.0 %fusion.1.refs_1_ = bf16[256,256]{1,0:T(8,128)(2,1)S(1)} fusion(bf16[1,256,1,256]{3,1,2,0:T(8,128)(2,1)} %param.8, bf16[1,256,1,256]{3,1,2,0:T(8,128)(2,1)} %param.9), kind=kLoop, calls=%fused_computation.6 | loop fusion | flops 393216 | bytes 393216 | tf_op jit(solution)/shard_map/mul | solution.py:357
  1.7 6.1 %collective-permute-start.1 = (bf16[256,256]{1,0:T(8,128)(2,1)S(1)}, bf16[256,256]{1,0:T(8,128)(2,1)S(1)}, u32[]{:S(2)}, u32[]{:S(2)}) collective-permute-start(bf16[256,256]{1,0:T(8,128)(2,1)S(1)} %fusion.1.refs_1_), channel_id=1, source_target_pairs={{0,7},{1,2},{2,1},{3,4},{4,3},{5,6},{6,5},{7,0},{8,15},{9,10},{10,... | collective-permute-start | bytes 393224 | tf_op jit(solution)/shard_map/ppermute | solution.py:359
  7.7 1.0 %copy.15 = bf16[1,64,2,1024]{3,1,2,0:T(8,128)(2,1)S(1)} copy(bf16[1,64,2,1024]{3,2,1,0:T(2,128)(2,1)} %param.6) | data formatting | bytes 524288 | tf_op jit(solution)/shard_map/optimization_barrier | solution.py:358
  8.7 1.3 %copy.14 = bf16[1,128,2,1024]{3,1,2,0:T(8,128)(2,1)S(1)} copy(bf16[1,128,2,1024]{3,2,1,0:T(2,128)(2,1)} %param.7) | data formatting | bytes 1048576 | tf_op jit(solution)/shard_map/optimization_barrier | solution.py:358
  10.0 0.5 shard_map.85
  10.6 2.1 %collective-permute-start.5 = (bf16[64,1024]{1,0:T(8,128)(2,1)S(1)}, bf16[64,1024]{1,0:T(8,128)(2,1)S(1)}, u32[]{:S(2)}, u32[]{:S(2)}) collective-permute-start(bf16[64,1024]{1,0:T(8,128)(2,1)S(1)} %get-tuple-element.86), channel_id=1, source_target_pairs={{0,1},{1,0},{2,3},{3,2},{4,5},{5,4},{6,7},{7,6},{8,9},{9,8},{10,11... | collective-permute-start | bytes 393224 | tf_op jit(solution)/shard_map/ppermute | solution.py:375
  12.7 0.1 collective-permute-start.6
  12.8 0.7 shard_map.86.refs_1_
  13.5 0.6 collective-permute-done.refs_2_
  14.2 1.6 %collective-permute-start.3 = (bf16[320,256]{1,0:T(8,128)(2,1)S(1)}, bf16[320,256]{1,0:T(8,128)(2,1)S(1)}, u32[]{:S(2)}, u32[]{:S(2)}) collective-permute-start(bf16[320,256]{1,0:T(8,128)(2,1)S(1)} %get-tuple-element.78), channel_id=1, source_target_pairs={{0,16},{8,24},{16,0},{24,8},{1,17},{9,25},{17,1},{25,9},{2,18},{10... | collective-permute-start | bytes 491528 | tf_op jit(solution)/shard_map/ppermute | solution.py:344
  15.8 1.6 %shard_map.88.refs_1_.refs_0_ = bf16[256,1024]{1,0:T(8,128)(2,1)S(1)} custom-call(bf16[3456,256]{1,0:T(8,128)(2,1)S(1)} %bitcast.32, bf16[256,256]{1,0:T(8,128)(2,1)S(1)} %fusion.1.refs_1_, bf16[256,256]{1,0:T(8,128)(2,1)S(1)} %get-tuple-element.80.refs_2_, bf16[256,256]{1,0:T(8,128)(2,1)S(1)} %get-tuple-element.81.refs_3_, ...), custom_call_target="tpu_custom_call" | custom-call | flops 262144 | bytes 1024 | tf_op jit(solution)/shard_map/pallas_call | solution.py:64
  17.4 1.6 %shard_map.89 = (bf16[64,1024]{1,0:T(8,128)(2,1)S(1)}, bf16[64,1024]{1,0:T(8,128)(2,1)S(1)}) custom-call(bf16[1728,128]{1,0:T(8,128)(2,1)S(1)} %bitcast.33, bf16[256,1024]{1,0:T(8,128)(2,1)S(1)} %shard_map.88.refs_1_.refs_0_), custom_call_target="tpu_custom_call" | custom-call | flops 65536 | bytes 1024 | tf_op jit(solution)/shard_map/pallas_call | solution.py:64
  19.0 1.4 %collective-permute-done.6.refs_3_ = bf16[64,1024]{1,0:T(8,128)(2,1)S(1)} collective-permute-done((bf16[64,1024]{1,0:T(8,128)(2,1)S(1)}, bf16[64,1024]{1,0:T(8,128)(2,1)S(1)}, u32[]{:S(2)}, u32[]{:S(2)}) %collective-permute-start.6) | collective-permute-done | bytes 131104 | tf_op jit(solution)/shard_map/ppermute | solution.py:375
  20.4 1.5 %shard_map.90 = (f32[448,128]{1,0:T(8,128)S(1)}, f32[448,128]{1,0:T(8,128)S(1)}, bf16[448,128]{1,0:T(8,128)(2,1)S(1)}, bf16[448,128]{1,0:T(8,128)(2,1)S(1)}) custom-call(bf16[256,1024]{1,0:T(8,128)(2,1)S(1)} %shard_map.88.refs_1_.refs_0_, bf16[2,576,1024]{2,1,0:T(8,128)(2,1)S(1)} %shard_map.86.refs_1_, bf16[64,1024]{1,0:T(8,128)(2,1)S(1)} %collective-permute-done.5.refs_2_, ...), custom_call_target="tpu_custom_call" | custom-call | flops 262144 | bytes 1024 | tf_op jit(solution)/shard_map/pallas_call | solution.py:64
  22.0 0.5 collective-permute-start.8
  22.5 1.5 %collective-permute-start.4 = (bf16[192,256]{1,0:T(8,128)(2,1)S(1)}, bf16[192,256]{1,0:T(8,128)(2,1)S(1)}, u32[]{:S(2)}, u32[]{:S(2)}) collective-permute-start(bf16[192,256]{1,0:T(8,128)(2,1)S(1)} %get-tuple-element.79), channel_id=1, source_target_pairs={{0,16},{8,24},{16,0},{24,8},{1,17},{9,25},{17,1},{25,9},{2,18},{10... | collective-permute-start | bytes 294920 | tf_op jit(solution)/shard_map/ppermute | solution.py:344
  24.0 1.9 %collective-permute-start.11 = (bf16[64,1024]{1,0:T(8,128)(2,1)S(1)}, bf16[64,1024]{1,0:T(8,128)(2,1)S(1)}, u32[]{:S(2)}, u32[]{:S(2)}) collective-permute-start(bf16[64,1024]{1,0:T(8,128)(2,1)S(1)} %get-tuple-element.97), channel_id=1, source_target_pairs={{0,7},{1,2},{2,1},{3,4},{4,3},{5,6},{6,5},{7,0},{8,15},{9,10},{10,... | collective-permute-start | bytes 393224 | tf_op jit(solution)/shard_map/ppermute | solution.py:457
  26.0 1.3 %collective-permute-start.12 = (bf16[448,128]{1,0:T(8,128)(2,1)S(1)}, bf16[448,128]{1,0:T(8,128)(2,1)S(1)}, u32[]{:S(2)}, u32[]{:S(2)}) collective-permute-start(bf16[448,128]{1,0:T(8,128)(2,1)S(1)} %get-tuple-element.100), channel_id=1, source_target_pairs={{0,16},{8,24},{16,0},{24,8},{1,17},{9,25},{17,1},{25,9},{2,18},{10... | collective-permute-start | bytes 344072 | tf_op jit(solution)/shard_map/ppermute | solution.py:344
  27.3 0.5 collective-permute-start.9
  27.8 0.9 %collective-permute-done.9.refs_3_ = bf16[128,256]{1,0:T(8,128)(2,1)S(1)} collective-permute-done((bf16[128,256]{1,0:T(8,128)(2,1)S(1)}, bf16[128,256]{1,0:T(8,128)(2,1)S(1)}, u32[]{:S(2)}, u32[]{:S(2)}) %collective-permute-start.9) | collective-permute-done | bytes 65568 | tf_op jit(solution)/shard_map/ppermute | solution.py:344
  28.7 1.1 %shard_map.92.refs_0_ = f32[8,216,128]{2,1,0:T(8,128)S(1)} custom-call(bf16[320,256]{1,0:T(8,128)(2,1)S(1)} %get-tuple-element.76.refs_0_.refs_4_, bf16[320,256]{1,0:T(8,128)(2,1)S(1)} %collective-permute-done.2.refs_1_.refs_5_, bf16[320,256]{1,0:T(8,128)(2,1)S(1)} %collective-permute-done.3.refs_2_.refs_6_, ...), custom_call_target="tpu_custom_call" | custom-call | flops 262144 | bytes 1024 | tf_op jit(solution)/shard_map/pallas_call | solution.py:64
  29.8 2.8 %collective-permute-done.11 = bf16[64,1024]{1,0:T(8,128)(2,1)S(1)} collective-permute-done((bf16[64,1024]{1,0:T(8,128)(2,1)S(1)}, bf16[64,1024]{1,0:T(8,128)(2,1)S(1)}, u32[]{:S(2)}, u32[]{:S(2)}) %collective-permute-start.11) | collective-permute-done | bytes 131104 | tf_op jit(solution)/shard_map/ppermute | solution.py:457
  32.6 0.1 shard_map.93
  32.8 3.4 %collective-permute-start.15 = (bf16[2,272,128]{2,1,0:T(8,128)(2,1)S(1)}, bf16[2,272,128]{2,1,0:T(8,128)(2,1)S(1)}, u32[]{:S(2)}, u32[]{:S(2)}) collective-permute-start(bf16[2,272,128]{2,1,0:T(8,128)(2,1)S(1)} %get-tuple-element.104), channel_id=1, source_target_pairs={{0,3},{1,2},{2,1},{3,0},{4,7},{5,6},{6,5},{7,4},{8,11},{9,10},{10,... | collective-permute-start | bytes 417800 | tf_op jit(solution)/shard_map/ppermute | solution.py:344
  36.2 1.5 %shard_map.94 = f32[2,64,1024]{2,1,0:T(8,128)S(1)} custom-call(bf16[1728,128]{1,0:T(8,128)(2,1)S(1)} %bitcast.34, bf16[256,1024]{1,0:T(8,128)(2,1)S(1)} %shard_map.88.refs_1_.refs_0_), custom_call_target="tpu_custom_call" | custom-call | flops 65536 | bytes 1024 | tf_op jit(solution)/shard_map/pallas_call | solution.py:64
  37.7 0.7 collective-permute-done.13.refs_1_
  38.4 1.0 %collective-permute-done.14.refs_2_ = bf16[2,272,128]{2,1,0:T(8,128)(2,1)S(1)} collective-permute-done((bf16[2,272,128]{2,1,0:T(8,128)(2,1)S(1)}, bf16[2,272,128]{2,1,0:T(8,128)(2,1)S(1)}, u32[]{:S(2)}, u32[]{:S(2)}) %collective-permute-start.14) | collective-permute-done | bytes 139296 | tf_op jit(solution)/shard_map/ppermute | solution.py:344
  39.4 2.8 %collective-permute-done.15.refs_3_ = bf16[2,272,128]{2,1,0:T(8,128)(2,1)S(1)} collective-permute-done((bf16[2,272,128]{2,1,0:T(8,128)(2,1)S(1)}, bf16[2,272,128]{2,1,0:T(8,128)(2,1)S(1)}, u32[]{:S(2)}, u32[]{:S(2)}) %collective-permute-start.15) | collective-permute-done | bytes 139296 | tf_op jit(solution)/shard_map/ppermute | solution.py:344
  42.3 0.7 collective-permute-start.17
  43.0 4.3 %collective-permute-done.17 = bf16[64,1024]{1,0:T(8,128)(2,1)S(1)} collective-permute-done((bf16[64,1024]{1,0:T(8,128)(2,1)S(1)}, bf16[64,1024]{1,0:T(8,128)(2,1)S(1)}, u32[]{:S(2)}, u32[]{:S(2)}) %collective-permute-start.17) | collective-permute-done | bytes 131104 | tf_op jit(solution)/shard_map/ppermute | solution.py:482
  47.4 2.6 %collective-permute-done.16.refs_1_ = bf16[2,272,128]{2,1,0:T(8,128)(2,1)S(1)} collective-permute-done((bf16[2,272,128]{2,1,0:T(8,128)(2,1)S(1)}, bf16[2,272,128]{2,1,0:T(8,128)(2,1)S(1)}, u32[]{:S(2)}, u32[]{:S(2)}) %collective-permute-start.16) | collective-permute-done | bytes 139296 | tf_op jit(solution)/shard_map/ppermute | solution.py:344
  50.1 1.0 %collective-permute-start.21 = (bf16[2,176,128]{2,1,0:T(8,128)(2,1)S(1)}, bf16[2,176,128]{2,1,0:T(8,128)(2,1)S(1)}, u32[]{:S(2)}, u32[]{:S(2)}) collective-permute-start(bf16[2,176,128]{2,1,0:T(8,128)(2,1)S(1)} %get-tuple-element.114), channel_id=1, source_target_pairs={{0,3},{1,2},{2,1},{3,0},{4,7},{5,6},{6,5},{7,4},{8,11},{9,10},{10,... | collective-permute-start | bytes 270344 | tf_op jit(solution)/shard_map/ppermute | solution.py:344
  51.1 1.0 %collective-permute-start.20 = (bf16[2,176,128]{2,1,0:T(8,128)(2,1)S(1)}, bf16[2,176,128]{2,1,0:T(8,128)(2,1)S(1)}, u32[]{:S(2)}, u32[]{:S(2)}) collective-permute-start(bf16[2,176,128]{2,1,0:T(8,128)(2,1)S(1)} %get-tuple-element.114), channel_id=1, source_target_pairs={{0,2},{1,3},{2,0},{3,1},{4,6},{5,7},{6,4},{7,5},{8,10},{9,11},{10,... | collective-permute-start | bytes 270344 | tf_op jit(solution)/shard_map/ppermute | solution.py:344
  52.2 1.5 %collective-permute-start.19 = (bf16[2,176,128]{2,1,0:T(8,128)(2,1)S(1)}, bf16[2,176,128]{2,1,0:T(8,128)(2,1)S(1)}, u32[]{:S(2)}, u32[]{:S(2)}) collective-permute-start(bf16[2,176,128]{2,1,0:T(8,128)(2,1)S(1)} %get-tuple-element.114), channel_id=1, source_target_pairs={{0,1},{1,0},{2,3},{3,2},{4,5},{5,4},{6,7},{7,6},{8,9},{9,8},{10,11... | collective-permute-start | bytes 270344 | tf_op jit(solution)/shard_map/ppermute | solution.py:344
  53.7 1.9 %collective-permute-done.21.refs_2_.refs_4_ = bf16[2,176,128]{2,1,0:T(8,128)(2,1)S(1)} collective-permute-done((bf16[2,176,128]{2,1,0:T(8,128)(2,1)S(1)}, bf16[2,176,128]{2,1,0:T(8,128)(2,1)S(1)}, u32[]{:S(2)}, u32[]{:S(2)}) %collective-permute-start.21) | collective-permute-done | bytes 90144 | tf_op jit(solution)/shard_map/ppermute | solution.py:344
  55.6 0.1 collective-permute-done.20.refs_1_.refs_3_
  55.8 1.0 %collective-permute-done.19.refs_0_.refs_2_ = bf16[2,176,128]{2,1,0:T(8,128)(2,1)S(1)} collective-permute-done((bf16[2,176,128]{2,1,0:T(8,128)(2,1)S(1)}, bf16[2,176,128]{2,1,0:T(8,128)(2,1)S(1)}, u32[]{:S(2)}, u32[]{:S(2)}) %collective-permute-start.19) | collective-permute-done | bytes 90144 | tf_op jit(solution)/shard_map/ppermute | solution.py:344
  56.9 2.0 %collective-permute-start.22 = (bf16[6,176,128]{2,1,0:T(8,128)(2,1)S(1)}, bf16[6,176,128]{2,1,0:T(8,128)(2,1)S(1)}, u32[]{:S(2)}, u32[]{:S(2)}) collective-permute-start(bf16[6,176,128]{2,1,0:T(8,128)(2,1)S(1)} %shard_map.97), channel_id=1, source_target_pairs={{0,16},{8,24},{16,0},{24,8},{1,17},{9,25},{17,1},{25,9},{2,18},{10... | collective-permute-start | bytes 811016 | tf_op jit(solution)/shard_map/ppermute | solution.py:344
  58.9 1.0 %collective-permute-start.25 = (bf16[4,96,128]{2,1,0:T(8,128)(2,1)S(1)}, bf16[4,96,128]{2,1,0:T(8,128)(2,1)S(1)}, u32[]{:S(2)}, u32[]{:S(2)}) collective-permute-start(bf16[4,96,128]{2,1,0:T(8,128)(2,1)S(1)} %shard_map.98), channel_id=1, source_target_pairs={{0,3},{1,2},{2,1},{3,0},{4,7},{5,6},{6,5},{7,4},{8,11},{9,10},{10,... | collective-permute-start | bytes 294920 | tf_op jit(solution)/shard_map/ppermute | solution.py:344
  60.0 2.0 %collective-permute-start.24 = (bf16[4,96,128]{2,1,0:T(8,128)(2,1)S(1)}, bf16[4,96,128]{2,1,0:T(8,128)(2,1)S(1)}, u32[]{:S(2)}, u32[]{:S(2)}) collective-permute-start(bf16[4,96,128]{2,1,0:T(8,128)(2,1)S(1)} %shard_map.98), channel_id=1, source_target_pairs={{0,2},{1,3},{2,0},{3,1},{4,6},{5,7},{6,4},{7,5},{8,10},{9,11},{10,... | collective-permute-start | bytes 294920 | tf_op jit(solution)/shard_map/ppermute | solution.py:344
  62.0 0.5 collective-permute-start.23
  62.5 3.0 %collective-permute-done.25.refs_4_ = bf16[4,96,128]{2,1,0:T(8,128)(2,1)S(1)} collective-permute-done((bf16[4,96,128]{2,1,0:T(8,128)(2,1)S(1)}, bf16[4,96,128]{2,1,0:T(8,128)(2,1)S(1)}, u32[]{:S(2)}, u32[]{:S(2)}) %collective-permute-start.25) | collective-permute-done | bytes 98336 | tf_op jit(solution)/shard_map/ppermute | solution.py:344
  65.5 1.4 %collective-permute-done.24.refs_3_ = bf16[4,96,128]{2,1,0:T(8,128)(2,1)S(1)} collective-permute-done((bf16[4,96,128]{2,1,0:T(8,128)(2,1)S(1)}, bf16[4,96,128]{2,1,0:T(8,128)(2,1)S(1)}, u32[]{:S(2)}, u32[]{:S(2)}) %collective-permute-start.24) | collective-permute-done | bytes 98336 | tf_op jit(solution)/shard_map/ppermute | solution.py:344
  67.1 0.5 collective-permute-start.28
  67.5 0.1 collective-permute-start.29
  67.6 0.4 collective-permute-start.30
  68.1 1.0 %copy.11 = bf16[1,64,2,1024]{3,2,1,0:T(2,128)(2,1)} copy(bf16[1,64,2,1024]{3,1,2,0:T(8,128)(2,1)S(1)} %fusion) | data formatting | bytes 524288
  69.1 2.6 %shard_map.100 = (f32[1728,128]{1,0:T(8,128)}, f32[3456,256]{1,0:T(8,128)}) custom-call(bf16[2144,128]{1,0:T(8,128)(2,1)S(1)} %shard_map.99.refs_0_, bf16[6,176,128]{2,1,0:T(8,128)(2,1)S(1)} %collective-permute-done.22.refs_1_, bf16[4,96,128]{2,1,0:T(8,128)(2,1)S(1)} %collective-permute-done.23.refs_2_, ...), custom_call_target="tpu_custom_call" | custom-call | flops 256 | bytes 1024 | tf_op jit(solution)/shard_map/pallas_call | solution.py:64
  (42 shorter events, 1.0 us)
Async XLA Ops:
  1.7 11.8 %collective-permute-start.1 = (bf16[256,256]{1,0:T(8,128)(2,1)S(1)}, bf16[256,256]{1,0:T(8,128)(2,1)S(1)}, u32[]{:S(2)}, u32[]{:S(2)}) collective-permute-start(bf16[256,256]{1,0:T(8,128)(2,1)S(1)} %fusion.1.refs_1_), channel_id=1, source_target_pairs={{0,7},{1,2},{2,1},{3,4},{4,3},{5,6},{6,5},{7,0},{8,15},{9,10},{10,... | collective-permute-start | bytes 393224 | tf_op jit(solution)/shard_map/ppermute | solution.py:359
  7.7 6.4 %collective-permute-start = (bf16[256,256]{1,0:T(8,128)(2,1)S(1)}, bf16[256,256]{1,0:T(8,128)(2,1)S(1)}, u32[]{:S(2)}, u32[]{:S(2)}) collective-permute-start(bf16[256,256]{1,0:T(8,128)(2,1)S(1)} %fusion.1.refs_1_), channel_id=1, source_target_pairs={{0,1},{1,0},{2,3},{3,2},{4,5},{5,4},{6,7},{7,6},{8,9},{9,8},{10,11... | collective-permute-start | bytes 393224 | tf_op jit(solution)/shard_map/ppermute | solution.py:359
  8.7 7.0 %copy-start = (bf16[27,128,256]{2,1,0:T(8,128)(2,1)S(1)}, bf16[27,128,256]{2,1,0:T(8,128)(2,1)}, u32[]{:S(2)}) copy-start(bf16[27,128,256]{2,1,0:T(8,128)(2,1)} %param.11) | copy-start | bytes 5308420
  10.6 8.3 %collective-permute-start.5 = (bf16[64,1024]{1,0:T(8,128)(2,1)S(1)}, bf16[64,1024]{1,0:T(8,128)(2,1)S(1)}, u32[]{:S(2)}, u32[]{:S(2)}) collective-permute-start(bf16[64,1024]{1,0:T(8,128)(2,1)S(1)} %get-tuple-element.86), channel_id=1, source_target_pairs={{0,1},{1,0},{2,3},{3,2},{4,5},{5,4},{6,7},{7,6},{8,9},{9,8},{10,11... | collective-permute-start | bytes 393224 | tf_op jit(solution)/shard_map/ppermute | solution.py:375
  12.7 7.7 %collective-permute-start.6 = (bf16[64,1024]{1,0:T(8,128)(2,1)S(1)}, bf16[64,1024]{1,0:T(8,128)(2,1)S(1)}, u32[]{:S(2)}, u32[]{:S(2)}) collective-permute-start(bf16[64,1024]{1,0:T(8,128)(2,1)S(1)} %get-tuple-element.87), channel_id=1, source_target_pairs={{0,7},{1,2},{2,1},{3,4},{4,3},{5,6},{6,5},{7,0},{8,15},{9,10},{10,... | collective-permute-start | bytes 393224 | tf_op jit(solution)/shard_map/ppermute | solution.py:375
  13.5 3.9 %copy-start.1 = (bf16[27,64,128]{2,1,0:T(8,128)(2,1)S(1)}, bf16[27,64,128]{2,1,0:T(8,128)(2,1)}, u32[]{:S(2)}) copy-start(bf16[27,64,128]{2,1,0:T(8,128)(2,1)} %param.10) | copy-start | bytes 1327108
  14.2 13.1 %collective-permute-start.3 = (bf16[320,256]{1,0:T(8,128)(2,1)S(1)}, bf16[320,256]{1,0:T(8,128)(2,1)S(1)}, u32[]{:S(2)}, u32[]{:S(2)}) collective-permute-start(bf16[320,256]{1,0:T(8,128)(2,1)S(1)} %get-tuple-element.78), channel_id=1, source_target_pairs={{0,16},{8,24},{16,0},{24,8},{1,17},{9,25},{17,1},{25,9},{2,18},{10... | collective-permute-start | bytes 491528 | tf_op jit(solution)/shard_map/ppermute | solution.py:344
  21.9 2.1 %collective-permute-start.7 = (bf16[448,128]{1,0:T(8,128)(2,1)S(1)}, bf16[448,128]{1,0:T(8,128)(2,1)S(1)}, u32[]{:S(2)}, u32[]{:S(2)}) collective-permute-start(bf16[448,128]{1,0:T(8,128)(2,1)S(1)} %get-tuple-element.92), channel_id=1, source_target_pairs={{0,8},{8,0},{16,24},{24,16},{1,9},{9,1},{17,25},{25,17},{2,10},{10... | collective-permute-start | bytes 344072 | tf_op jit(solution)/shard_map/ppermute | solution.py:344
  22.0 3.9 %collective-permute-start.8 = (bf16[448,128]{1,0:T(8,128)(2,1)S(1)}, bf16[448,128]{1,0:T(8,128)(2,1)S(1)}, u32[]{:S(2)}, u32[]{:S(2)}) collective-permute-start(bf16[448,128]{1,0:T(8,128)(2,1)S(1)} %get-tuple-element.93), channel_id=1, source_target_pairs={{0,8},{8,0},{16,24},{24,16},{1,9},{9,1},{17,25},{25,17},{2,10},{10... | collective-permute-start | bytes 344072 | tf_op jit(solution)/shard_map/ppermute | solution.py:344
  22.5 4.8 %collective-permute-start.4 = (bf16[192,256]{1,0:T(8,128)(2,1)S(1)}, bf16[192,256]{1,0:T(8,128)(2,1)S(1)}, u32[]{:S(2)}, u32[]{:S(2)}) collective-permute-start(bf16[192,256]{1,0:T(8,128)(2,1)S(1)} %get-tuple-element.79), channel_id=1, source_target_pairs={{0,16},{8,24},{16,0},{24,8},{1,17},{9,25},{17,1},{25,9},{2,18},{10... | collective-permute-start | bytes 294920 | tf_op jit(solution)/shard_map/ppermute | solution.py:344
  24.0 3.8 %collective-permute-start.2 = (bf16[320,256]{1,0:T(8,128)(2,1)S(1)}, bf16[320,256]{1,0:T(8,128)(2,1)S(1)}, u32[]{:S(2)}, u32[]{:S(2)}) collective-permute-start(bf16[320,256]{1,0:T(8,128)(2,1)S(1)} %get-tuple-element.77), channel_id=1, source_target_pairs={{0,8},{8,0},{16,24},{24,16},{1,9},{9,1},{17,25},{25,17},{2,10},{10... | collective-permute-start | bytes 491528 | tf_op jit(solution)/shard_map/ppermute | solution.py:344
  24.0 8.6 %collective-permute-start.11 = (bf16[64,1024]{1,0:T(8,128)(2,1)S(1)}, bf16[64,1024]{1,0:T(8,128)(2,1)S(1)}, u32[]{:S(2)}, u32[]{:S(2)}) collective-permute-start(bf16[64,1024]{1,0:T(8,128)(2,1)S(1)} %get-tuple-element.97), channel_id=1, source_target_pairs={{0,7},{1,2},{2,1},{3,4},{4,3},{5,6},{6,5},{7,0},{8,15},{9,10},{10,... | collective-permute-start | bytes 393224 | tf_op jit(solution)/shard_map/ppermute | solution.py:457
  26.0 6.6 %collective-permute-start.12 = (bf16[448,128]{1,0:T(8,128)(2,1)S(1)}, bf16[448,128]{1,0:T(8,128)(2,1)S(1)}, u32[]{:S(2)}, u32[]{:S(2)}) collective-permute-start(bf16[448,128]{1,0:T(8,128)(2,1)S(1)} %get-tuple-element.100), channel_id=1, source_target_pairs={{0,16},{8,24},{16,0},{24,8},{1,17},{9,25},{17,1},{25,9},{2,18},{10... | collective-permute-start | bytes 344072 | tf_op jit(solution)/shard_map/ppermute | solution.py:344
  27.2 1.4 %collective-permute-start.10 = (bf16[192,256]{1,0:T(8,128)(2,1)S(1)}, bf16[192,256]{1,0:T(8,128)(2,1)S(1)}, u32[]{:S(2)}, u32[]{:S(2)}) collective-permute-start(bf16[192,256]{1,0:T(8,128)(2,1)S(1)} %collective-permute-done.4), channel_id=1, source_target_pairs={{0,8},{8,0},{16,24},{24,16},{1,9},{9,1},{17,25},{25,17},{2,10},{10... | collective-permute-start | bytes 294920 | tf_op jit(solution)/shard_map/ppermute | solution.py:344
  27.3 1.4 %collective-permute-start.9 = (bf16[128,256]{1,0:T(8,128)(2,1)S(1)}, bf16[128,256]{1,0:T(8,128)(2,1)S(1)}, u32[]{:S(2)}, u32[]{:S(2)}) collective-permute-start(bf16[128,256]{1,0:T(8,128)(2,1)S(1)} %slice.11), channel_id=1, source_target_pairs={{0,8},{8,0},{16,24},{24,16},{1,9},{9,1},{17,25},{25,17},{2,10},{10... | collective-permute-start | bytes 196616 | tf_op jit(solution)/shard_map/ppermute | solution.py:344
  32.7 5.8 %collective-permute-start.13 = (bf16[2,272,128]{2,1,0:T(8,128)(2,1)S(1)}, bf16[2,272,128]{2,1,0:T(8,128)(2,1)S(1)}, u32[]{:S(2)}, u32[]{:S(2)}) collective-permute-start(bf16[2,272,128]{2,1,0:T(8,128)(2,1)S(1)} %get-tuple-element.102), channel_id=1, source_target_pairs={{0,1},{1,0},{2,3},{3,2},{4,5},{5,4},{6,7},{7,6},{8,9},{9,8},{10,11... | collective-permute-start | bytes 417800 | tf_op jit(solution)/shard_map/ppermute | solution.py:344
  32.7 6.6 %collective-permute-start.14 = (bf16[2,272,128]{2,1,0:T(8,128)(2,1)S(1)}, bf16[2,272,128]{2,1,0:T(8,128)(2,1)S(1)}, u32[]{:S(2)}, u32[]{:S(2)}) collective-permute-start(bf16[2,272,128]{2,1,0:T(8,128)(2,1)S(1)} %get-tuple-element.103), channel_id=1, source_target_pairs={{0,2},{1,3},{2,0},{3,1},{4,6},{5,7},{6,4},{7,5},{8,10},{9,11},{10,... | collective-permute-start | bytes 417800 | tf_op jit(solution)/shard_map/ppermute | solution.py:344
  32.8 9.4 %collective-permute-start.15 = (bf16[2,272,128]{2,1,0:T(8,128)(2,1)S(1)}, bf16[2,272,128]{2,1,0:T(8,128)(2,1)S(1)}, u32[]{:S(2)}, u32[]{:S(2)}) collective-permute-start(bf16[2,272,128]{2,1,0:T(8,128)(2,1)S(1)} %get-tuple-element.104), channel_id=1, source_target_pairs={{0,3},{1,2},{2,1},{3,0},{4,7},{5,6},{6,5},{7,4},{8,11},{9,10},{10,... | collective-permute-start | bytes 417800 | tf_op jit(solution)/shard_map/ppermute | solution.py:344
  42.3 7.8 %collective-permute-start.16 = (bf16[2,272,128]{2,1,0:T(8,128)(2,1)S(1)}, bf16[2,272,128]{2,1,0:T(8,128)(2,1)S(1)}, u32[]{:S(2)}, u32[]{:S(2)}) collective-permute-start(bf16[2,272,128]{2,1,0:T(8,128)(2,1)S(1)} %shard_map.95.refs_0_), channel_id=1, source_target_pairs={{0,4},{1,5},{2,6},{3,7},{4,0},{5,1},{6,2},{7,3},{8,12},{9,13},{10,... | collective-permute-start | bytes 417800 | tf_op jit(solution)/shard_map/ppermute | solution.py:344
  42.3 5.0 %collective-permute-start.17 = (bf16[64,1024]{1,0:T(8,128)(2,1)S(1)}, bf16[64,1024]{1,0:T(8,128)(2,1)S(1)}, u32[]{:S(2)}, u32[]{:S(2)}) collective-permute-start(bf16[64,1024]{1,0:T(8,128)(2,1)S(1)} %get-tuple-element.111), channel_id=1, source_target_pairs={{0,1},{1,0},{2,3},{3,2},{4,5},{5,4},{6,7},{7,6},{8,9},{9,8},{10,11... | collective-permute-start | bytes 393224 | tf_op jit(solution)/shard_map/ppermute | solution.py:482
  50.1 6.7 %collective-permute-start.18 = (bf16[2,272,128]{2,1,0:T(8,128)(2,1)S(1)}, bf16[2,272,128]{2,1,0:T(8,128)(2,1)S(1)}, u32[]{:S(2)}, u32[]{:S(2)}) collective-permute-start(bf16[2,272,128]{2,1,0:T(8,128)(2,1)S(1)} %get-tuple-element.118.refs_0_), channel_id=1, source_target_pairs={{0,16},{8,24},{16,0},{24,8},{1,17},{9,25},{17,1},{25,9},{2,18},{10... | collective-permute-start | bytes 417800 | tf_op jit(solution)/shard_map/ppermute | solution.py:344
  50.1 5.5 %collective-permute-start.21 = (bf16[2,176,128]{2,1,0:T(8,128)(2,1)S(1)}, bf16[2,176,128]{2,1,0:T(8,128)(2,1)S(1)}, u32[]{:S(2)}, u32[]{:S(2)}) collective-permute-start(bf16[2,176,128]{2,1,0:T(8,128)(2,1)S(1)} %get-tuple-element.114), channel_id=1, source_target_pairs={{0,3},{1,2},{2,1},{3,0},{4,7},{5,6},{6,5},{7,4},{8,11},{9,10},{10,... | collective-permute-start | bytes 270344 | tf_op jit(solution)/shard_map/ppermute | solution.py:344
  51.1 4.6 %collective-permute-start.20 = (bf16[2,176,128]{2,1,0:T(8,128)(2,1)S(1)}, bf16[2,176,128]{2,1,0:T(8,128)(2,1)S(1)}, u32[]{:S(2)}, u32[]{:S(2)}) collective-permute-start(bf16[2,176,128]{2,1,0:T(8,128)(2,1)S(1)} %get-tuple-element.114), channel_id=1, source_target_pairs={{0,2},{1,3},{2,0},{3,1},{4,6},{5,7},{6,4},{7,5},{8,10},{9,11},{10,... | collective-permute-start | bytes 270344 | tf_op jit(solution)/shard_map/ppermute | solution.py:344
  52.2 4.5 %collective-permute-start.19 = (bf16[2,176,128]{2,1,0:T(8,128)(2,1)S(1)}, bf16[2,176,128]{2,1,0:T(8,128)(2,1)S(1)}, u32[]{:S(2)}, u32[]{:S(2)}) collective-permute-start(bf16[2,176,128]{2,1,0:T(8,128)(2,1)S(1)} %get-tuple-element.114), channel_id=1, source_target_pairs={{0,1},{1,0},{2,3},{3,2},{4,5},{5,4},{6,7},{7,6},{8,9},{9,8},{10,11... | collective-permute-start | bytes 270344 | tf_op jit(solution)/shard_map/ppermute | solution.py:344
  56.8 10.2 %collective-permute-start.26 = (bf16[2144,128]{1,0:T(8,128)(2,1)S(1)}, bf16[2144,128]{1,0:T(8,128)(2,1)S(1)}, u32[]{:S(2)}, u32[]{:S(2)}) collective-permute-start(bf16[2144,128]{1,0:T(8,128)(2,1)S(1)} %shard_map.99.refs_0_), channel_id=1, source_target_pairs={{0,8},{8,0},{16,24},{24,16},{1,9},{9,1},{17,25},{25,17},{2,10},{10... | collective-permute-start | bytes 1646600 | tf_op jit(solution)/shard_map/ppermute | solution.py:344
  56.9 10.1 %collective-permute-start.22 = (bf16[6,176,128]{2,1,0:T(8,128)(2,1)S(1)}, bf16[6,176,128]{2,1,0:T(8,128)(2,1)S(1)}, u32[]{:S(2)}, u32[]{:S(2)}) collective-permute-start(bf16[6,176,128]{2,1,0:T(8,128)(2,1)S(1)} %shard_map.97), channel_id=1, source_target_pairs={{0,16},{8,24},{16,0},{24,8},{1,17},{9,25},{17,1},{25,9},{2,18},{10... | collective-permute-start | bytes 811016 | tf_op jit(solution)/shard_map/ppermute | solution.py:344
  58.9 6.6 %collective-permute-start.25 = (bf16[4,96,128]{2,1,0:T(8,128)(2,1)S(1)}, bf16[4,96,128]{2,1,0:T(8,128)(2,1)S(1)}, u32[]{:S(2)}, u32[]{:S(2)}) collective-permute-start(bf16[4,96,128]{2,1,0:T(8,128)(2,1)S(1)} %shard_map.98), channel_id=1, source_target_pairs={{0,3},{1,2},{2,1},{3,0},{4,7},{5,6},{6,5},{7,4},{8,11},{9,10},{10,... | collective-permute-start | bytes 294920 | tf_op jit(solution)/shard_map/ppermute | solution.py:344
  60.0 7.0 %collective-permute-start.24 = (bf16[4,96,128]{2,1,0:T(8,128)(2,1)S(1)}, bf16[4,96,128]{2,1,0:T(8,128)(2,1)S(1)}, u32[]{:S(2)}, u32[]{:S(2)}) collective-permute-start(bf16[4,96,128]{2,1,0:T(8,128)(2,1)S(1)} %shard_map.98), channel_id=1, source_target_pairs={{0,2},{1,3},{2,0},{3,1},{4,6},{5,7},{6,4},{7,5},{8,10},{9,11},{10,... | collective-permute-start | bytes 294920 | tf_op jit(solution)/shard_map/ppermute | solution.py:344
  62.0 5.0 %collective-permute-start.23 = (bf16[4,96,128]{2,1,0:T(8,128)(2,1)S(1)}, bf16[4,96,128]{2,1,0:T(8,128)(2,1)S(1)}, u32[]{:S(2)}, u32[]{:S(2)}) collective-permute-start(bf16[4,96,128]{2,1,0:T(8,128)(2,1)S(1)} %shard_map.98), channel_id=1, source_target_pairs={{0,1},{1,0},{2,3},{3,2},{4,5},{5,4},{6,7},{7,6},{8,9},{9,8},{10,11... | collective-permute-start | bytes 294920 | tf_op jit(solution)/shard_map/ppermute | solution.py:344
  67.0 2.1 %collective-permute-start.27 = (bf16[6,176,128]{2,1,0:T(8,128)(2,1)S(1)}, bf16[6,176,128]{2,1,0:T(8,128)(2,1)S(1)}, u32[]{:S(2)}, u32[]{:S(2)}) collective-permute-start(bf16[6,176,128]{2,1,0:T(8,128)(2,1)S(1)} %collective-permute-done.22.refs_1_), channel_id=1, source_target_pairs={{0,8},{8,0},{16,24},{24,16},{1,9},{9,1},{17,25},{25,17},{2,10},{10... | collective-permute-start | bytes 811016 | tf_op jit(solution)/shard_map/ppermute | solution.py:344
  67.1 2.0 %collective-permute-start.28 = (bf16[4,96,128]{2,1,0:T(8,128)(2,1)S(1)}, bf16[4,96,128]{2,1,0:T(8,128)(2,1)S(1)}, u32[]{:S(2)}, u32[]{:S(2)}) collective-permute-start(bf16[4,96,128]{2,1,0:T(8,128)(2,1)S(1)} %collective-permute-done.23.refs_2_), channel_id=1, source_target_pairs={{0,8},{8,0},{16,24},{24,16},{1,9},{9,1},{17,25},{25,17},{2,10},{10... | collective-permute-start | bytes 294920 | tf_op jit(solution)/shard_map/ppermute | solution.py:344
  67.5 1.5 %collective-permute-start.29 = (bf16[4,96,128]{2,1,0:T(8,128)(2,1)S(1)}, bf16[4,96,128]{2,1,0:T(8,128)(2,1)S(1)}, u32[]{:S(2)}, u32[]{:S(2)}) collective-permute-start(bf16[4,96,128]{2,1,0:T(8,128)(2,1)S(1)} %collective-permute-done.24.refs_3_), channel_id=1, source_target_pairs={{0,8},{8,0},{16,24},{24,16},{1,9},{9,1},{17,25},{25,17},{2,10},{10... | collective-permute-start | bytes 294920 | tf_op jit(solution)/shard_map/ppermute | solution.py:344
  67.6 1.4 %collective-permute-start.30 = (bf16[4,96,128]{2,1,0:T(8,128)(2,1)S(1)}, bf16[4,96,128]{2,1,0:T(8,128)(2,1)S(1)}, u32[]{:S(2)}, u32[]{:S(2)}) collective-permute-start(bf16[4,96,128]{2,1,0:T(8,128)(2,1)S(1)} %collective-permute-done.25.refs_4_), channel_id=1, source_target_pairs={{0,8},{8,0},{16,24},{24,16},{1,9},{9,1},{17,25},{25,17},{2,10},{10... | collective-permute-start | bytes 294920 | tf_op jit(solution)/shard_map/ppermute | solution.py:344

commit v3 on v2

--- a/solution.py
+++ b/solution.py
@@ -231,7 +231,7 @@
         self.rows_b = -(-3 * self.tall // (8 * slabs)) * 8
         self.rows_a = -(-27 * chan // (8 * samples * slabs)) * 8
         self.block = -(-(self.rows_b + self.rows_a) // 16) * 16
-        self.low = -(-self.block * 5 // 128) * 16
+        self.low = -(-self.block * 11 // 256) * 16
         self.far = slabs // 2
 
 

time: 71.8 us -> 71.4 us (level)
  transfers between devices with their start and end apart: 31 -> 31, of which waited for: 14 -> 16; matrix products, arithmetic and copies ran while one was open for 5% -> 5% of each run, Pallas kernels for 12% -> 12%
where the time goes in v3:
time: 71.4 us; the launch traced here: 71.3 us
  starting transfers between devices  30.1 us (42%)
  waiting for transfers between devices  24.4 us (34%)
  Pallas kernels  11.5 us (16%)
  local copies, waits for them, and re-layouts  3.27 us (5%)
  other arithmetic  1.12 us (2%)
  between operations  0.9 us (1%)
    ppermute x25, starting transfers between devices, swapped(): lax.ppermute(part, axis, [(i, i ^ distance) for i in range(lax.axis_size(...  19.2 us
    ppermute x25, waiting for transfers between devices, swapped(): lax.ppermute(part, axis, [(i, i ^ distance) for i in range(lax.axis_size(...  15.2 us
    pallas_call x16, Pallas kernels, call(): pl.pallas_call(kernel, out_shape=out_shape, in_specs=[vmem] * len(args),...  11.5 us
    ppermute x2, starting transfers between devices, per_device(): grad_sides = [lax.ppermute(grad, 'space', pairs) for pairs in (even, odd)]  6.07 us
    ppermute x1, waiting for transfers between devices, per_device(): from_even = lax.ppermute(even_edge, 'space', even)  4.33 us
    ppermute x1, waiting for transfers between devices, per_device(): from_odd = lax.ppermute(edges[1], 'space', odd)  2.75 us
    optimization_barrier x2, local copies, waits for them, and re-layouts, per_device(): lax.optimization_barrier((grad, layer_input, hidden_pre))  2.28 us
    ppermute x2, starting transfers between devices, per_device(): lax.ppermute(part, 'space', pairs)  2.17 us
  transfers between devices with their start and end apart: 31, of which 16 were waited for; matrix products, arithmetic and copies ran while one was open for 5% of the time, Pallas kernels for 12%

profile of v3, /device:TPU:0, one launch (start us, length us, event | category | flops | bytes accessed | tf_op | source)
XLA Modules:
  0.0 71.3 jit_solution(14937214768984541066)
XLA Ops:
  0.6 1.0 %fusion.1.refs_1_ = bf16[256,256]{1,0:T(8,128)(2,1)S(1)} fusion(bf16[1,256,1,256]{3,1,2,0:T(8,128)(2,1)} %param.8, bf16[1,256,1,256]{3,1,2,0:T(8,128)(2,1)} %param.9), kind=kLoop, calls=%fused_computation.6 | loop fusion | flops 393216 | bytes 393216 | tf_op jit(solution)/shard_map/mul | solution.py:357
  1.7 6.1 %collective-permute-start.1 = (bf16[256,256]{1,0:T(8,128)(2,1)S(1)}, bf16[256,256]{1,0:T(8,128)(2,1)S(1)}, u32[]{:S(2)}, u32[]{:S(2)}) collective-permute-start(bf16[256,256]{1,0:T(8,128)(2,1)S(1)} %fusion.1.refs_1_), channel_id=1, source_target_pairs={{0,7},{1,2},{2,1},{3,4},{4,3},{5,6},{6,5},{7,0},{8,15},{9,10},{10,... | collective-permute-start | bytes 393224 | tf_op jit(solution)/shard_map/ppermute | solution.py:359
  7.7 1.0 %copy.15 = bf16[1,64,2,1024]{3,1,2,0:T(8,128)(2,1)S(1)} copy(bf16[1,64,2,1024]{3,2,1,0:T(2,128)(2,1)} %param.6) | data formatting | bytes 524288 | tf_op jit(solution)/shard_map/optimization_barrier | solution.py:358
  8.7 1.3 %copy.14 = bf16[1,128,2,1024]{3,1,2,0:T(8,128)(2,1)S(1)} copy(bf16[1,128,2,1024]{3,2,1,0:T(2,128)(2,1)} %param.7) | data formatting | bytes 1048576 | tf_op jit(solution)/shard_map/optimization_barrier | solution.py:358
  10.0 0.5 shard_map.85
  10.6 2.1 %collective-permute-start.5 = (bf16[64,1024]{1,0:T(8,128)(2,1)S(1)}, bf16[64,1024]{1,0:T(8,128)(2,1)S(1)}, u32[]{:S(2)}, u32[]{:S(2)}) collective-permute-start(bf16[64,1024]{1,0:T(8,128)(2,1)S(1)} %get-tuple-element.86), channel_id=1, source_target_pairs={{0,1},{1,0},{2,3},{3,2},{4,5},{5,4},{6,7},{7,6},{8,9},{9,8},{10,11... | collective-permute-start | bytes 393224 | tf_op jit(solution)/shard_map/ppermute | solution.py:375
  12.7 0.1 collective-permute-start.6
  12.8 0.7 shard_map.86.refs_1_
  13.5 0.6 collective-permute-done.refs_2_
  14.2 1.6 %collective-permute-start.3 = (bf16[320,256]{1,0:T(8,128)(2,1)S(1)}, bf16[320,256]{1,0:T(8,128)(2,1)S(1)}, u32[]{:S(2)}, u32[]{:S(2)}) collective-permute-start(bf16[320,256]{1,0:T(8,128)(2,1)S(1)} %get-tuple-element.78), channel_id=1, source_target_pairs={{0,16},{8,24},{16,0},{24,8},{1,17},{9,25},{17,1},{25,9},{2,18},{10... | collective-permute-start | bytes 491528 | tf_op jit(solution)/shard_map/ppermute | solution.py:344
  15.8 1.6 %shard_map.88.refs_1_.refs_0_ = bf16[256,1024]{1,0:T(8,128)(2,1)S(1)} custom-call(bf16[3456,256]{1,0:T(8,128)(2,1)S(1)} %bitcast.32, bf16[256,256]{1,0:T(8,128)(2,1)S(1)} %fusion.1.refs_1_, bf16[256,256]{1,0:T(8,128)(2,1)S(1)} %get-tuple-element.80.refs_2_, bf16[256,256]{1,0:T(8,128)(2,1)S(1)} %get-tuple-element.81.refs_3_, ...), custom_call_target="tpu_custom_call" | custom-call | flops 262144 | bytes 1024 | tf_op jit(solution)/shard_map/pallas_call | solution.py:64
  17.4 1.6 %shard_map.89 = (bf16[64,1024]{1,0:T(8,128)(2,1)S(1)}, bf16[64,1024]{1,0:T(8,128)(2,1)S(1)}) custom-call(bf16[1728,128]{1,0:T(8,128)(2,1)S(1)} %bitcast.33, bf16[256,1024]{1,0:T(8,128)(2,1)S(1)} %shard_map.88.refs_1_.refs_0_), custom_call_target="tpu_custom_call" | custom-call | flops 65536 | bytes 1024 | tf_op jit(solution)/shard_map/pallas_call | solution.py:64
  19.0 1.4 %collective-permute-done.6.refs_3_ = bf16[64,1024]{1,0:T(8,128)(2,1)S(1)} collective-permute-done((bf16[64,1024]{1,0:T(8,128)(2,1)S(1)}, bf16[64,1024]{1,0:T(8,128)(2,1)S(1)}, u32[]{:S(2)}, u32[]{:S(2)}) %collective-permute-start.6) | collective-permute-done | bytes 131104 | tf_op jit(solution)/shard_map/ppermute | solution.py:375
  20.4 1.5 %shard_map.90 = (f32[448,128]{1,0:T(8,128)S(1)}, f32[448,128]{1,0:T(8,128)S(1)}, bf16[448,128]{1,0:T(8,128)(2,1)S(1)}, bf16[448,128]{1,0:T(8,128)(2,1)S(1)}) custom-call(bf16[256,1024]{1,0:T(8,128)(2,1)S(1)} %shard_map.88.refs_1_.refs_0_, bf16[2,576,1024]{2,1,0:T(8,128)(2,1)S(1)} %shard_map.86.refs_1_, bf16[64,1024]{1,0:T(8,128)(2,1)S(1)} %collective-permute-done.5.refs_2_, ...), custom_call_target="tpu_custom_call" | custom-call | flops 262144 | bytes 1024 | tf_op jit(solution)/shard_map/pallas_call | solution.py:64
  22.0 0.5 collective-permute-start.8
  22.5 1.5 %collective-permute-start.4 = (bf16[192,256]{1,0:T(8,128)(2,1)S(1)}, bf16[192,256]{1,0:T(8,128)(2,1)S(1)}, u32[]{:S(2)}, u32[]{:S(2)}) collective-permute-start(bf16[192,256]{1,0:T(8,128)(2,1)S(1)} %get-tuple-element.79), channel_id=1, source_target_pairs={{0,16},{8,24},{16,0},{24,8},{1,17},{9,25},{17,1},{25,9},{2,18},{10... | collective-permute-start | bytes 294920 | tf_op jit(solution)/shard_map/ppermute | solution.py:344
  24.0 1.9 %collective-permute-start.11 = (bf16[64,1024]{1,0:T(8,128)(2,1)S(1)}, bf16[64,1024]{1,0:T(8,128)(2,1)S(1)}, u32[]{:S(2)}, u32[]{:S(2)}) collective-permute-start(bf16[64,1024]{1,0:T(8,128)(2,1)S(1)} %get-tuple-element.97), channel_id=1, source_target_pairs={{0,7},{1,2},{2,1},{3,4},{4,3},{5,6},{6,5},{7,0},{8,15},{9,10},{10,... | collective-permute-start | bytes 393224 | tf_op jit(solution)/shard_map/ppermute | solution.py:457
  26.0 1.3 %collective-permute-start.12 = (bf16[448,128]{1,0:T(8,128)(2,1)S(1)}, bf16[448,128]{1,0:T(8,128)(2,1)S(1)}, u32[]{:S(2)}, u32[]{:S(2)}) collective-permute-start(bf16[448,128]{1,0:T(8,128)(2,1)S(1)} %get-tuple-element.100), channel_id=1, source_target_pairs={{0,16},{8,24},{16,0},{24,8},{1,17},{9,25},{17,1},{25,9},{2,18},{10... | collective-permute-start | bytes 344072 | tf_op jit(solution)/shard_map/ppermute | solution.py:344
  27.3 0.5 collective-permute-start.9
  27.8 0.9 %collective-permute-done.9.refs_3_ = bf16[128,256]{1,0:T(8,128)(2,1)S(1)} collective-permute-done((bf16[128,256]{1,0:T(8,128)(2,1)S(1)}, bf16[128,256]{1,0:T(8,128)(2,1)S(1)}, u32[]{:S(2)}, u32[]{:S(2)}) %collective-permute-start.9) | collective-permute-done | bytes 65568 | tf_op jit(solution)/shard_map/ppermute | solution.py:344
  28.7 1.1 %shard_map.92.refs_0_ = f32[8,216,128]{2,1,0:T(8,128)S(1)} custom-call(bf16[320,256]{1,0:T(8,128)(2,1)S(1)} %get-tuple-element.76.refs_0_.refs_4_, bf16[320,256]{1,0:T(8,128)(2,1)S(1)} %collective-permute-done.2.refs_1_.refs_5_, bf16[320,256]{1,0:T(8,128)(2,1)S(1)} %collective-permute-done.3.refs_2_.refs_6_, ...), custom_call_target="tpu_custom_call" | custom-call | flops 262144 | bytes 1024 | tf_op jit(solution)/shard_map/pallas_call | solution.py:64
  29.8 2.8 %collective-permute-done.11 = bf16[64,1024]{1,0:T(8,128)(2,1)S(1)} collective-permute-done((bf16[64,1024]{1,0:T(8,128)(2,1)S(1)}, bf16[64,1024]{1,0:T(8,128)(2,1)S(1)}, u32[]{:S(2)}, u32[]{:S(2)}) %collective-permute-start.11) | collective-permute-done | bytes 131104 | tf_op jit(solution)/shard_map/ppermute | solution.py:457
  32.8 3.4 %collective-permute-start.15 = (bf16[2,272,128]{2,1,0:T(8,128)(2,1)S(1)}, bf16[2,272,128]{2,1,0:T(8,128)(2,1)S(1)}, u32[]{:S(2)}, u32[]{:S(2)}) collective-permute-start(bf16[2,272,128]{2,1,0:T(8,128)(2,1)S(1)} %get-tuple-element.104), channel_id=1, source_target_pairs={{0,3},{1,2},{2,1},{3,0},{4,7},{5,6},{6,5},{7,4},{8,11},{9,10},{10,... | collective-permute-start | bytes 417800 | tf_op jit(solution)/shard_map/ppermute | solution.py:344
  36.2 1.5 %shard_map.94 = f32[2,64,1024]{2,1,0:T(8,128)S(1)} custom-call(bf16[1728,128]{1,0:T(8,128)(2,1)S(1)} %bitcast.34, bf16[256,1024]{1,0:T(8,128)(2,1)S(1)} %shard_map.88.refs_1_.refs_0_), custom_call_target="tpu_custom_call" | custom-call | flops 65536 | bytes 1024 | tf_op jit(solution)/shard_map/pallas_call | solution.py:64
  37.7 0.7 collective-permute-done.13.refs_1_
  38.4 1.0 %collective-permute-done.14.refs_2_ = bf16[2,272,128]{2,1,0:T(8,128)(2,1)S(1)} collective-permute-done((bf16[2,272,128]{2,1,0:T(8,128)(2,1)S(1)}, bf16[2,272,128]{2,1,0:T(8,128)(2,1)S(1)}, u32[]{:S(2)}, u32[]{:S(2)}) %collective-permute-start.14) | collective-permute-done | bytes 139296 | tf_op jit(solution)/shard_map/ppermute | solution.py:344
  39.4 2.8 %collective-permute-done.15.refs_3_ = bf16[2,272,128]{2,1,0:T(8,128)(2,1)S(1)} collective-permute-done((bf16[2,272,128]{2,1,0:T(8,128)(2,1)S(1)}, bf16[2,272,128]{2,1,0:T(8,128)(2,1)S(1)}, u32[]{:S(2)}, u32[]{:S(2)}) %collective-permute-start.15) | collective-permute-done | bytes 139296 | tf_op jit(solution)/shard_map/ppermute | solution.py:344
  42.3 0.7 collective-permute-start.17
  43.0 4.3 %collective-permute-done.17 = bf16[64,1024]{1,0:T(8,128)(2,1)S(1)} collective-permute-done((bf16[64,1024]{1,0:T(8,128)(2,1)S(1)}, bf16[64,1024]{1,0:T(8,128)(2,1)S(1)}, u32[]{:S(2)}, u32[]{:S(2)}) %collective-permute-start.17) | collective-permute-done | bytes 131104 | tf_op jit(solution)/shard_map/ppermute | solution.py:482
  47.4 2.6 %collective-permute-done.16.refs_1_ = bf16[2,272,128]{2,1,0:T(8,128)(2,1)S(1)} collective-permute-done((bf16[2,272,128]{2,1,0:T(8,128)(2,1)S(1)}, bf16[2,272,128]{2,1,0:T(8,128)(2,1)S(1)}, u32[]{:S(2)}, u32[]{:S(2)}) %collective-permute-start.16) | collective-permute-done | bytes 139296 | tf_op jit(solution)/shard_map/ppermute | solution.py:344
  50.1 1.0 %collective-permute-start.21 = (bf16[2,192,128]{2,1,0:T(8,128)(2,1)S(1)}, bf16[2,192,128]{2,1,0:T(8,128)(2,1)S(1)}, u32[]{:S(2)}, u32[]{:S(2)}) collective-permute-start(bf16[2,192,128]{2,1,0:T(8,128)(2,1)S(1)} %get-tuple-element.114), channel_id=1, source_target_pairs={{0,3},{1,2},{2,1},{3,0},{4,7},{5,6},{6,5},{7,4},{8,11},{9,10},{10,... | collective-permute-start | bytes 294920 | tf_op jit(solution)/shard_map/ppermute | solution.py:344
  51.1 1.0 %collective-permute-start.20 = (bf16[2,192,128]{2,1,0:T(8,128)(2,1)S(1)}, bf16[2,192,128]{2,1,0:T(8,128)(2,1)S(1)}, u32[]{:S(2)}, u32[]{:S(2)}) collective-permute-start(bf16[2,192,128]{2,1,0:T(8,128)(2,1)S(1)} %get-tuple-element.114), channel_id=1, source_target_pairs={{0,2},{1,3},{2,0},{3,1},{4,6},{5,7},{6,4},{7,5},{8,10},{9,11},{10,... | collective-permute-start | bytes 294920 | tf_op jit(solution)/shard_map/ppermute | solution.py:344
  52.2 1.5 %collective-permute-start.19 = (bf16[2,192,128]{2,1,0:T(8,128)(2,1)S(1)}, bf16[2,192,128]{2,1,0:T(8,128)(2,1)S(1)}, u32[]{:S(2)}, u32[]{:S(2)}) collective-permute-start(bf16[2,192,128]{2,1,0:T(8,128)(2,1)S(1)} %get-tuple-element.114), channel_id=1, source_target_pairs={{0,1},{1,0},{2,3},{3,2},{4,5},{5,4},{6,7},{7,6},{8,9},{9,8},{10,11... | collective-permute-start | bytes 294920 | tf_op jit(solution)/shard_map/ppermute | solution.py:344
  53.7 2.1 %collective-permute-done.21.refs_2_.refs_4_ = bf16[2,192,128]{2,1,0:T(8,128)(2,1)S(1)} collective-permute-done((bf16[2,192,128]{2,1,0:T(8,128)(2,1)S(1)}, bf16[2,192,128]{2,1,0:T(8,128)(2,1)S(1)}, u32[]{:S(2)}, u32[]{:S(2)}) %collective-permute-start.21) | collective-permute-done | bytes 98336 | tf_op jit(solution)/shard_map/ppermute | solution.py:344
  55.8 0.3 collective-permute-done.20.refs_1_.refs_3_
  56.1 0.8 %collective-permute-done.19.refs_0_.refs_2_ = bf16[2,192,128]{2,1,0:T(8,128)(2,1)S(1)} collective-permute-done((bf16[2,192,128]{2,1,0:T(8,128)(2,1)S(1)}, bf16[2,192,128]{2,1,0:T(8,128)(2,1)S(1)}, u32[]{:S(2)}, u32[]{:S(2)}) %collective-permute-start.19) | collective-permute-done | bytes 98336 | tf_op jit(solution)/shard_map/ppermute | solution.py:344
  57.1 1.9 %collective-permute-start.22 = (bf16[6,192,128]{2,1,0:T(8,128)(2,1)S(1)}, bf16[6,192,128]{2,1,0:T(8,128)(2,1)S(1)}, u32[]{:S(2)}, u32[]{:S(2)}) collective-permute-start(bf16[6,192,128]{2,1,0:T(8,128)(2,1)S(1)} %shard_map.97), channel_id=1, source_target_pairs={{0,16},{8,24},{16,0},{24,8},{1,17},{9,25},{17,1},{25,9},{2,18},{10... | collective-permute-start | bytes 884744 | tf_op jit(solution)/shard_map/ppermute | solution.py:344
  59.0 1.0 %collective-permute-start.25 = (bf16[4,80,128]{2,1,0:T(8,128)(2,1)S(1)}, bf16[4,80,128]{2,1,0:T(8,128)(2,1)S(1)}, u32[]{:S(2)}, u32[]{:S(2)}) collective-permute-start(bf16[4,80,128]{2,1,0:T(8,128)(2,1)S(1)} %shard_map.98), channel_id=1, source_target_pairs={{0,3},{1,2},{2,1},{3,0},{4,7},{5,6},{6,5},{7,4},{8,11},{9,10},{10,... | collective-permute-start | bytes 245768 | tf_op jit(solution)/shard_map/ppermute | solution.py:344
  60.0 2.0 %collective-permute-start.24 = (bf16[4,80,128]{2,1,0:T(8,128)(2,1)S(1)}, bf16[4,80,128]{2,1,0:T(8,128)(2,1)S(1)}, u32[]{:S(2)}, u32[]{:S(2)}) collective-permute-start(bf16[4,80,128]{2,1,0:T(8,128)(2,1)S(1)} %shard_map.98), channel_id=1, source_target_pairs={{0,2},{1,3},{2,0},{3,1},{4,6},{5,7},{6,4},{7,5},{8,10},{9,11},{10,... | collective-permute-start | bytes 245768 | tf_op jit(solution)/shard_map/ppermute | solution.py:344
  62.1 0.5 collective-permute-start.23
  62.6 2.6 %collective-permute-done.25.refs_4_ = bf16[4,80,128]{2,1,0:T(8,128)(2,1)S(1)} collective-permute-done((bf16[4,80,128]{2,1,0:T(8,128)(2,1)S(1)}, bf16[4,80,128]{2,1,0:T(8,128)(2,1)S(1)}, u32[]{:S(2)}, u32[]{:S(2)}) %collective-permute-start.25) | collective-permute-done | bytes 81952 | tf_op jit(solution)/shard_map/ppermute | solution.py:344
  65.3 1.1 %collective-permute-done.24.refs_3_ = bf16[4,80,128]{2,1,0:T(8,128)(2,1)S(1)} collective-permute-done((bf16[4,80,128]{2,1,0:T(8,128)(2,1)S(1)}, bf16[4,80,128]{2,1,0:T(8,128)(2,1)S(1)}, u32[]{:S(2)}, u32[]{:S(2)}) %collective-permute-start.24) | collective-permute-done | bytes 81952 | tf_op jit(solution)/shard_map/ppermute | solution.py:344
  66.3 0.2 collective-permute-done.23.refs_2_
  66.5 0.1 collective-permute-done.22.refs_1_
  66.6 0.5 collective-permute-start.28
  67.2 0.5 collective-permute-start.30
  67.7 1.0 %copy.11 = bf16[1,64,2,1024]{3,2,1,0:T(2,128)(2,1)} copy(bf16[1,64,2,1024]{3,1,2,0:T(8,128)(2,1)S(1)} %fusion) | data formatting | bytes 524288
  68.7 2.6 %shard_map.100 = (f32[1728,128]{1,0:T(8,128)}, f32[3456,256]{1,0:T(8,128)}) custom-call(bf16[2240,128]{1,0:T(8,128)(2,1)S(1)} %shard_map.99.refs_0_, bf16[6,192,128]{2,1,0:T(8,128)(2,1)S(1)} %collective-permute-done.22.refs_1_, bf16[4,80,128]{2,1,0:T(8,128)(2,1)S(1)} %collective-permute-done.23.refs_2_, ...), custom_call_target="tpu_custom_call" | custom-call | flops 256 | bytes 1024 | tf_op jit(solution)/shard_map/pallas_call | solution.py:64
  (42 shorter events, 1.0 us)
Async XLA Ops:
  1.7 11.8 %collective-permute-start.1 = (bf16[256,256]{1,0:T(8,128)(2,1)S(1)}, bf16[256,256]{1,0:T(8,128)(2,1)S(1)}, u32[]{:S(2)}, u32[]{:S(2)}) collective-permute-start(bf16[256,256]{1,0:T(8,128)(2,1)S(1)} %fusion.1.refs_1_), channel_id=1, source_target_pairs={{0,7},{1,2},{2,1},{3,4},{4,3},{5,6},{6,5},{7,0},{8,15},{9,10},{10,... | collective-permute-start | bytes 393224 | tf_op jit(solution)/shard_map/ppermute | solution.py:359
  7.7 6.4 %collective-permute-start = (bf16[256,256]{1,0:T(8,128)(2,1)S(1)}, bf16[256,256]{1,0:T(8,128)(2,1)S(1)}, u32[]{:S(2)}, u32[]{:S(2)}) collective-permute-start(bf16[256,256]{1,0:T(8,128)(2,1)S(1)} %fusion.1.refs_1_), channel_id=1, source_target_pairs={{0,1},{1,0},{2,3},{3,2},{4,5},{5,4},{6,7},{7,6},{8,9},{9,8},{10,11... | collective-permute-start | bytes 393224 | tf_op jit(solution)/shard_map/ppermute | solution.py:359
  8.7 7.0 %copy-start = (bf16[27,128,256]{2,1,0:T(8,128)(2,1)S(1)}, bf16[27,128,256]{2,1,0:T(8,128)(2,1)}, u32[]{:S(2)}) copy-start(bf16[27,128,256]{2,1,0:T(8,128)(2,1)} %param.11) | copy-start | bytes 5308420
  10.6 8.3 %collective-permute-start.5 = (bf16[64,1024]{1,0:T(8,128)(2,1)S(1)}, bf16[64,1024]{1,0:T(8,128)(2,1)S(1)}, u32[]{:S(2)}, u32[]{:S(2)}) collective-permute-start(bf16[64,1024]{1,0:T(8,128)(2,1)S(1)} %get-tuple-element.86), channel_id=1, source_target_pairs={{0,1},{1,0},{2,3},{3,2},{4,5},{5,4},{6,7},{7,6},{8,9},{9,8},{10,11... | collective-permute-start | bytes 393224 | tf_op jit(solution)/shard_map/ppermute | solution.py:375
  12.7 7.7 %collective-permute-start.6 = (bf16[64,1024]{1,0:T(8,128)(2,1)S(1)}, bf16[64,1024]{1,0:T(8,128)(2,1)S(1)}, u32[]{:S(2)}, u32[]{:S(2)}) collective-permute-start(bf16[64,1024]{1,0:T(8,128)(2,1)S(1)} %get-tuple-element.87), channel_id=1, source_target_pairs={{0,7},{1,2},{2,1},{3,4},{4,3},{5,6},{6,5},{7,0},{8,15},{9,10},{10,... | collective-permute-start | bytes 393224 | tf_op jit(solution)/shard_map/ppermute | solution.py:375
  13.5 3.9 %copy-start.1 = (bf16[27,64,128]{2,1,0:T(8,128)(2,1)S(1)}, bf16[27,64,128]{2,1,0:T(8,128)(2,1)}, u32[]{:S(2)}) copy-start(bf16[27,64,128]{2,1,0:T(8,128)(2,1)} %param.10) | copy-start | bytes 1327108
  14.2 13.1 %collective-permute-start.3 = (bf16[320,256]{1,0:T(8,128)(2,1)S(1)}, bf16[320,256]{1,0:T(8,128)(2,1)S(1)}, u32[]{:S(2)}, u32[]{:S(2)}) collective-permute-start(bf16[320,256]{1,0:T(8,128)(2,1)S(1)} %get-tuple-element.78), channel_id=1, source_target_pairs={{0,16},{8,24},{16,0},{24,8},{1,17},{9,25},{17,1},{25,9},{2,18},{10... | collective-permute-start | bytes 491528 | tf_op jit(solution)/shard_map/ppermute | solution.py:344
  21.9 2.1 %collective-permute-start.7 = (bf16[448,128]{1,0:T(8,128)(2,1)S(1)}, bf16[448,128]{1,0:T(8,128)(2,1)S(1)}, u32[]{:S(2)}, u32[]{:S(2)}) collective-permute-start(bf16[448,128]{1,0:T(8,128)(2,1)S(1)} %get-tuple-element.92), channel_id=1, source_target_pairs={{0,8},{8,0},{16,24},{24,16},{1,9},{9,1},{17,25},{25,17},{2,10},{10... | collective-permute-start | bytes 344072 | tf_op jit(solution)/shard_map/ppermute | solution.py:344
  22.0 3.9 %collective-permute-start.8 = (bf16[448,128]{1,0:T(8,128)(2,1)S(1)}, bf16[448,128]{1,0:T(8,128)(2,1)S(1)}, u32[]{:S(2)}, u32[]{:S(2)}) collective-permute-start(bf16[448,128]{1,0:T(8,128)(2,1)S(1)} %get-tuple-element.93), channel_id=1, source_target_pairs={{0,8},{8,0},{16,24},{24,16},{1,9},{9,1},{17,25},{25,17},{2,10},{10... | collective-permute-start | bytes 344072 | tf_op jit(solution)/shard_map/ppermute | solution.py:344
  22.5 4.8 %collective-permute-start.4 = (bf16[192,256]{1,0:T(8,128)(2,1)S(1)}, bf16[192,256]{1,0:T(8,128)(2,1)S(1)}, u32[]{:S(2)}, u32[]{:S(2)}) collective-permute-start(bf16[192,256]{1,0:T(8,128)(2,1)S(1)} %get-tuple-element.79), channel_id=1, source_target_pairs={{0,16},{8,24},{16,0},{24,8},{1,17},{9,25},{17,1},{25,9},{2,18},{10... | collective-permute-start | bytes 294920 | tf_op jit(solution)/shard_map/ppermute | solution.py:344
  24.0 3.8 %collective-permute-start.2 = (bf16[320,256]{1,0:T(8,128)(2,1)S(1)}, bf16[320,256]{1,0:T(8,128)(2,1)S(1)}, u32[]{:S(2)}, u32[]{:S(2)}) collective-permute-start(bf16[320,256]{1,0:T(8,128)(2,1)S(1)} %get-tuple-element.77), channel_id=1, source_target_pairs={{0,8},{8,0},{16,24},{24,16},{1,9},{9,1},{17,25},{25,17},{2,10},{10... | collective-permute-start | bytes 491528 | tf_op jit(solution)/shard_map/ppermute | solution.py:344
  24.0 8.6 %collective-permute-start.11 = (bf16[64,1024]{1,0:T(8,128)(2,1)S(1)}, bf16[64,1024]{1,0:T(8,128)(2,1)S(1)}, u32[]{:S(2)}, u32[]{:S(2)}) collective-permute-start(bf16[64,1024]{1,0:T(8,128)(2,1)S(1)} %get-tuple-element.97), channel_id=1, source_target_pairs={{0,7},{1,2},{2,1},{3,4},{4,3},{5,6},{6,5},{7,0},{8,15},{9,10},{10,... | collective-permute-start | bytes 393224 | tf_op jit(solution)/shard_map/ppermute | solution.py:457
  26.0 6.6 %collective-permute-start.12 = (bf16[448,128]{1,0:T(8,128)(2,1)S(1)}, bf16[448,128]{1,0:T(8,128)(2,1)S(1)}, u32[]{:S(2)}, u32[]{:S(2)}) collective-permute-start(bf16[448,128]{1,0:T(8,128)(2,1)S(1)} %get-tuple-element.100), channel_id=1, source_target_pairs={{0,16},{8,24},{16,0},{24,8},{1,17},{9,25},{17,1},{25,9},{2,18},{10... | collective-permute-start | bytes 344072 | tf_op jit(solution)/shard_map/ppermute | solution.py:344
  27.2 1.4 %collective-permute-start.10 = (bf16[192,256]{1,0:T(8,128)(2,1)S(1)}, bf16[192,256]{1,0:T(8,128)(2,1)S(1)}, u32[]{:S(2)}, u32[]{:S(2)}) collective-permute-start(bf16[192,256]{1,0:T(8,128)(2,1)S(1)} %collective-permute-done.4), channel_id=1, source_target_pairs={{0,8},{8,0},{16,24},{24,16},{1,9},{9,1},{17,25},{25,17},{2,10},{10... | collective-permute-start | bytes 294920 | tf_op jit(solution)/shard_map/ppermute | solution.py:344
  27.3 1.4 %collective-permute-start.9 = (bf16[128,256]{1,0:T(8,128)(2,1)S(1)}, bf16[128,256]{1,0:T(8,128)(2,1)S(1)}, u32[]{:S(2)}, u32[]{:S(2)}) collective-permute-start(bf16[128,256]{1,0:T(8,128)(2,1)S(1)} %slice.11), channel_id=1, source_target_pairs={{0,8},{8,0},{16,24},{24,16},{1,9},{9,1},{17,25},{25,17},{2,10},{10... | collective-permute-start | bytes 196616 | tf_op jit(solution)/shard_map/ppermute | solution.py:344
  32.7 5.8 %collective-permute-start.13 = (bf16[2,272,128]{2,1,0:T(8,128)(2,1)S(1)}, bf16[2,272,128]{2,1,0:T(8,128)(2,1)S(1)}, u32[]{:S(2)}, u32[]{:S(2)}) collective-permute-start(bf16[2,272,128]{2,1,0:T(8,128)(2,1)S(1)} %get-tuple-element.102), channel_id=1, source_target_pairs={{0,1},{1,0},{2,3},{3,2},{4,5},{5,4},{6,7},{7,6},{8,9},{9,8},{10,11... | collective-permute-start | bytes 417800 | tf_op jit(solution)/shard_map/ppermute | solution.py:344
  32.7 6.6 %collective-permute-start.14 = (bf16[2,272,128]{2,1,0:T(8,128)(2,1)S(1)}, bf16[2,272,128]{2,1,0:T(8,128)(2,1)S(1)}, u32[]{:S(2)}, u32[]{:S(2)}) collective-permute-start(bf16[2,272,128]{2,1,0:T(8,128)(2,1)S(1)} %get-tuple-element.103), channel_id=1, source_target_pairs={{0,2},{1,3},{2,0},{3,1},{4,6},{5,7},{6,4},{7,5},{8,10},{9,11},{10,... | collective-permute-start | bytes 417800 | tf_op jit(solution)/shard_map/ppermute | solution.py:344
  32.8 9.4 %collective-permute-start.15 = (bf16[2,272,128]{2,1,0:T(8,128)(2,1)S(1)}, bf16[2,272,128]{2,1,0:T(8,128)(2,1)S(1)}, u32[]{:S(2)}, u32[]{:S(2)}) collective-permute-start(bf16[2,272,128]{2,1,0:T(8,128)(2,1)S(1)} %get-tuple-element.104), channel_id=1, source_target_pairs={{0,3},{1,2},{2,1},{3,0},{4,7},{5,6},{6,5},{7,4},{8,11},{9,10},{10,... | collective-permute-start | bytes 417800 | tf_op jit(solution)/shard_map/ppermute | solution.py:344
  42.3 7.8 %collective-permute-start.16 = (bf16[2,272,128]{2,1,0:T(8,128)(2,1)S(1)}, bf16[2,272,128]{2,1,0:T(8,128)(2,1)S(1)}, u32[]{:S(2)}, u32[]{:S(2)}) collective-permute-start(bf16[2,272,128]{2,1,0:T(8,128)(2,1)S(1)} %shard_map.95.refs_0_), channel_id=1, source_target_pairs={{0,4},{1,5},{2,6},{3,7},{4,0},{5,1},{6,2},{7,3},{8,12},{9,13},{10,... | collective-permute-start | bytes 417800 | tf_op jit(solution)/shard_map/ppermute | solution.py:344
  42.3 5.0 %collective-permute-start.17 = (bf16[64,1024]{1,0:T(8,128)(2,1)S(1)}, bf16[64,1024]{1,0:T(8,128)(2,1)S(1)}, u32[]{:S(2)}, u32[]{:S(2)}) collective-permute-start(bf16[64,1024]{1,0:T(8,128)(2,1)S(1)} %get-tuple-element.111), channel_id=1, source_target_pairs={{0,1},{1,0},{2,3},{3,2},{4,5},{5,4},{6,7},{7,6},{8,9},{9,8},{10,11... | collective-permute-start | bytes 393224 | tf_op jit(solution)/shard_map/ppermute | solution.py:482
  50.1 6.8 %collective-permute-start.18 = (bf16[2,272,128]{2,1,0:T(8,128)(2,1)S(1)}, bf16[2,272,128]{2,1,0:T(8,128)(2,1)S(1)}, u32[]{:S(2)}, u32[]{:S(2)}) collective-permute-start(bf16[2,272,128]{2,1,0:T(8,128)(2,1)S(1)} %get-tuple-element.118.refs_0_), channel_id=1, source_target_pairs={{0,16},{8,24},{16,0},{24,8},{1,17},{9,25},{17,1},{25,9},{2,18},{10... | collective-permute-start | bytes 417800 | tf_op jit(solution)/shard_map/ppermute | solution.py:344
  50.1 5.7 %collective-permute-start.21 = (bf16[2,192,128]{2,1,0:T(8,128)(2,1)S(1)}, bf16[2,192,128]{2,1,0:T(8,128)(2,1)S(1)}, u32[]{:S(2)}, u32[]{:S(2)}) collective-permute-start(bf16[2,192,128]{2,1,0:T(8,128)(2,1)S(1)} %get-tuple-element.114), channel_id=1, source_target_pairs={{0,3},{1,2},{2,1},{3,0},{4,7},{5,6},{6,5},{7,4},{8,11},{9,10},{10,... | collective-permute-start | bytes 294920 | tf_op jit(solution)/shard_map/ppermute | solution.py:344
  51.1 5.0 %collective-permute-start.20 = (bf16[2,192,128]{2,1,0:T(8,128)(2,1)S(1)}, bf16[2,192,128]{2,1,0:T(8,128)(2,1)S(1)}, u32[]{:S(2)}, u32[]{:S(2)}) collective-permute-start(bf16[2,192,128]{2,1,0:T(8,128)(2,1)S(1)} %get-tuple-element.114), channel_id=1, source_target_pairs={{0,2},{1,3},{2,0},{3,1},{4,6},{5,7},{6,4},{7,5},{8,10},{9,11},{10,... | collective-permute-start | bytes 294920 | tf_op jit(solution)/shard_map/ppermute | solution.py:344
  52.2 4.7 %collective-permute-start.19 = (bf16[2,192,128]{2,1,0:T(8,128)(2,1)S(1)}, bf16[2,192,128]{2,1,0:T(8,128)(2,1)S(1)}, u32[]{:S(2)}, u32[]{:S(2)}) collective-permute-start(bf16[2,192,128]{2,1,0:T(8,128)(2,1)S(1)} %get-tuple-element.114), channel_id=1, source_target_pairs={{0,1},{1,0},{2,3},{3,2},{4,5},{5,4},{6,7},{7,6},{8,9},{9,8},{10,11... | collective-permute-start | bytes 294920 | tf_op jit(solution)/shard_map/ppermute | solution.py:344
  56.9 9.7 %collective-permute-start.26 = (bf16[2240,128]{1,0:T(8,128)(2,1)S(1)}, bf16[2240,128]{1,0:T(8,128)(2,1)S(1)}, u32[]{:S(2)}, u32[]{:S(2)}) collective-permute-start(bf16[2240,128]{1,0:T(8,128)(2,1)S(1)} %shard_map.99.refs_0_), channel_id=1, source_target_pairs={{0,8},{8,0},{16,24},{24,16},{1,9},{9,1},{17,25},{25,17},{2,10},{10... | collective-permute-start | bytes 1720328 | tf_op jit(solution)/shard_map/ppermute | solution.py:344
  57.1 9.6 %collective-permute-start.22 = (bf16[6,192,128]{2,1,0:T(8,128)(2,1)S(1)}, bf16[6,192,128]{2,1,0:T(8,128)(2,1)S(1)}, u32[]{:S(2)}, u32[]{:S(2)}) collective-permute-start(bf16[6,192,128]{2,1,0:T(8,128)(2,1)S(1)} %shard_map.97), channel_id=1, source_target_pairs={{0,16},{8,24},{16,0},{24,8},{1,17},{9,25},{17,1},{25,9},{2,18},{10... | collective-permute-start | bytes 884744 | tf_op jit(solution)/shard_map/ppermute | solution.py:344
  59.0 6.2 %collective-permute-start.25 = (bf16[4,80,128]{2,1,0:T(8,128)(2,1)S(1)}, bf16[4,80,128]{2,1,0:T(8,128)(2,1)S(1)}, u32[]{:S(2)}, u32[]{:S(2)}) collective-permute-start(bf16[4,80,128]{2,1,0:T(8,128)(2,1)S(1)} %shard_map.98), channel_id=1, source_target_pairs={{0,3},{1,2},{2,1},{3,0},{4,7},{5,6},{6,5},{7,4},{8,11},{9,10},{10,... | collective-permute-start | bytes 245768 | tf_op jit(solution)/shard_map/ppermute | solution.py:344
  60.0 6.3 %collective-permute-start.24 = (bf16[4,80,128]{2,1,0:T(8,128)(2,1)S(1)}, bf16[4,80,128]{2,1,0:T(8,128)(2,1)S(1)}, u32[]{:S(2)}, u32[]{:S(2)}) collective-permute-start(bf16[4,80,128]{2,1,0:T(8,128)(2,1)S(1)} %shard_map.98), channel_id=1, source_target_pairs={{0,2},{1,3},{2,0},{3,1},{4,6},{5,7},{6,4},{7,5},{8,10},{9,11},{10,... | collective-permute-start | bytes 245768 | tf_op jit(solution)/shard_map/ppermute | solution.py:344
  62.1 4.5 %collective-permute-start.23 = (bf16[4,80,128]{2,1,0:T(8,128)(2,1)S(1)}, bf16[4,80,128]{2,1,0:T(8,128)(2,1)S(1)}, u32[]{:S(2)}, u32[]{:S(2)}) collective-permute-start(bf16[4,80,128]{2,1,0:T(8,128)(2,1)S(1)} %shard_map.98), channel_id=1, source_target_pairs={{0,1},{1,0},{2,3},{3,2},{4,5},{5,4},{6,7},{7,6},{8,9},{9,8},{10,11... | collective-permute-start | bytes 245768 | tf_op jit(solution)/shard_map/ppermute | solution.py:344
  66.6 2.0 %collective-permute-start.27 = (bf16[6,192,128]{2,1,0:T(8,128)(2,1)S(1)}, bf16[6,192,128]{2,1,0:T(8,128)(2,1)S(1)}, u32[]{:S(2)}, u32[]{:S(2)}) collective-permute-start(bf16[6,192,128]{2,1,0:T(8,128)(2,1)S(1)} %collective-permute-done.22.refs_1_), channel_id=1, source_target_pairs={{0,8},{8,0},{16,24},{24,16},{1,9},{9,1},{17,25},{25,17},{2,10},{10... | collective-permute-start | bytes 884744 | tf_op jit(solution)/shard_map/ppermute | solution.py:344
  66.6 2.0 %collective-permute-start.28 = (bf16[4,80,128]{2,1,0:T(8,128)(2,1)S(1)}, bf16[4,80,128]{2,1,0:T(8,128)(2,1)S(1)}, u32[]{:S(2)}, u32[]{:S(2)}) collective-permute-start(bf16[4,80,128]{2,1,0:T(8,128)(2,1)S(1)} %collective-permute-done.23.refs_2_), channel_id=1, source_target_pairs={{0,8},{8,0},{16,24},{24,16},{1,9},{9,1},{17,25},{25,17},{2,10},{10... | collective-permute-start | bytes 245768 | tf_op jit(solution)/shard_map/ppermute | solution.py:344
  67.2 1.5 %collective-permute-start.29 = (bf16[4,80,128]{2,1,0:T(8,128)(2,1)S(1)}, bf16[4,80,128]{2,1,0:T(8,128)(2,1)S(1)}, u32[]{:S(2)}, u32[]{:S(2)}) collective-permute-start(bf16[4,80,128]{2,1,0:T(8,128)(2,1)S(1)} %collective-permute-done.24.refs_3_), channel_id=1, source_target_pairs={{0,8},{8,0},{16,24},{24,16},{1,9},{9,1},{17,25},{25,17},{2,10},{10... | collective-permute-start | bytes 245768 | tf_op jit(solution)/shard_map/ppermute | solution.py:344
  67.2 1.5 %collective-permute-start.30 = (bf16[4,80,128]{2,1,0:T(8,128)(2,1)S(1)}, bf16[4,80,128]{2,1,0:T(8,128)(2,1)S(1)}, u32[]{:S(2)}, u32[]{:S(2)}) collective-permute-start(bf16[4,80,128]{2,1,0:T(8,128)(2,1)S(1)} %collective-permute-done.25.refs_4_), channel_id=1, source_target_pairs={{0,8},{8,0},{16,24},{24,16},{1,9},{9,1},{17,25},{25,17},{2,10},{10... | collective-permute-start | bytes 245768 | tf_op jit(solution)/shard_map/ppermute | solution.py:344

commit v4 on v3

--- a/solution.py
+++ b/solution.py
@@ -454,7 +454,8 @@
         *pooled_parts,
         *channel_parts,
     )
-    from_odd = lax.ppermute(edges[1], "space", odd)
+    inside = [(i, k) if abs(i - k) == 1 else (i, i) for i, k in odd]
+    from_odd = lax.ppermute(edges[1], "space", inside)
     far = plan.far
     totals, from_odd = lax.optimization_barrier((totals, from_odd))
     blocks = call(

time: 71.4 us -> 71 us (level)
  waiting for transfers between devices: 24.4 us -> 21.8 us
  starting transfers between devices: 30.1 us -> 32 us
    ppermute x1, waiting for transfers between devices: 2.75 us -> 0.01 us  [per_device(): from_odd = lax.ppermute(edges[1], 'space', inside)]
    ppermute x25, starting transfers between devices: 19.2 us -> 21.4 us  [swapped(): lax.ppermute(part, axis, [(i, i ^ distance) for i in range(lax.axis_size(...]
    ppermute x1, starting transfers between devices: 1.94 us -> 0.84 us  [per_device(): from_odd = lax.ppermute(edges[1], 'space', inside)]
    ppermute x25, waiting for transfers between devices: 15.2 us -> 16.3 us  [swapped(): lax.ppermute(part, axis, [(i, i ^ distance) for i in range(lax.axis_size(...]
    ppermute x1, waiting for transfers between devices: 4.33 us -> 3.4 us  [per_device(): from_even = lax.ppermute(even_edge, 'space', even)]
    ppermute x1, starting transfers between devices: 0.7 us -> 1.57 us  [per_device(): from_even = lax.ppermute(even_edge, 'space', even)]
  transfers between devices with their start and end apart: 31 -> 31, of which waited for: 16 -> 17; matrix products, arithmetic and copies ran while one was open for 5% -> 5% of each run, Pallas kernels for 12% -> 12%
where the time goes in v4:
time: 71 us; the launch traced here: 70.8 us
  starting transfers between devices  32 us (45%)
  waiting for transfers between devices  21.8 us (31%)
  Pallas kernels  11.5 us (16%)
  local copies, waits for them, and re-layouts  3.27 us (5%)
  other arithmetic  1.12 us (2%)
  between operations  1.05 us (1%)
    ppermute x25, starting transfers between devices, swapped(): lax.ppermute(part, axis, [(i, i ^ distance) for i in range(lax.axis_size(...  21.4 us
    ppermute x25, waiting for transfers between devices, swapped(): lax.ppermute(part, axis, [(i, i ^ distance) for i in range(lax.axis_size(...  16.3 us
    pallas_call x16, Pallas kernels, call(): pl.pallas_call(kernel, out_shape=out_shape, in_specs=[vmem] * len(args),...  11.5 us
    ppermute x2, starting transfers between devices, per_device(): grad_sides = [lax.ppermute(grad, 'space', pairs) for pairs in (even, odd)]  6.07 us
    ppermute x1, waiting for transfers between devices, per_device(): from_even = lax.ppermute(even_edge, 'space', even)  3.4 us
    optimization_barrier x2, local copies, waits for them, and re-layouts, per_device(): lax.optimization_barrier((grad, layer_input, hidden_pre))  2.28 us
    ppermute x2, starting transfers between devices, per_device(): lax.ppermute(part, 'space', pairs)  2.17 us
    ppermute x1, starting transfers between devices, per_device(): from_even = lax.ppermute(even_edge, 'space', even)  1.57 us
  transfers between devices with their start and end apart: 31, of which 17 were waited for; matrix products, arithmetic and copies ran while one was open for 5% of the time, Pallas kernels for 12%

profile of v4, /device:TPU:0, one launch (start us, length us, event | category | flops | bytes accessed | tf_op | source)
XLA Modules:
  0.0 70.8 jit_solution(4451637829255931542)
XLA Ops:
  0.6 1.0 %fusion.1.refs_1_ = bf16[256,256]{1,0:T(8,128)(2,1)S(1)} fusion(bf16[1,256,1,256]{3,1,2,0:T(8,128)(2,1)} %param.8, bf16[1,256,1,256]{3,1,2,0:T(8,128)(2,1)} %param.9), kind=kLoop, calls=%fused_computation.6 | loop fusion | flops 393216 | bytes 393216 | tf_op jit(solution)/shard_map/mul | solution.py:357
  1.7 6.1 %collective-permute-start.1 = (bf16[256,256]{1,0:T(8,128)(2,1)S(1)}, bf16[256,256]{1,0:T(8,128)(2,1)S(1)}, u32[]{:S(2)}, u32[]{:S(2)}) collective-permute-start(bf16[256,256]{1,0:T(8,128)(2,1)S(1)} %fusion.1.refs_1_), channel_id=1, source_target_pairs={{0,7},{1,2},{2,1},{3,4},{4,3},{5,6},{6,5},{7,0},{8,15},{9,10},{10,... | collective-permute-start | bytes 393224 | tf_op jit(solution)/shard_map/ppermute | solution.py:359
  7.7 1.0 %copy.15 = bf16[1,64,2,1024]{3,1,2,0:T(8,128)(2,1)S(1)} copy(bf16[1,64,2,1024]{3,2,1,0:T(2,128)(2,1)} %param.6) | data formatting | bytes 524288 | tf_op jit(solution)/shard_map/optimization_barrier | solution.py:358
  8.7 1.3 %copy.14 = bf16[1,128,2,1024]{3,1,2,0:T(8,128)(2,1)S(1)} copy(bf16[1,128,2,1024]{3,2,1,0:T(2,128)(2,1)} %param.7) | data formatting | bytes 1048576 | tf_op jit(solution)/shard_map/optimization_barrier | solution.py:358
  10.0 0.5 shard_map.85
  10.6 2.1 %collective-permute-start.5 = (bf16[64,1024]{1,0:T(8,128)(2,1)S(1)}, bf16[64,1024]{1,0:T(8,128)(2,1)S(1)}, u32[]{:S(2)}, u32[]{:S(2)}) collective-permute-start(bf16[64,1024]{1,0:T(8,128)(2,1)S(1)} %get-tuple-element.86), channel_id=1, source_target_pairs={{0,1},{1,0},{2,3},{3,2},{4,5},{5,4},{6,7},{7,6},{8,9},{9,8},{10,11... | collective-permute-start | bytes 393224 | tf_op jit(solution)/shard_map/ppermute | solution.py:375
  12.8 0.7 shard_map.86.refs_1_
  13.5 0.6 collective-permute-done.refs_2_
  14.2 1.6 %collective-permute-start.3 = (bf16[320,256]{1,0:T(8,128)(2,1)S(1)}, bf16[320,256]{1,0:T(8,128)(2,1)S(1)}, u32[]{:S(2)}, u32[]{:S(2)}) collective-permute-start(bf16[320,256]{1,0:T(8,128)(2,1)S(1)} %get-tuple-element.78), channel_id=1, source_target_pairs={{0,16},{8,24},{16,0},{24,8},{1,17},{9,25},{17,1},{25,9},{2,18},{10... | collective-permute-start | bytes 491528 | tf_op jit(solution)/shard_map/ppermute | solution.py:344
  15.8 1.6 %shard_map.88.refs_1_.refs_0_ = bf16[256,1024]{1,0:T(8,128)(2,1)S(1)} custom-call(bf16[3456,256]{1,0:T(8,128)(2,1)S(1)} %bitcast.32, bf16[256,256]{1,0:T(8,128)(2,1)S(1)} %fusion.1.refs_1_, bf16[256,256]{1,0:T(8,128)(2,1)S(1)} %get-tuple-element.80.refs_2_, bf16[256,256]{1,0:T(8,128)(2,1)S(1)} %get-tuple-element.81.refs_3_, ...), custom_call_target="tpu_custom_call" | custom-call | flops 262144 | bytes 1024 | tf_op jit(solution)/shard_map/pallas_call | solution.py:64
  17.4 1.5 %shard_map.89 = (bf16[64,1024]{1,0:T(8,128)(2,1)S(1)}, bf16[64,1024]{1,0:T(8,128)(2,1)S(1)}) custom-call(bf16[1728,128]{1,0:T(8,128)(2,1)S(1)} %bitcast.33, bf16[256,1024]{1,0:T(8,128)(2,1)S(1)} %shard_map.88.refs_1_.refs_0_), custom_call_target="tpu_custom_call" | custom-call | flops 65536 | bytes 1024 | tf_op jit(solution)/shard_map/pallas_call | solution.py:64
  19.0 1.4 %collective-permute-done.6.refs_3_ = bf16[64,1024]{1,0:T(8,128)(2,1)S(1)} collective-permute-done((bf16[64,1024]{1,0:T(8,128)(2,1)S(1)}, bf16[64,1024]{1,0:T(8,128)(2,1)S(1)}, u32[]{:S(2)}, u32[]{:S(2)}) %collective-permute-start.6) | collective-permute-done | bytes 131104 | tf_op jit(solution)/shard_map/ppermute | solution.py:375
  20.4 1.5 %shard_map.90 = (f32[448,128]{1,0:T(8,128)S(1)}, f32[448,128]{1,0:T(8,128)S(1)}, bf16[448,128]{1,0:T(8,128)(2,1)S(1)}, bf16[448,128]{1,0:T(8,128)(2,1)S(1)}) custom-call(bf16[256,1024]{1,0:T(8,128)(2,1)S(1)} %shard_map.88.refs_1_.refs_0_, bf16[2,576,1024]{2,1,0:T(8,128)(2,1)S(1)} %shard_map.86.refs_1_, bf16[64,1024]{1,0:T(8,128)(2,1)S(1)} %collective-permute-done.5.refs_2_, ...), custom_call_target="tpu_custom_call" | custom-call | flops 262144 | bytes 1024 | tf_op jit(solution)/shard_map/pallas_call | solution.py:64
  22.5 1.5 %collective-permute-start.4 = (bf16[192,256]{1,0:T(8,128)(2,1)S(1)}, bf16[192,256]{1,0:T(8,128)(2,1)S(1)}, u32[]{:S(2)}, u32[]{:S(2)}) collective-permute-start(bf16[192,256]{1,0:T(8,128)(2,1)S(1)} %get-tuple-element.79), channel_id=1, source_target_pairs={{0,16},{8,24},{16,0},{24,8},{1,17},{9,25},{17,1},{25,9},{2,18},{10... | collective-permute-start | bytes 294920 | tf_op jit(solution)/shard_map/ppermute | solution.py:344
  24.0 0.8 %collective-permute-start.11 = (bf16[64,1024]{1,0:T(8,128)(2,1)S(1)}, bf16[64,1024]{1,0:T(8,128)(2,1)S(1)}, u32[]{:S(2)}, u32[]{:S(2)}) collective-permute-start(bf16[64,1024]{1,0:T(8,128)(2,1)S(1)} %get-tuple-element.97), channel_id=1, source_target_pairs={{0,0},{1,2},{2,1},{3,4},{4,3},{5,6},{6,5},{7,7},{8,8},{9,10},{10,9... | collective-permute-start | bytes 393224 | tf_op jit(solution)/shard_map/ppermute | solution.py:458
  24.9 0.9 %collective-permute-start.12 = (bf16[448,128]{1,0:T(8,128)(2,1)S(1)}, bf16[448,128]{1,0:T(8,128)(2,1)S(1)}, u32[]{:S(2)}, u32[]{:S(2)}) collective-permute-start(bf16[448,128]{1,0:T(8,128)(2,1)S(1)} %get-tuple-element.100), channel_id=1, source_target_pairs={{0,16},{8,24},{16,0},{24,8},{1,17},{9,25},{17,1},{25,9},{2,18},{10... | collective-permute-start | bytes 344072 | tf_op jit(solution)/shard_map/ppermute | solution.py:344
  25.7 1.5 %collective-permute-done.4 = bf16[192,256]{1,0:T(8,128)(2,1)S(1)} collective-permute-done((bf16[192,256]{1,0:T(8,128)(2,1)S(1)}, bf16[192,256]{1,0:T(8,128)(2,1)S(1)}, u32[]{:S(2)}, u32[]{:S(2)}) %collective-permute-start.4) | collective-permute-done | bytes 98336 | tf_op jit(solution)/shard_map/ppermute | solution.py:344
  27.3 0.5 collective-permute-start.9
  27.8 0.9 %collective-permute-done.9.refs_3_ = bf16[128,256]{1,0:T(8,128)(2,1)S(1)} collective-permute-done((bf16[128,256]{1,0:T(8,128)(2,1)S(1)}, bf16[128,256]{1,0:T(8,128)(2,1)S(1)}, u32[]{:S(2)}, u32[]{:S(2)}) %collective-permute-start.9) | collective-permute-done | bytes 65568 | tf_op jit(solution)/shard_map/ppermute | solution.py:344
  28.7 1.1 %shard_map.92.refs_0_ = f32[8,216,128]{2,1,0:T(8,128)S(1)} custom-call(bf16[320,256]{1,0:T(8,128)(2,1)S(1)} %get-tuple-element.76.refs_0_.refs_4_, bf16[320,256]{1,0:T(8,128)(2,1)S(1)} %collective-permute-done.2.refs_1_.refs_5_, bf16[320,256]{1,0:T(8,128)(2,1)S(1)} %collective-permute-done.3.refs_2_.refs_6_, ...), custom_call_target="tpu_custom_call" | custom-call | flops 262144 | bytes 1024 | tf_op jit(solution)/shard_map/pallas_call | solution.py:64
  29.8 0.7 collective-permute-done.12.refs_2_
  30.6 2.1 %collective-permute-start.13 = (bf16[2,272,128]{2,1,0:T(8,128)(2,1)S(1)}, bf16[2,272,128]{2,1,0:T(8,128)(2,1)S(1)}, u32[]{:S(2)}, u32[]{:S(2)}) collective-permute-start(bf16[2,272,128]{2,1,0:T(8,128)(2,1)S(1)} %get-tuple-element.102), channel_id=1, source_target_pairs={{0,1},{1,0},{2,3},{3,2},{4,5},{5,4},{6,7},{7,6},{8,9},{9,8},{10,11... | collective-permute-start | bytes 417800 | tf_op jit(solution)/shard_map/ppermute | solution.py:344
  32.6 0.9 %collective-permute-start.14 = (bf16[2,272,128]{2,1,0:T(8,128)(2,1)S(1)}, bf16[2,272,128]{2,1,0:T(8,128)(2,1)S(1)}, u32[]{:S(2)}, u32[]{:S(2)}) collective-permute-start(bf16[2,272,128]{2,1,0:T(8,128)(2,1)S(1)} %get-tuple-element.103), channel_id=1, source_target_pairs={{0,2},{1,3},{2,0},{3,1},{4,6},{5,7},{6,4},{7,5},{8,10},{9,11},{10,... | collective-permute-start | bytes 417800 | tf_op jit(solution)/shard_map/ppermute | solution.py:344
  33.6 0.8 %collective-permute-start.15 = (bf16[2,272,128]{2,1,0:T(8,128)(2,1)S(1)}, bf16[2,272,128]{2,1,0:T(8,128)(2,1)S(1)}, u32[]{:S(2)}, u32[]{:S(2)}) collective-permute-start(bf16[2,272,128]{2,1,0:T(8,128)(2,1)S(1)} %get-tuple-element.104), channel_id=1, source_target_pairs={{0,3},{1,2},{2,1},{3,0},{4,7},{5,6},{6,5},{7,4},{8,11},{9,10},{10,... | collective-permute-start | bytes 417800 | tf_op jit(solution)/shard_map/ppermute | solution.py:344
  34.4 1.5 %shard_map.94 = f32[2,64,1024]{2,1,0:T(8,128)S(1)} custom-call(bf16[1728,128]{1,0:T(8,128)(2,1)S(1)} %bitcast.34, bf16[256,1024]{1,0:T(8,128)(2,1)S(1)} %shard_map.88.refs_1_.refs_0_), custom_call_target="tpu_custom_call" | custom-call | flops 65536 | bytes 1024 | tf_op jit(solution)/shard_map/pallas_call | solution.py:64
  35.9 0.5 collective-permute-done.13.refs_1_
  36.4 2.7 %collective-permute-done.14.refs_2_ = bf16[2,272,128]{2,1,0:T(8,128)(2,1)S(1)} collective-permute-done((bf16[2,272,128]{2,1,0:T(8,128)(2,1)S(1)}, bf16[2,272,128]{2,1,0:T(8,128)(2,1)S(1)}, u32[]{:S(2)}, u32[]{:S(2)}) %collective-permute-start.14) | collective-permute-done | bytes 139296 | tf_op jit(solution)/shard_map/ppermute | solution.py:344
  39.1 1.3 %collective-permute-done.15.refs_3_ = bf16[2,272,128]{2,1,0:T(8,128)(2,1)S(1)} collective-permute-done((bf16[2,272,128]{2,1,0:T(8,128)(2,1)S(1)}, bf16[2,272,128]{2,1,0:T(8,128)(2,1)S(1)}, u32[]{:S(2)}, u32[]{:S(2)}) %collective-permute-start.15) | collective-permute-done | bytes 139296 | tf_op jit(solution)/shard_map/ppermute | solution.py:344
  40.5 1.8 %collective-permute-start.16 = (bf16[2,272,128]{2,1,0:T(8,128)(2,1)S(1)}, bf16[2,272,128]{2,1,0:T(8,128)(2,1)S(1)}, u32[]{:S(2)}, u32[]{:S(2)}) collective-permute-start(bf16[2,272,128]{2,1,0:T(8,128)(2,1)S(1)} %shard_map.95.refs_0_), channel_id=1, source_target_pairs={{0,4},{1,5},{2,6},{3,7},{4,0},{5,1},{6,2},{7,3},{8,12},{9,13},{10,... | collective-permute-start | bytes 417800 | tf_op jit(solution)/shard_map/ppermute | solution.py:344
  42.3 1.6 %collective-permute-start.17 = (bf16[64,1024]{1,0:T(8,128)(2,1)S(1)}, bf16[64,1024]{1,0:T(8,128)(2,1)S(1)}, u32[]{:S(2)}, u32[]{:S(2)}) collective-permute-start(bf16[64,1024]{1,0:T(8,128)(2,1)S(1)} %get-tuple-element.111), channel_id=1, source_target_pairs={{0,1},{1,0},{2,3},{3,2},{4,5},{5,4},{6,7},{7,6},{8,9},{9,8},{10,11... | collective-permute-start | bytes 393224 | tf_op jit(solution)/shard_map/ppermute | solution.py:483
  43.9 3.4 %collective-permute-done.17 = bf16[64,1024]{1,0:T(8,128)(2,1)S(1)} collective-permute-done((bf16[64,1024]{1,0:T(8,128)(2,1)S(1)}, bf16[64,1024]{1,0:T(8,128)(2,1)S(1)}, u32[]{:S(2)}, u32[]{:S(2)}) %collective-permute-start.17) | collective-permute-done | bytes 131104 | tf_op jit(solution)/shard_map/ppermute | solution.py:483
  47.3 1.4 %collective-permute-done.16.refs_1_ = bf16[2,272,128]{2,1,0:T(8,128)(2,1)S(1)} collective-permute-done((bf16[2,272,128]{2,1,0:T(8,128)(2,1)S(1)}, bf16[2,272,128]{2,1,0:T(8,128)(2,1)S(1)}, u32[]{:S(2)}, u32[]{:S(2)}) %collective-permute-start.16) | collective-permute-done | bytes 139296 | tf_op jit(solution)/shard_map/ppermute | solution.py:344
  48.7 1.1 %collective-permute-start.18 = (bf16[2,272,128]{2,1,0:T(8,128)(2,1)S(1)}, bf16[2,272,128]{2,1,0:T(8,128)(2,1)S(1)}, u32[]{:S(2)}, u32[]{:S(2)}) collective-permute-start(bf16[2,272,128]{2,1,0:T(8,128)(2,1)S(1)} %get-tuple-element.118.refs_0_), channel_id=1, source_target_pairs={{0,16},{8,24},{16,0},{24,8},{1,17},{9,25},{17,1},{25,9},{2,18},{10... | collective-permute-start | bytes 417800 | tf_op jit(solution)/shard_map/ppermute | solution.py:344
  50.1 1.6 %collective-permute-start.20 = (bf16[2,192,128]{2,1,0:T(8,128)(2,1)S(1)}, bf16[2,192,128]{2,1,0:T(8,128)(2,1)S(1)}, u32[]{:S(2)}, u32[]{:S(2)}) collective-permute-start(bf16[2,192,128]{2,1,0:T(8,128)(2,1)S(1)} %get-tuple-element.114), channel_id=1, source_target_pairs={{0,2},{1,3},{2,0},{3,1},{4,6},{5,7},{6,4},{7,5},{8,10},{9,11},{10,... | collective-permute-start | bytes 294920 | tf_op jit(solution)/shard_map/ppermute | solution.py:344
  51.7 1.6 %collective-permute-start.19 = (bf16[2,192,128]{2,1,0:T(8,128)(2,1)S(1)}, bf16[2,192,128]{2,1,0:T(8,128)(2,1)S(1)}, u32[]{:S(2)}, u32[]{:S(2)}) collective-permute-start(bf16[2,192,128]{2,1,0:T(8,128)(2,1)S(1)} %get-tuple-element.114), channel_id=1, source_target_pairs={{0,1},{1,0},{2,3},{3,2},{4,5},{5,4},{6,7},{7,6},{8,9},{9,8},{10,11... | collective-permute-start | bytes 294920 | tf_op jit(solution)/shard_map/ppermute | solution.py:344
  53.3 2.0 %collective-permute-done.21.refs_2_.refs_4_ = bf16[2,192,128]{2,1,0:T(8,128)(2,1)S(1)} collective-permute-done((bf16[2,192,128]{2,1,0:T(8,128)(2,1)S(1)}, bf16[2,192,128]{2,1,0:T(8,128)(2,1)S(1)}, u32[]{:S(2)}, u32[]{:S(2)}) %collective-permute-start.21) | collective-permute-done | bytes 98336 | tf_op jit(solution)/shard_map/ppermute | solution.py:344
  55.4 1.0 %collective-permute-done.19.refs_0_.refs_2_ = bf16[2,192,128]{2,1,0:T(8,128)(2,1)S(1)} collective-permute-done((bf16[2,192,128]{2,1,0:T(8,128)(2,1)S(1)}, bf16[2,192,128]{2,1,0:T(8,128)(2,1)S(1)}, u32[]{:S(2)}, u32[]{:S(2)}) %collective-permute-start.19) | collective-permute-done | bytes 98336 | tf_op jit(solution)/shard_map/ppermute | solution.py:344
  56.5 1.6 %collective-permute-start.22 = (bf16[6,192,128]{2,1,0:T(8,128)(2,1)S(1)}, bf16[6,192,128]{2,1,0:T(8,128)(2,1)S(1)}, u32[]{:S(2)}, u32[]{:S(2)}) collective-permute-start(bf16[6,192,128]{2,1,0:T(8,128)(2,1)S(1)} %shard_map.97), channel_id=1, source_target_pairs={{0,16},{8,24},{16,0},{24,8},{1,17},{9,25},{17,1},{25,9},{2,18},{10... | collective-permute-start | bytes 884744 | tf_op jit(solution)/shard_map/ppermute | solution.py:344
  58.2 0.7 collective-permute-start.25
  58.9 1.8 %collective-permute-start.24 = (bf16[4,80,128]{2,1,0:T(8,128)(2,1)S(1)}, bf16[4,80,128]{2,1,0:T(8,128)(2,1)S(1)}, u32[]{:S(2)}, u32[]{:S(2)}) collective-permute-start(bf16[4,80,128]{2,1,0:T(8,128)(2,1)S(1)} %shard_map.98), channel_id=1, source_target_pairs={{0,2},{1,3},{2,0},{3,1},{4,6},{5,7},{6,4},{7,5},{8,10},{9,11},{10,... | collective-permute-start | bytes 245768 | tf_op jit(solution)/shard_map/ppermute | solution.py:344
  60.7 1.0 %collective-permute-start.23 = (bf16[4,80,128]{2,1,0:T(8,128)(2,1)S(1)}, bf16[4,80,128]{2,1,0:T(8,128)(2,1)S(1)}, u32[]{:S(2)}, u32[]{:S(2)}) collective-permute-start(bf16[4,80,128]{2,1,0:T(8,128)(2,1)S(1)} %shard_map.98), channel_id=1, source_target_pairs={{0,1},{1,0},{2,3},{3,2},{4,5},{5,4},{6,7},{7,6},{8,9},{9,8},{10,11... | collective-permute-start | bytes 245768 | tf_op jit(solution)/shard_map/ppermute | solution.py:344
  61.8 2.6 %collective-permute-done.25.refs_4_ = bf16[4,80,128]{2,1,0:T(8,128)(2,1)S(1)} collective-permute-done((bf16[4,80,128]{2,1,0:T(8,128)(2,1)S(1)}, bf16[4,80,128]{2,1,0:T(8,128)(2,1)S(1)}, u32[]{:S(2)}, u32[]{:S(2)}) %collective-permute-start.25) | collective-permute-done | bytes 81952 | tf_op jit(solution)/shard_map/ppermute | solution.py:344
  64.4 0.6 collective-permute-done.24.refs_3_
  65.5 0.5 collective-permute-done.22.refs_1_
  66.0 0.5 collective-permute-start.28
  66.5 0.5 collective-permute-start.30
  67.0 1.0 %copy.11 = bf16[1,64,2,1024]{3,2,1,0:T(2,128)(2,1)} copy(bf16[1,64,2,1024]{3,1,2,0:T(8,128)(2,1)S(1)} %fusion) | data formatting | bytes 524288
  68.0 2.6 %shard_map.100 = (f32[1728,128]{1,0:T(8,128)}, f32[3456,256]{1,0:T(8,128)}) custom-call(bf16[2240,128]{1,0:T(8,128)(2,1)S(1)} %shard_map.99.refs_0_, bf16[6,192,128]{2,1,0:T(8,128)(2,1)S(1)} %collective-permute-done.22.refs_1_, bf16[4,80,128]{2,1,0:T(8,128)(2,1)S(1)} %collective-permute-done.23.refs_2_, ...), custom_call_target="tpu_custom_call" | custom-call | flops 256 | bytes 1024 | tf_op jit(solution)/shard_map/pallas_call | solution.py:64
  (42 shorter events, 2.1 us)
Async XLA Ops:
  1.7 11.8 %collective-permute-start.1 = (bf16[256,256]{1,0:T(8,128)(2,1)S(1)}, bf16[256,256]{1,0:T(8,128)(2,1)S(1)}, u32[]{:S(2)}, u32[]{:S(2)}) collective-permute-start(bf16[256,256]{1,0:T(8,128)(2,1)S(1)} %fusion.1.refs_1_), channel_id=1, source_target_pairs={{0,7},{1,2},{2,1},{3,4},{4,3},{5,6},{6,5},{7,0},{8,15},{9,10},{10,... | collective-permute-start | bytes 393224 | tf_op jit(solution)/shard_map/ppermute | solution.py:359
  7.7 6.4 %collective-permute-start = (bf16[256,256]{1,0:T(8,128)(2,1)S(1)}, bf16[256,256]{1,0:T(8,128)(2,1)S(1)}, u32[]{:S(2)}, u32[]{:S(2)}) collective-permute-start(bf16[256,256]{1,0:T(8,128)(2,1)S(1)} %fusion.1.refs_1_), channel_id=1, source_target_pairs={{0,1},{1,0},{2,3},{3,2},{4,5},{5,4},{6,7},{7,6},{8,9},{9,8},{10,11... | collective-permute-start | bytes 393224 | tf_op jit(solution)/shard_map/ppermute | solution.py:359
  8.7 7.0 %copy-start = (bf16[27,128,256]{2,1,0:T(8,128)(2,1)S(1)}, bf16[27,128,256]{2,1,0:T(8,128)(2,1)}, u32[]{:S(2)}) copy-start(bf16[27,128,256]{2,1,0:T(8,128)(2,1)} %param.11) | copy-start | bytes 5308420
  10.6 8.3 %collective-permute-start.5 = (bf16[64,1024]{1,0:T(8,128)(2,1)S(1)}, bf16[64,1024]{1,0:T(8,128)(2,1)S(1)}, u32[]{:S(2)}, u32[]{:S(2)}) collective-permute-start(bf16[64,1024]{1,0:T(8,128)(2,1)S(1)} %get-tuple-element.86), channel_id=1, source_target_pairs={{0,1},{1,0},{2,3},{3,2},{4,5},{5,4},{6,7},{7,6},{8,9},{9,8},{10,11... | collective-permute-start | bytes 393224 | tf_op jit(solution)/shard_map/ppermute | solution.py:375
  12.7 7.7 %collective-permute-start.6 = (bf16[64,1024]{1,0:T(8,128)(2,1)S(1)}, bf16[64,1024]{1,0:T(8,128)(2,1)S(1)}, u32[]{:S(2)}, u32[]{:S(2)}) collective-permute-start(bf16[64,1024]{1,0:T(8,128)(2,1)S(1)} %get-tuple-element.87), channel_id=1, source_target_pairs={{0,7},{1,2},{2,1},{3,4},{4,3},{5,6},{6,5},{7,0},{8,15},{9,10},{10,... | collective-permute-start | bytes 393224 | tf_op jit(solution)/shard_map/ppermute | solution.py:375
  13.5 3.9 %copy-start.1 = (bf16[27,64,128]{2,1,0:T(8,128)(2,1)S(1)}, bf16[27,64,128]{2,1,0:T(8,128)(2,1)}, u32[]{:S(2)}) copy-start(bf16[27,64,128]{2,1,0:T(8,128)(2,1)} %param.10) | copy-start | bytes 1327108
  14.2 13.1 %collective-permute-start.3 = (bf16[320,256]{1,0:T(8,128)(2,1)S(1)}, bf16[320,256]{1,0:T(8,128)(2,1)S(1)}, u32[]{:S(2)}, u32[]{:S(2)}) collective-permute-start(bf16[320,256]{1,0:T(8,128)(2,1)S(1)} %get-tuple-element.78), channel_id=1, source_target_pairs={{0,16},{8,24},{16,0},{24,8},{1,17},{9,25},{17,1},{25,9},{2,18},{10... | collective-permute-start | bytes 491528 | tf_op jit(solution)/shard_map/ppermute | solution.py:344
  21.9 2.1 %collective-permute-start.7 = (bf16[448,128]{1,0:T(8,128)(2,1)S(1)}, bf16[448,128]{1,0:T(8,128)(2,1)S(1)}, u32[]{:S(2)}, u32[]{:S(2)}) collective-permute-start(bf16[448,128]{1,0:T(8,128)(2,1)S(1)} %get-tuple-element.92), channel_id=1, source_target_pairs={{0,8},{8,0},{16,24},{24,16},{1,9},{9,1},{17,25},{25,17},{2,10},{10... | collective-permute-start | bytes 344072 | tf_op jit(solution)/shard_map/ppermute | solution.py:344
  22.0 2.8 %collective-permute-start.8 = (bf16[448,128]{1,0:T(8,128)(2,1)S(1)}, bf16[448,128]{1,0:T(8,128)(2,1)S(1)}, u32[]{:S(2)}, u32[]{:S(2)}) collective-permute-start(bf16[448,128]{1,0:T(8,128)(2,1)S(1)} %get-tuple-element.93), channel_id=1, source_target_pairs={{0,8},{8,0},{16,24},{24,16},{1,9},{9,1},{17,25},{25,17},{2,10},{10... | collective-permute-start | bytes 344072 | tf_op jit(solution)/shard_map/ppermute | solution.py:344
  22.5 4.8 %collective-permute-start.4 = (bf16[192,256]{1,0:T(8,128)(2,1)S(1)}, bf16[192,256]{1,0:T(8,128)(2,1)S(1)}, u32[]{:S(2)}, u32[]{:S(2)}) collective-permute-start(bf16[192,256]{1,0:T(8,128)(2,1)S(1)} %get-tuple-element.79), channel_id=1, source_target_pairs={{0,16},{8,24},{16,0},{24,8},{1,17},{9,25},{17,1},{25,9},{2,18},{10... | collective-permute-start | bytes 294920 | tf_op jit(solution)/shard_map/ppermute | solution.py:344
  23.9 3.8 %collective-permute-start.2 = (bf16[320,256]{1,0:T(8,128)(2,1)S(1)}, bf16[320,256]{1,0:T(8,128)(2,1)S(1)}, u32[]{:S(2)}, u32[]{:S(2)}) collective-permute-start(bf16[320,256]{1,0:T(8,128)(2,1)S(1)} %get-tuple-element.77), channel_id=1, source_target_pairs={{0,8},{8,0},{16,24},{24,16},{1,9},{9,1},{17,25},{25,17},{2,10},{10... | collective-permute-start | bytes 491528 | tf_op jit(solution)/shard_map/ppermute | solution.py:344
  24.0 5.9 %collective-permute-start.11 = (bf16[64,1024]{1,0:T(8,128)(2,1)S(1)}, bf16[64,1024]{1,0:T(8,128)(2,1)S(1)}, u32[]{:S(2)}, u32[]{:S(2)}) collective-permute-start(bf16[64,1024]{1,0:T(8,128)(2,1)S(1)} %get-tuple-element.97), channel_id=1, source_target_pairs={{0,0},{1,2},{2,1},{3,4},{4,3},{5,6},{6,5},{7,7},{8,8},{9,10},{10,9... | collective-permute-start | bytes 393224 | tf_op jit(solution)/shard_map/ppermute | solution.py:458
  24.9 5.6 %collective-permute-start.12 = (bf16[448,128]{1,0:T(8,128)(2,1)S(1)}, bf16[448,128]{1,0:T(8,128)(2,1)S(1)}, u32[]{:S(2)}, u32[]{:S(2)}) collective-permute-start(bf16[448,128]{1,0:T(8,128)(2,1)S(1)} %get-tuple-element.100), channel_id=1, source_target_pairs={{0,16},{8,24},{16,0},{24,8},{1,17},{9,25},{17,1},{25,9},{2,18},{10... | collective-permute-start | bytes 344072 | tf_op jit(solution)/shard_map/ppermute | solution.py:344
  27.3 1.4 %collective-permute-start.10 = (bf16[192,256]{1,0:T(8,128)(2,1)S(1)}, bf16[192,256]{1,0:T(8,128)(2,1)S(1)}, u32[]{:S(2)}, u32[]{:S(2)}) collective-permute-start(bf16[192,256]{1,0:T(8,128)(2,1)S(1)} %collective-permute-done.4), channel_id=1, source_target_pairs={{0,8},{8,0},{16,24},{24,16},{1,9},{9,1},{17,25},{25,17},{2,10},{10... | collective-permute-start | bytes 294920 | tf_op jit(solution)/shard_map/ppermute | solution.py:344
  27.3 1.4 %collective-permute-start.9 = (bf16[128,256]{1,0:T(8,128)(2,1)S(1)}, bf16[128,256]{1,0:T(8,128)(2,1)S(1)}, u32[]{:S(2)}, u32[]{:S(2)}) collective-permute-start(bf16[128,256]{1,0:T(8,128)(2,1)S(1)} %slice.11), channel_id=1, source_target_pairs={{0,8},{8,0},{16,24},{24,16},{1,9},{9,1},{17,25},{25,17},{2,10},{10... | collective-permute-start | bytes 196616 | tf_op jit(solution)/shard_map/ppermute | solution.py:344
  30.6 5.8 %collective-permute-start.13 = (bf16[2,272,128]{2,1,0:T(8,128)(2,1)S(1)}, bf16[2,272,128]{2,1,0:T(8,128)(2,1)S(1)}, u32[]{:S(2)}, u32[]{:S(2)}) collective-permute-start(bf16[2,272,128]{2,1,0:T(8,128)(2,1)S(1)} %get-tuple-element.102), channel_id=1, source_target_pairs={{0,1},{1,0},{2,3},{3,2},{4,5},{5,4},{6,7},{7,6},{8,9},{9,8},{10,11... | collective-permute-start | bytes 417800 | tf_op jit(solution)/shard_map/ppermute | solution.py:344
  32.6 6.5 %collective-permute-start.14 = (bf16[2,272,128]{2,1,0:T(8,128)(2,1)S(1)}, bf16[2,272,128]{2,1,0:T(8,128)(2,1)S(1)}, u32[]{:S(2)}, u32[]{:S(2)}) collective-permute-start(bf16[2,272,128]{2,1,0:T(8,128)(2,1)S(1)} %get-tuple-element.103), channel_id=1, source_target_pairs={{0,2},{1,3},{2,0},{3,1},{4,6},{5,7},{6,4},{7,5},{8,10},{9,11},{10,... | collective-permute-start | bytes 417800 | tf_op jit(solution)/shard_map/ppermute | solution.py:344
  33.6 6.9 %collective-permute-start.15 = (bf16[2,272,128]{2,1,0:T(8,128)(2,1)S(1)}, bf16[2,272,128]{2,1,0:T(8,128)(2,1)S(1)}, u32[]{:S(2)}, u32[]{:S(2)}) collective-permute-start(bf16[2,272,128]{2,1,0:T(8,128)(2,1)S(1)} %get-tuple-element.104), channel_id=1, source_target_pairs={{0,3},{1,2},{2,1},{3,0},{4,7},{5,6},{6,5},{7,4},{8,11},{9,10},{10,... | collective-permute-start | bytes 417800 | tf_op jit(solution)/shard_map/ppermute | solution.py:344
  40.5 8.2 %collective-permute-start.16 = (bf16[2,272,128]{2,1,0:T(8,128)(2,1)S(1)}, bf16[2,272,128]{2,1,0:T(8,128)(2,1)S(1)}, u32[]{:S(2)}, u32[]{:S(2)}) collective-permute-start(bf16[2,272,128]{2,1,0:T(8,128)(2,1)S(1)} %shard_map.95.refs_0_), channel_id=1, source_target_pairs={{0,4},{1,5},{2,6},{3,7},{4,0},{5,1},{6,2},{7,3},{8,12},{9,13},{10,... | collective-permute-start | bytes 417800 | tf_op jit(solution)/shard_map/ppermute | solution.py:344
  42.3 5.0 %collective-permute-start.17 = (bf16[64,1024]{1,0:T(8,128)(2,1)S(1)}, bf16[64,1024]{1,0:T(8,128)(2,1)S(1)}, u32[]{:S(2)}, u32[]{:S(2)}) collective-permute-start(bf16[64,1024]{1,0:T(8,128)(2,1)S(1)} %get-tuple-element.111), channel_id=1, source_target_pairs={{0,1},{1,0},{2,3},{3,2},{4,5},{5,4},{6,7},{7,6},{8,9},{9,8},{10,11... | collective-permute-start | bytes 393224 | tf_op jit(solution)/shard_map/ppermute | solution.py:483
  48.7 7.7 %collective-permute-start.18 = (bf16[2,272,128]{2,1,0:T(8,128)(2,1)S(1)}, bf16[2,272,128]{2,1,0:T(8,128)(2,1)S(1)}, u32[]{:S(2)}, u32[]{:S(2)}) collective-permute-start(bf16[2,272,128]{2,1,0:T(8,128)(2,1)S(1)} %get-tuple-element.118.refs_0_), channel_id=1, source_target_pairs={{0,16},{8,24},{16,0},{24,8},{1,17},{9,25},{17,1},{25,9},{2,18},{10... | collective-permute-start | bytes 417800 | tf_op jit(solution)/shard_map/ppermute | solution.py:344
  49.8 5.5 %collective-permute-start.21 = (bf16[2,192,128]{2,1,0:T(8,128)(2,1)S(1)}, bf16[2,192,128]{2,1,0:T(8,128)(2,1)S(1)}, u32[]{:S(2)}, u32[]{:S(2)}) collective-permute-start(bf16[2,192,128]{2,1,0:T(8,128)(2,1)S(1)} %get-tuple-element.114), channel_id=1, source_target_pairs={{0,3},{1,2},{2,1},{3,0},{4,7},{5,6},{6,5},{7,4},{8,11},{9,10},{10,... | collective-permute-start | bytes 294920 | tf_op jit(solution)/shard_map/ppermute | solution.py:344
  50.1 5.3 %collective-permute-start.20 = (bf16[2,192,128]{2,1,0:T(8,128)(2,1)S(1)}, bf16[2,192,128]{2,1,0:T(8,128)(2,1)S(1)}, u32[]{:S(2)}, u32[]{:S(2)}) collective-permute-start(bf16[2,192,128]{2,1,0:T(8,128)(2,1)S(1)} %get-tuple-element.114), channel_id=1, source_target_pairs={{0,2},{1,3},{2,0},{3,1},{4,6},{5,7},{6,4},{7,5},{8,10},{9,11},{10,... | collective-permute-start | bytes 294920 | tf_op jit(solution)/shard_map/ppermute | solution.py:344
  51.7 4.7 %collective-permute-start.19 = (bf16[2,192,128]{2,1,0:T(8,128)(2,1)S(1)}, bf16[2,192,128]{2,1,0:T(8,128)(2,1)S(1)}, u32[]{:S(2)}, u32[]{:S(2)}) collective-permute-start(bf16[2,192,128]{2,1,0:T(8,128)(2,1)S(1)} %get-tuple-element.114), channel_id=1, source_target_pairs={{0,1},{1,0},{2,3},{3,2},{4,5},{5,4},{6,7},{7,6},{8,9},{9,8},{10,11... | collective-permute-start | bytes 294920 | tf_op jit(solution)/shard_map/ppermute | solution.py:344
  56.4 9.6 %collective-permute-start.26 = (bf16[2240,128]{1,0:T(8,128)(2,1)S(1)}, bf16[2240,128]{1,0:T(8,128)(2,1)S(1)}, u32[]{:S(2)}, u32[]{:S(2)}) collective-permute-start(bf16[2240,128]{1,0:T(8,128)(2,1)S(1)} %shard_map.99.refs_0_), channel_id=1, source_target_pairs={{0,8},{8,0},{16,24},{24,16},{1,9},{9,1},{17,25},{25,17},{2,10},{10... | collective-permute-start | bytes 1720328 | tf_op jit(solution)/shard_map/ppermute | solution.py:344
  56.5 9.5 %collective-permute-start.22 = (bf16[6,192,128]{2,1,0:T(8,128)(2,1)S(1)}, bf16[6,192,128]{2,1,0:T(8,128)(2,1)S(1)}, u32[]{:S(2)}, u32[]{:S(2)}) collective-permute-start(bf16[6,192,128]{2,1,0:T(8,128)(2,1)S(1)} %shard_map.97), channel_id=1, source_target_pairs={{0,16},{8,24},{16,0},{24,8},{1,17},{9,25},{17,1},{25,9},{2,18},{10... | collective-permute-start | bytes 884744 | tf_op jit(solution)/shard_map/ppermute | solution.py:344
  58.2 6.2 %collective-permute-start.25 = (bf16[4,80,128]{2,1,0:T(8,128)(2,1)S(1)}, bf16[4,80,128]{2,1,0:T(8,128)(2,1)S(1)}, u32[]{:S(2)}, u32[]{:S(2)}) collective-permute-start(bf16[4,80,128]{2,1,0:T(8,128)(2,1)S(1)} %shard_map.98), channel_id=1, source_target_pairs={{0,3},{1,2},{2,1},{3,0},{4,7},{5,6},{6,5},{7,4},{8,11},{9,10},{10,... | collective-permute-start | bytes 245768 | tf_op jit(solution)/shard_map/ppermute | solution.py:344
  58.9 6.1 %collective-permute-start.24 = (bf16[4,80,128]{2,1,0:T(8,128)(2,1)S(1)}, bf16[4,80,128]{2,1,0:T(8,128)(2,1)S(1)}, u32[]{:S(2)}, u32[]{:S(2)}) collective-permute-start(bf16[4,80,128]{2,1,0:T(8,128)(2,1)S(1)} %shard_map.98), channel_id=1, source_target_pairs={{0,2},{1,3},{2,0},{3,1},{4,6},{5,7},{6,4},{7,5},{8,10},{9,11},{10,... | collective-permute-start | bytes 245768 | tf_op jit(solution)/shard_map/ppermute | solution.py:344
  60.7 4.7 %collective-permute-start.23 = (bf16[4,80,128]{2,1,0:T(8,128)(2,1)S(1)}, bf16[4,80,128]{2,1,0:T(8,128)(2,1)S(1)}, u32[]{:S(2)}, u32[]{:S(2)}) collective-permute-start(bf16[4,80,128]{2,1,0:T(8,128)(2,1)S(1)} %shard_map.98), channel_id=1, source_target_pairs={{0,1},{1,0},{2,3},{3,2},{4,5},{5,4},{6,7},{7,6},{8,9},{9,8},{10,11... | collective-permute-start | bytes 245768 | tf_op jit(solution)/shard_map/ppermute | solution.py:344
  66.0 2.0 %collective-permute-start.27 = (bf16[6,192,128]{2,1,0:T(8,128)(2,1)S(1)}, bf16[6,192,128]{2,1,0:T(8,128)(2,1)S(1)}, u32[]{:S(2)}, u32[]{:S(2)}) collective-permute-start(bf16[6,192,128]{2,1,0:T(8,128)(2,1)S(1)} %collective-permute-done.22.refs_1_), channel_id=1, source_target_pairs={{0,8},{8,0},{16,24},{24,16},{1,9},{9,1},{17,25},{25,17},{2,10},{10... | collective-permute-start | bytes 884744 | tf_op jit(solution)/shard_map/ppermute | solution.py:344
  66.0 2.0 %collective-permute-start.28 = (bf16[4,80,128]{2,1,0:T(8,128)(2,1)S(1)}, bf16[4,80,128]{2,1,0:T(8,128)(2,1)S(1)}, u32[]{:S(2)}, u32[]{:S(2)}) collective-permute-start(bf16[4,80,128]{2,1,0:T(8,128)(2,1)S(1)} %collective-permute-done.23.refs_2_), channel_id=1, source_target_pairs={{0,8},{8,0},{16,24},{24,16},{1,9},{9,1},{17,25},{25,17},{2,10},{10... | collective-permute-start | bytes 245768 | tf_op jit(solution)/shard_map/ppermute | solution.py:344
  66.5 1.5 %collective-permute-start.29 = (bf16[4,80,128]{2,1,0:T(8,128)(2,1)S(1)}, bf16[4,80,128]{2,1,0:T(8,128)(2,1)S(1)}, u32[]{:S(2)}, u32[]{:S(2)}) collective-permute-start(bf16[4,80,128]{2,1,0:T(8,128)(2,1)S(1)} %collective-permute-done.24.refs_3_), channel_id=1, source_target_pairs={{0,8},{8,0},{16,24},{24,16},{1,9},{9,1},{17,25},{25,17},{2,10},{10... | collective-permute-start | bytes 245768 | tf_op jit(solution)/shard_map/ppermute | solution.py:344
  66.5 1.5 %collective-permute-start.30 = (bf16[4,80,128]{2,1,0:T(8,128)(2,1)S(1)}, bf16[4,80,128]{2,1,0:T(8,128)(2,1)S(1)}, u32[]{:S(2)}, u32[]{:S(2)}) collective-permute-start(bf16[4,80,128]{2,1,0:T(8,128)(2,1)S(1)} %collective-permute-done.25.refs_4_), channel_id=1, source_target_pairs={{0,8},{8,0},{16,24},{24,16},{1,9},{9,1},{17,25},{25,17},{2,10},{10... | collective-permute-start | bytes 245768 | tf_op jit(solution)/shard_map/ppermute | solution.py:344
